TPU v7x, 32 devices: a whole 2x2x4 slice. The times are simulated.
32 devices in a mesh: dev: 32 (over z, y, x, core).
Axes of the slice: x: 2, y: 2, z: 4, core: 2. Of those that a mesh axis runs over, the one named last changes fastest.
Arguments:
- tokens: float32 [10240, 1024], P('dev'), may hold values from -6 to 6
- segments: int32 [10240], P('dev'), may hold values from 0 to 1, as said below
- norm1_gain: float32 [1024], P('dev'), may hold values from 0.5 to 1.5
- norm1_bias: float32 [1024], P('dev'), may hold values from -4 to 4
- qkv_weight: float32 [1024, 3072], P('dev'), may hold values from -0.1875 to 0.1875
- qv_bias: float32 [2048], P('dev'), may hold values from -6 to 6
- out_weight: float32 [1024, 1024], P('dev'), may hold values from -1.5 to 1.5
- out_bias: float32 [1024], P('dev'), may hold values from -6 to 6
- norm2_gain: float32 [1024], P('dev'), may hold values from 0.5 to 1.5
- norm2_bias: float32 [1024], P('dev'), may hold values from -4 to 4
- fc1_weight: float32 [1024, 4096], P('dev'), may hold values from -0.1875 to 0.1875
- fc1_bias: float32 [4096], P('dev'), may hold values from -6 to 6
- fc2_weight: float32 [4096, 1024], P('dev'), may hold values from -0.09375 to 0.09375
- fc2_bias: float32 [1024], P('dev'), may hold values from -6 to 6
- cotangent: float32 [10240, 1024], P('dev'), may hold values from -6 to 6
Outputs:
- activations: float32 [10240, 1024], P('dev')
- input_grad: float32 [10240, 1024], P('dev')
- grad_norm1_gain: float32 [1024], P('dev')
- grad_norm1_bias: float32 [1024], P('dev')
- grad_qkv_weight: float32 [1024, 3072], P('dev')
- grad_qv_bias: float32 [2048], P('dev')
- grad_out_weight: float32 [1024, 1024], P('dev')
- grad_out_bias: float32 [1024], P('dev')
- grad_norm2_gain: float32 [1024], P('dev')
- grad_norm2_bias: float32 [1024], P('dev')
- grad_fc1_weight: float32 [1024, 4096], P('dev')
- grad_fc1_bias: float32 [4096], P('dev')
- grad_fc2_weight: float32 [4096, 1024], P('dev')
- grad_fc2_bias: float32 [1024], P('dev')
Inputs may be any that keep to these rules, and one draw needn't show every extreme that they name: `segments`: each block of 320 slots holds one image, image k numbered k, each of 64 to 320 consecutive slots; in every draw some image has exactly 320 slots; the slots after a block's last image are padding, numbered 1.
All inputs are finite; a program needn't handle non-finite values.
Results may differ from a plain program's by a relative error of at most 0.012.
The roundings to bfloat16 on the way count: a program that leaves them out, or rounds other values in their place, can miss the bound.
Values may be sent and summed in bfloat16 or wider, within the bound.
A program may use at most 256 MiB of HBM per device.

v0:
```python
from functools import partial

import jax
import jax.numpy as jnp
from jax import lax
from jax.sharding import PartitionSpec as P

HEAD_DIM = 64
IMG_DEV = 1


def layer_norm(rows_in, gain, bias):
    centre = rows_in - jnp.mean(rows_in, -1, keepdims=True)
    spread = jnp.mean(centre * centre, -1, keepdims=True)
    return centre * lax.rsqrt(spread + 1e-06) * gain + bias


def halved(array_in):
    return array_in.astype(jnp.bfloat16)


def contract_rows(left, right):
    return lax.dot_general(
        left, right, (((0,), (0,)), ((), ())), preferred_element_type=jnp.float32
    )


def contract_cols(left, right):
    return lax.dot_general(
        left, right, (((1,), (1,)), ((), ())), preferred_element_type=jnp.float32
    )


def head_pairs(block):
    return block.reshape(block.shape[0], -1, 2 * HEAD_DIM).transpose(1, 0, 2)


def join_pairs(stack):
    return stack.transpose(1, 0, 2).reshape(stack.shape[1], stack.shape[0] * stack.shape[2])


def masked_scores(query_heads, key_heads, allowed):
    scores = jnp.einsum("qhd,khd->hqk", query_heads, key_heads, preferred_element_type=jnp.float32)
    return jnp.where(allowed[None], scores, -1e30)


def pair_forward(pieces, allowed):
    q_pair, k_pair, v_pair = pieces
    row_count = q_pair.shape[0]
    query_heads = q_pair.reshape(row_count, 2, HEAD_DIM)
    key_heads = k_pair.reshape(row_count, 2, HEAD_DIM)
    value_heads = v_pair.reshape(row_count, 2, HEAD_DIM)
    scores = masked_scores(query_heads, key_heads, allowed)
    row_top = jnp.max(scores, -1, keepdims=True)
    powered = jnp.exp(scores - row_top)
    totals = jnp.sum(powered, -1, keepdims=True)
    probability = halved(powered / totals)
    attended = jnp.einsum(
        "hqk,khd->qhd", probability, value_heads, preferred_element_type=jnp.float32
    )
    return (attended.reshape(row_count, 2 * HEAD_DIM), row_top + jnp.log(totals))


def pair_backward(pieces, allowed):
    q_pair, k_pair, v_pair, g_pair, lse_pair = pieces
    row_count = q_pair.shape[0]
    query_heads = q_pair.reshape(row_count, 2, HEAD_DIM)
    key_heads = k_pair.reshape(row_count, 2, HEAD_DIM)
    value_heads = v_pair.reshape(row_count, 2, HEAD_DIM)
    grad_heads = g_pair.reshape(row_count, 2, HEAD_DIM)
    probability = jnp.exp(masked_scores(query_heads, key_heads, allowed) - lse_pair)
    d_prob = jnp.einsum("qhd,khd->hqk", grad_heads, value_heads, preferred_element_type=jnp.float32)
    row_inner = jnp.sum(probability * d_prob, -1, keepdims=True)
    d_scores = halved(probability * (d_prob - row_inner))
    d_query = halved(
        jnp.einsum("hqk,khd->qhd", d_scores, key_heads, preferred_element_type=jnp.float32)
    )
    d_query = d_query * jnp.bfloat16(HEAD_DIM ** (-0.5))
    d_key = halved(
        jnp.einsum("hqk,qhd->khd", d_scores, query_heads, preferred_element_type=jnp.float32)
    )
    d_value = halved(
        jnp.einsum(
            "hqk,qhd->khd", halved(probability), grad_heads, preferred_element_type=jnp.float32
        )
    )
    width_pair = 2 * HEAD_DIM
    return (
        d_query.reshape(row_count, width_pair),
        d_key.reshape(row_count, width_pair),
        d_value.reshape(row_count, width_pair),
    )


def shards(
    tokens,
    segments,
    norm1_gain,
    norm1_bias,
    qkv_weight,
    qv_bias,
    out_weight,
    out_bias,
    norm2_gain,
    norm2_bias,
    fc1_weight,
    fc1_bias,
    fc2_weight,
    fc2_bias,
    cotangent,
):
    model_width = tokens.shape[1]
    attn_shards = (
        halved(norm1_gain),
        halved(norm1_bias),
        halved(qkv_weight),
        halved(qv_bias),
        halved(out_weight),
        halved(out_bias),
    )
    mlp_shards = (
        halved(norm2_gain),
        halved(norm2_bias),
        halved(fc1_weight),
        halved(fc1_bias),
        halved(fc2_weight),
        halved(fc2_bias),
    )
    attn_full = (
        lax.all_gather(attn_shards[0], "dev", axis=0, tiled=True),
        lax.all_gather(attn_shards[1], "dev", axis=0, tiled=True),
        lax.all_gather(attn_shards[2], "dev", axis=0, tiled=True),
        lax.all_gather(attn_shards[3], "dev", axis=0, tiled=True),
        lax.all_gather(attn_shards[4], "dev", axis=0, tiled=True),
        lax.all_gather(attn_shards[5], "dev", axis=0, tiled=True),
    )
    gain_one, bias_one, mix_weight, mix_bias, proj_weight, proj_bias = attn_full
    valid_slot = segments < IMG_DEV
    allowed = (segments[:, None] == segments[None, :]) & valid_slot[None, :]
    gain_one_f = gain_one.astype(jnp.float32)
    bias_one_f = bias_one.astype(jnp.float32)
    first = halved(layer_norm(tokens, gain_one_f, bias_one_f))
    mix_bias_f = mix_bias.astype(jnp.float32)
    bias_row = jnp.concatenate(
        [mix_bias_f[:model_width], jnp.zeros((model_width,), jnp.float32), mix_bias_f[model_width:]]
    )
    projected = jnp.dot(first, mix_weight, preferred_element_type=jnp.float32) + bias_row
    queries = halved(projected[:, :model_width] * HEAD_DIM ** (-0.5))
    key_rows = halved(projected[:, model_width : 2 * model_width])
    values = halved(projected[:, 2 * model_width :])
    attended_stack, lse_stack = lax.map(
        lambda pieces: pair_forward(pieces, allowed),
        (head_pairs(queries), head_pairs(key_rows), head_pairs(values)),
    )
    attended = halved(join_pairs(attended_stack))
    residual = (
        tokens
        + jnp.dot(attended, proj_weight, preferred_element_type=jnp.float32)
        + proj_bias.astype(jnp.float32)
    )
    mlp_full = (
        lax.all_gather(mlp_shards[0], "dev", axis=0, tiled=True),
        lax.all_gather(mlp_shards[1], "dev", axis=0, tiled=True),
        lax.all_gather(mlp_shards[2], "dev", axis=0, tiled=True),
        lax.all_gather(mlp_shards[3], "dev", axis=0, tiled=True),
        lax.all_gather(mlp_shards[4], "dev", axis=0, tiled=True),
        lax.all_gather(mlp_shards[5], "dev", axis=0, tiled=True),
    )
    gain_two, bias_two, up_weight, up_bias, down_weight, down_bias = mlp_full
    gain_two_f = gain_two.astype(jnp.float32)
    bias_two_f = bias_two.astype(jnp.float32)
    second = halved(layer_norm(residual, gain_two_f, bias_two_f))
    inner = jnp.dot(second, up_weight, preferred_element_type=jnp.float32) + up_bias.astype(
        jnp.float32
    )
    active = halved(jax.nn.gelu(inner, approximate=False))
    branch = jnp.dot(active, down_weight, preferred_element_type=jnp.float32) + down_bias.astype(
        jnp.float32
    )
    activations = jnp.where(valid_slot[:, None], residual + branch, 0.0)
    late_shards, activations = lax.optimization_barrier((mlp_shards, activations))
    mlp_back = (
        lax.all_gather(late_shards[0], "dev", axis=0, tiled=True),
        lax.all_gather(late_shards[1], "dev", axis=0, tiled=True),
        lax.all_gather(late_shards[2], "dev", axis=0, tiled=True),
        lax.all_gather(late_shards[3], "dev", axis=0, tiled=True),
        lax.all_gather(late_shards[4], "dev", axis=0, tiled=True),
        lax.all_gather(late_shards[5], "dev", axis=0, tiled=True),
    )
    up_back = mlp_back[2]
    down_back = mlp_back[4]
    gain_two_b = mlp_back[0].astype(jnp.float32)
    bias_two_b = mlp_back[1].astype(jnp.float32)
    d_out = jnp.where(valid_slot[:, None], cotangent, 0.0)
    d_mlp = halved(d_out)
    grad_fc2_bias = jnp.sum(d_mlp, 0, dtype=jnp.float32)
    grad_fc2_weight = contract_rows(active, d_mlp)
    d_active = contract_cols(d_mlp, down_back)
    gelu_back = jax.vjp(partial(jax.nn.gelu, approximate=False), inner)[1]
    d_inner = halved(gelu_back(d_active)[0])
    grad_fc1_bias = jnp.sum(d_inner, 0, dtype=jnp.float32)
    grad_fc1_weight = contract_rows(second, d_inner)
    d_second = contract_cols(d_inner, up_back)
    norm_two_back = jax.vjp(layer_norm, residual, gain_two_b, bias_two_b)[1]
    d_norm2, grad_norm2_gain, grad_norm2_bias = norm_two_back(d_second)
    d_resid = d_out + d_norm2
    d_branch = halved(d_resid)
    late_attn, d_branch = lax.optimization_barrier((attn_shards, d_branch))
    attn_back = (
        lax.all_gather(late_attn[0], "dev", axis=0, tiled=True),
        lax.all_gather(late_attn[1], "dev", axis=0, tiled=True),
        lax.all_gather(late_attn[2], "dev", axis=0, tiled=True),
        lax.all_gather(late_attn[3], "dev", axis=0, tiled=True),
        lax.all_gather(late_attn[4], "dev", axis=0, tiled=True),
        lax.all_gather(late_attn[5], "dev", axis=0, tiled=True),
    )
    gain_one_b = attn_back[0].astype(jnp.float32)
    bias_one_b = attn_back[1].astype(jnp.float32)
    mix_back = attn_back[2]
    proj_back = attn_back[4]
    grad_out_bias = jnp.sum(d_branch, 0, dtype=jnp.float32)
    grad_out_weight = contract_rows(attended, d_branch)
    d_attended = halved(contract_cols(d_branch, proj_back))
    d_query_stack, d_key_stack, d_value_stack = lax.map(
        lambda pieces: pair_backward(pieces, allowed),
        (
            head_pairs(queries),
            head_pairs(key_rows),
            head_pairs(values),
            head_pairs(d_attended),
            lse_stack,
        ),
    )
    d_query = join_pairs(d_query_stack)
    d_value = join_pairs(d_value_stack)
    d_projected = jnp.concatenate([d_query, join_pairs(d_key_stack), d_value], 1)
    grad_qv_bias = jnp.concatenate(
        [jnp.sum(d_query, 0, dtype=jnp.float32), jnp.sum(d_value, 0, dtype=jnp.float32)]
    )
    grad_qkv_weight = contract_rows(first, d_projected)
    d_first = contract_cols(d_projected, mix_back)
    norm_one_back = jax.vjp(layer_norm, tokens, gain_one_b, bias_one_b)[1]
    d_norm1, grad_norm1_gain, grad_norm1_bias = norm_one_back(d_first)
    input_grad = d_resid + d_norm1
    owned = (
        lax.psum_scatter(grad_norm1_gain, "dev", scatter_dimension=0, tiled=True),
        lax.psum_scatter(grad_norm1_bias, "dev", scatter_dimension=0, tiled=True),
        lax.psum_scatter(grad_qkv_weight, "dev", scatter_dimension=0, tiled=True),
        lax.psum_scatter(grad_qv_bias, "dev", scatter_dimension=0, tiled=True),
        lax.psum_scatter(grad_out_weight, "dev", scatter_dimension=0, tiled=True),
        lax.psum_scatter(grad_out_bias, "dev", scatter_dimension=0, tiled=True),
        lax.psum_scatter(grad_norm2_gain, "dev", scatter_dimension=0, tiled=True),
        lax.psum_scatter(grad_norm2_bias, "dev", scatter_dimension=0, tiled=True),
        lax.psum_scatter(grad_fc1_weight, "dev", scatter_dimension=0, tiled=True),
        lax.psum_scatter(grad_fc1_bias, "dev", scatter_dimension=0, tiled=True),
        lax.psum_scatter(grad_fc2_weight, "dev", scatter_dimension=0, tiled=True),
        lax.psum_scatter(grad_fc2_bias, "dev", scatter_dimension=0, tiled=True),
    )
    return (
        activations,
        input_grad,
        owned[0],
        owned[1],
        owned[2],
        owned[3],
        owned[4],
        owned[5],
        owned[6],
        owned[7],
        owned[8],
        owned[9],
        owned[10],
        owned[11],
    )


def solution(mesh):
    in_specs = (
        P("dev", None),
        P("dev"),
        P("dev"),
        P("dev"),
        P("dev", None),
        P("dev"),
        P("dev", None),
        P("dev"),
        P("dev"),
        P("dev"),
        P("dev", None),
        P("dev"),
        P("dev", None),
        P("dev"),
        P("dev", None),
    )
    out_specs = (
        P("dev", None),
        P("dev", None),
        P("dev"),
        P("dev"),
        P("dev", None),
        P("dev"),
        P("dev", None),
        P("dev"),
        P("dev"),
        P("dev"),
        P("dev", None),
        P("dev"),
        P("dev", None),
        P("dev"),
    )
    return jax.shard_map(shards, mesh=mesh, in_specs=in_specs, out_specs=out_specs, check_vma=False)
```

profile of v0, /device:TPU:0, one launch (start us, length us, event | category | flops | bytes accessed | tf_op | source)
XLA Modules:
  0.0 1279.0 jit_solution(6447398192419510245)
XLA Ops:
  7.3 1.8 convert_element_type.154
  9.2 1.5 convert_element_type.161
  10.8 1.8 convert_element_type.145
  12.7 1.8 convert_element_type.147
  16.2 42.4 %all-reduce.18 = (bf16[2048]{0:T(1024)(128)(2,1)S(1)}, bf16[1024]{0:T(1024)(128)(2,1)S(1)}, bf16[1024]{0:T(1024)(128)(2,1)S(1)}, bf16[1024]{0:T(1024)(128)(2,1)S...) all-reduce(bf16[2048]{0:T(1024)(128)(2,1)S(1)} %dynamic-update-slic, ...), channel_id=1, replica_groups=mesh['dev'=32] {'dev'}, use_global_device_ids=true, to_apply=%add.2 | all-reduce | flops 8192 | bytes 32768
  59.2 40.6 %all-gather = bf16[32,1,128]{2,1,0:T(2,128)(2,1)S(1)} all-gather(bf16[1,1,128]{2,1,0:T(2,128)(2,1)S(1)} %convert_bitcast_fusion), channel_id=1, replica_groups=mesh['dev'=32] {'dev'}, dimensions={0}, use_global_device_ids=true | all-gather | bytes 8448 | tf_op jit(solution)/shard_map/all_gather | solution.py:165
  99.8 7.0 fusion.34
  106.8 1.1 fusion.32
  108.0 1.4 copy.49
  109.4 2.3 copy.51
  111.8 2.3 fusion.19
  114.0 2.2 copy.50
  116.3 16.5 %while.28 = (s32[]{:T(128)}, bf16[8,320,128]{1,2,0:T(8,128)(2,1)S(1)}, f32[8,2,320,1]{2,1,3,0:T(2,128)S(1)}, bf16[8,320,128]{1,2,0:T(8,128)(2,1)S(1)}, bf16[8,32...) while((s32[]{:T(128)}, ...), condition=%wide.region_5.6_spmd.clone, body=%wide.region_2.5_spmd.clone.sunk | while | flops 54066560 | bytes 3701933 | solution.py:151
  118.3 1.0 constant_dynamic-slice_fusion.14
  120.4 1.0 constant_dynamic-slice_fusion.14
  122.4 1.0 constant_dynamic-slice_fusion.14
  130.7 1.0 constant_dynamic-slice_fusion.14
  132.8 8.8 all-gather.12.cloned.1.call-done
  141.6 2.6 fusion.35
  144.5 76.9 %all-gather.14.cloned.1.call-done = bf16[1024,4096]{1,0:T(8,128)(2,1)} async-done(((bf16[32,4096]{1,0:T(8,128)(2,1)}), bf16[1024,4096]{1,0:T(8,128)(2,1)}) %all-gather.14.cloned.1.call-update) | async-done | bytes 8388624 | tf_op jit(solution)/shard_map/all_gather | solution.py:164
  221.3 17.7 %multiply_convert_fusion.1 = (bf16[320,4096]{1,0:T(8,128)(2,1)}, f32[320,4096]{1,0:T(8,128)}, f32[320,4096]{1,0:T(8,128)}) fusion(f32[4096]{0:T(1024)S(1)} %bitcast.160, bf16[1024,4096]{1,0:T(8,128)(2,1)} %all-gather.14.cloned.1.call-done, f32[320,1024]{1,0:T(8,128)S(1)} %get-tuple-element.257, f32[1024]{0:T(1024)S(1)} %convert_element_type.165, ...), kind=kOutput, calls=%fused_computation.37 | convolution fusion | flops 2772500480 | bytes 22833664 | tf_op jit(solution)/shard_map/dot_general | solution.py:173
  239.0 61.7 %all-gather.16.cloned.1.call-done = bf16[4096,1024]{1,0:T(8,128)(2,1)} async-done(((bf16[128,1024]{1,0:T(8,128)(2,1)}), bf16[4096,1024]{1,0:T(8,128)(2,1)}) %all-gather.16.cloned.1.call-update) | async-done | bytes 8388624 | tf_op jit(solution)/shard_map/all_gather | solution.py:166
  300.7 8.1 fusion.18
  309.5 1.5 convert_reduce_fusion.3
  311.2 39.7 %all-reduce.7 = bf16[1024]{0:T(1024)(128)(2,1)S(1)} all-reduce(bf16[1024]{0:T(1024)(128)(2,1)S(1)} %dynamic-update-slice.7), channel_id=1, replica_groups=mesh['dev'=32] {'dev'}, use_global_device_ids=true, to_apply=%add.7 | all-reduce | flops 1024 | bytes 4096
  351.0 34.0 %all-gather.18.cloned.1.call-done = bf16[4096,1024]{1,0:T(8,128)(2,1)} async-done(((bf16[128,1024]{1,0:T(8,128)(2,1)}), bf16[4096,1024]{1,0:T(8,128)(2,1)}) %all-gather.18.cloned.1.call-update) | async-done | bytes 8388624 | tf_op jit(solution)/shard_map/all_gather | solution.py:187
  384.9 13.3 %convert_reduce_fusion = (f32[4096]{0:T(1024)S(1)}, bf16[320,4096]{1,0:T(8,128)(2,1)}) fusion(f32[320,4096]{1,0:T(8,128)} %get-tuple-element.241, f32[320,4096]{1,0:T(8,128)} %get-tuple-element.258, bf16[320,1024]{1,0:T(8,128)(2,1)S(1)} %get-tuple-element.233, bf16[4096,1024]{1,0:T(8,128)(2,1)} %all-gather.18.cloned.1.call-done), kind=kOutput, calls=%fused_computation.35 | convolution fusion | flops 2705321984 | bytes 22167552 | tf_op jit(solution)/shard_map/dot_general | solution.py:29
  398.2 66.2 %all-gather.20.cloned.1.call-done = bf16[1024,4096]{1,0:T(8,128)(2,1)} async-done(((bf16[32,4096]{1,0:T(8,128)(2,1)}), bf16[1024,4096]{1,0:T(8,128)(2,1)}) %all-gather.20.cloned.1.call-update) | async-done | bytes 8388624 | tf_op jit(solution)/shard_map/all_gather | solution.py:185
  464.4 6.5 multiply_reduce_fusion.1
  471.4 1.1 copy-done.3
  473.5 4.3 fusion.37
  478.0 12.2 fusion.38
  490.5 37.4 %all-gather.22.cloned.1.call-done = bf16[1024,1024]{1,0:T(8,128)(2,1)} async-done(((bf16[32,1024]{1,0:T(8,128)(2,1)}), bf16[1024,1024]{1,0:T(8,128)(2,1)}) %all-gather.22.cloned.1.call-update) | async-done | bytes 2097168 | tf_op jit(solution)/shard_map/all_gather | solution.py:214
  527.9 3.3 convolution_convert_fusion.3
  531.2 2.2 copy.52
  533.4 55.5 %while.29 = (s32[]{:T(128)}, bf16[8,320,128]{1,2,0:T(8,128)(2,1)}, bf16[8,320,128]{1,2,0:T(8,128)(2,1)}, bf16[8,320,128]{1,2,0:T(8,128)(2,1)}, bf16[8,320,128]{1...) while((s32[]{:T(128)}, bf16[8,320,128]{1,2,0:T(8,128)(2,1)}, ...), condition=%wide.region_12.13_spmd.clone, body=%wide.region_10.12_spmd.clone.sunk | while | flops 133078400 | bytes 8379593 | solution.py:224
  588.9 8.4 fusion.20
  597.4 10.2 fusion.27
  607.9 38.7 %all-reduce.8 = bf16[1024]{0:T(1024)(128)(2,1)S(1)} all-reduce(bf16[1024]{0:T(1024)(128)(2,1)S(1)} %dynamic-update-slice.8), channel_id=1, replica_groups=mesh['dev'=32] {'dev'}, use_global_device_ids=true, to_apply=%add.8 | all-reduce | flops 1024 | bytes 4096
  646.7 1.5 convert_reduce_fusion.1
  648.2 7.3 multiply_reduce_fusion.2
  655.5 42.1 %all-reduce.17 = (f32[1024]{0:T(1024)S(1)}, f32[1024]{0:T(1024)S(1)}, f32[2048]{0:T(1024)S(1)}, f32[1024]{0:T(1024)S(1)}, f32[1024]{0:T(1024)S(1)}, /*index=5*/f...) all-reduce(f32[1024]{0:T(1024)S(1)} %get-tuple-element.175, ...), channel_id=2, replica_groups=mesh['dev'=32] {'dev'}, use_global_device_ids=true, to_apply=%region_16.17.clone | all-reduce | flops 12288 | bytes 98304
  702.3 1.8 fusion.28
  704.1 1.4 add_add_fusion.2
  705.5 36.2 %reduce-scatter.7.cloned.1.call-done = f32[32,1024]{1,0:T(8,128)} async-done(((f32[1024,1024]{1,0:T(8,128)}), f32[32,1024]{1,0:T(8,128)}) %reduce-scatter.7.cloned.1.call-update) | async-done | bytes 131088 | tf_op jit(solution)/shard_map/reduce_scatter | solution.py:250
  741.7 181.5 %reduce-scatter.11.cloned.1.call-done = f32[128,1024]{1,0:T(8,128)} async-done(((f32[4096,1024]{1,0:T(8,128)}), f32[128,1024]{1,0:T(8,128)}) %reduce-scatter.11.cloned.1.call-update) | async-done | bytes 524304 | tf_op jit(solution)/shard_map/reduce_scatter | solution.py:256
  923.2 163.8 %reduce-scatter.5.cloned.1.call-done = f32[32,3072]{1,0:T(8,128)} async-done(((f32[1024,3072]{1,0:T(8,128)}), f32[32,3072]{1,0:T(8,128)}) %reduce-scatter.5.cloned.1.call-update) | async-done | bytes 393232 | tf_op jit(solution)/shard_map/reduce_scatter | solution.py:248
  1087.0 184.7 %reduce-scatter.9.cloned.1.call-done = f32[32,4096]{1,0:T(8,128)} async-done(((f32[1024,4096]{1,0:T(8,128)}), f32[32,4096]{1,0:T(8,128)}) %reduce-scatter.9.cloned.1.call-update) | async-done | bytes 524304 | tf_op jit(solution)/shard_map/reduce_scatter | solution.py:254
  (300 shorter events, 77.8 us)
Async XLA Ops:
  7.2 7.4 copy-start.10
  7.2 7.4 copy-start.11
  7.2 7.4 copy-start.12
  7.2 7.4 copy-start.13
  7.2 7.4 copy-start.14
  7.2 7.4 copy-start.15
  7.2 7.4 copy-start.16
  7.3 51.4 %copy-start = (f32[320,1024]{1,0:T(8,128)S(1)}, f32[320,1024]{1,0:T(8,128)}, u32[]{:S(2)}) copy-start(f32[320,1024]{1,0:T(8,128)} %param.19) | copy-start | bytes 3932164
  7.3 92.6 %all-gather.10.cloned.1.call-start = ((), (), s32[]{:S(2)}) async-start(), calls=%async_computation.4 | async-start | bytes 6488064 | tf_op jit(solution)/shard_map/all_gather | solution.py:132
  9.1 50.0 %copy-start.9 = (s32[320]{0:T(512)S(1)}, s32[320]{0:T(512)}, u32[]{:S(2)}) copy-start(s32[320]{0:T(512)} %param.20) | copy-start | bytes 3844
  9.1 50.0 %copy-start.17 = (f32[128]{0:T(128)S(1)}, f32[128]{0:T(128)}, u32[]{:S(2)}) copy-start(f32[128]{0:T(128)} %param.30) | copy-start | bytes 1540
  9.1 132.4 %all-gather.12.cloned.1.call-start = ((), (), s32[]{:S(2)}) async-start(), calls=%async_computation.5 | async-start | bytes 2162688 | tf_op jit(solution)/shard_map/all_gather | solution.py:134
  10.8 210.6 %all-gather.14.cloned.1.call-start = ((), (), s32[]{:S(2)}) async-start(), calls=%async_computation.6 | async-start | bytes 8650752 | tf_op jit(solution)/shard_map/all_gather | solution.py:164
  12.6 288.1 %all-gather.16.cloned.1.call-start = ((), (), s32[]{:S(2)}) async-start(), calls=%async_computation.7 | async-start | bytes 8650752 | tf_op jit(solution)/shard_map/all_gather | solution.py:166
  14.5 370.5 %all-gather.18.cloned.1.call-start = ((), (), s32[]{:S(2)}) async-start(), calls=%async_computation.8 | async-start | bytes 8650752 | tf_op jit(solution)/shard_map/all_gather | solution.py:187
  132.7 8.8 copy-start.6
  132.7 11.4 copy-start.5
  308.9 155.6 %all-gather.20.cloned.1.call-start = ((), (), s32[]{:S(2)}) async-start(), calls=%async_computation.9 | async-start | bytes 8650752 | tf_op jit(solution)/shard_map/all_gather | solution.py:185
  309.4 218.4 %all-gather.22.cloned.1.call-start = ((), (), s32[]{:S(2)}) async-start(), calls=%async_computation.10 | async-start | bytes 2162688 | tf_op jit(solution)/shard_map/all_gather | solution.py:214
  311.0 87.2 %copy-start.8 = (bf16[320,1024]{1,0:T(8,128)(2,1)}, bf16[320,1024]{1,0:T(8,128)(2,1)S(1)}, u32[]{:S(2)}) copy-start(bf16[320,1024]{1,0:T(8,128)(2,1)S(1)} %get-tuple-element.233) | copy-start | bytes 1966084
  470.9 1.6 copy-start.1
  471.4 1.1 copy-start.3
  472.7 175.5 %all-gather.24.cloned.1.call-start = ((), (), s32[]{:S(2)}) async-start(), calls=%async_computation.11 | async-start | bytes 6488064 | tf_op jit(solution)/shard_map/all_gather | solution.py:212
  473.5 268.2 %reduce-scatter.7.cloned.1.call-start = ((), (), s32[]{:S(2)}) async-start(), calls=%async_computation.13 | async-start | bytes 4325376 | tf_op jit(solution)/shard_map/reduce_scatter | solution.py:250
  477.9 445.3 %reduce-scatter.11.cloned.1.call-start = ((), (), s32[]{:S(2)}) async-start(), calls=%async_computation.15 | async-start | bytes 17301504 | tf_op jit(solution)/shard_map/reduce_scatter | solution.py:256
  490.2 596.8 %reduce-scatter.5.cloned.1.call-start = ((), (), s32[]{:S(2)}) async-start(), calls=%async_computation.12 | async-start | bytes 12976128 | tf_op jit(solution)/shard_map/reduce_scatter | solution.py:248
  597.4 674.3 %reduce-scatter.9.cloned.1.call-start = ((), (), s32[]{:S(2)}) async-start(), calls=%async_computation.14 | async-start | bytes 17301504 | tf_op jit(solution)/shard_map/reduce_scatter | solution.py:254
  607.6 39.1 %copy-start.7 = (bf16[8,320,128]{1,2,0:T(8,128)(2,1)S(1)}, bf16[8,320,128]{1,2,0:T(8,128)(2,1)}, u32[]{:S(2)}) copy-start(bf16[8,320,128]{1,2,0:T(8,128)(2,1)} %get-tuple-element.124) | copy-start | bytes 1966084
  655.5 48.6 %copy-start.2 = (f32[320,1024]{1,0:T(8,128)S(1)}, f32[320,1024]{1,0:T(8,128)}, u32[]{:S(2)}) copy-start(f32[320,1024]{1,0:T(8,128)} %param.33) | copy-start | bytes 3932164
  697.6 6.5 copy-start.4
Sparse Core Ops, SparseCore 0:
  11.0 72.2 all-gather.9
  86.7 54.8 all-gather.11
  145.0 76.2 all-gather.13
  224.6 76.0 all-gather.15
  309.0 75.9 all-gather.17
  388.2 76.1 all-gather.19
  472.9 54.9 all-gather.21
  530.7 68.3 all-gather.23
  602.0 139.6 reduce-scatter.6
  744.4 178.7 reduce-scatter.10
  929.8 157.1 reduce-scatter.4
  1089.8 181.8 reduce-scatter.8
where the time goes:
time: 1280 us
  waiting for transfers between devices  852 us (67%)
  blocking collectives  203 us (16%)
  matrix products  119 us (9%)
  local copies, waits for them, and re-layouts  65.3 us (5%)
  other arithmetic  21.9 us (2%)
  between operations  15.2 us (1%)
    reduce_scatter x1, waiting for transfers between devices, shards(): lax.psum_scatter(grad_fc1_weight, 'dev', scatter_dimension=0, tiled=True)  185 us
    reduce_scatter x1, waiting for transfers between devices, shards(): lax.psum_scatter(grad_fc2_weight, 'dev', scatter_dimension=0, tiled=True)  181 us
    reduce_scatter x1, waiting for transfers between devices, shards(): lax.psum_scatter(grad_qkv_weight, 'dev', scatter_dimension=0, tiled=True)  164 us
    unnamed x4, blocking collectives  163 us
    all_gather x1, waiting for transfers between devices, shards(): lax.all_gather(mlp_shards[2], 'dev', axis=0, tiled=True)  76.9 us
    all_gather x1, waiting for transfers between devices, shards(): lax.all_gather(late_shards[2], 'dev', axis=0, tiled=True)  66.2 us
    all_gather x1, waiting for transfers between devices, shards(): lax.all_gather(mlp_shards[4], 'dev', axis=0, tiled=True)  61.7 us
    all_gather x1, blocking collectives, shards(): lax.all_gather(mlp_shards[3], 'dev', axis=0, tiled=True)  40.6 us
  transfers between devices with their start and end apart: 12, of which 10 were waited for; matrix products, arithmetic and copies ran while one was open for 15% of the time, Pallas kernels for 0%

commit v1 on v0

v1 whole, which is shorter than its diff:
```python
import functools
from functools import partial

import jax
import jax.numpy as jnp
from jax import lax
from jax.experimental import pallas as pl
from jax.experimental.pallas import tpu as pltpu
from jax.sharding import PartitionSpec as P

HEAD_DIM = 64
IMG_DEV = 1
MESH = pl.DeviceIdType.MESH


def layer_norm(rows_in, gain, bias):
    centre = rows_in - jnp.mean(rows_in, -1, keepdims=True)
    spread = jnp.mean(centre * centre, -1, keepdims=True)
    return centre * lax.rsqrt(spread + 1e-06) * gain + bias


def halved(array_in):
    return array_in.astype(jnp.bfloat16)


def contract_rows(left, right):
    return lax.dot_general(
        left, right, (((0,), (0,)), ((), ())), preferred_element_type=jnp.float32
    )


def contract_cols(left, right):
    return lax.dot_general(
        left, right, (((1,), (1,)), ((), ())), preferred_element_type=jnp.float32
    )


def head_pairs(block):
    return block.reshape(block.shape[0], -1, 2 * HEAD_DIM).transpose(1, 0, 2)


def join_pairs(stack):
    return stack.transpose(1, 0, 2).reshape(stack.shape[1], stack.shape[0] * stack.shape[2])


def masked_scores(query_heads, key_heads, allowed):
    scores = jnp.einsum("qhd,khd->hqk", query_heads, key_heads, preferred_element_type=jnp.float32)
    return jnp.where(allowed[None], scores, -1e30)


def pair_forward(pieces, allowed):
    q_pair, k_pair, v_pair = pieces
    row_count = q_pair.shape[0]
    query_heads = q_pair.reshape(row_count, 2, HEAD_DIM)
    key_heads = k_pair.reshape(row_count, 2, HEAD_DIM)
    value_heads = v_pair.reshape(row_count, 2, HEAD_DIM)
    scores = masked_scores(query_heads, key_heads, allowed)
    row_top = jnp.max(scores, -1, keepdims=True)
    powered = jnp.exp(scores - row_top)
    totals = jnp.sum(powered, -1, keepdims=True)
    probability = halved(powered / totals)
    attended = jnp.einsum(
        "hqk,khd->qhd", probability, value_heads, preferred_element_type=jnp.float32
    )
    return (attended.reshape(row_count, 2 * HEAD_DIM), row_top + jnp.log(totals))


def pair_backward(pieces, allowed):
    q_pair, k_pair, v_pair, g_pair, lse_pair = pieces
    row_count = q_pair.shape[0]
    query_heads = q_pair.reshape(row_count, 2, HEAD_DIM)
    key_heads = k_pair.reshape(row_count, 2, HEAD_DIM)
    value_heads = v_pair.reshape(row_count, 2, HEAD_DIM)
    grad_heads = g_pair.reshape(row_count, 2, HEAD_DIM)
    probability = jnp.exp(masked_scores(query_heads, key_heads, allowed) - lse_pair)
    d_prob = jnp.einsum("qhd,khd->hqk", grad_heads, value_heads, preferred_element_type=jnp.float32)
    row_inner = jnp.sum(probability * d_prob, -1, keepdims=True)
    d_scores = halved(probability * (d_prob - row_inner))
    d_query = halved(
        jnp.einsum("hqk,khd->qhd", d_scores, key_heads, preferred_element_type=jnp.float32)
    )
    d_query = d_query * jnp.bfloat16(HEAD_DIM ** (-0.5))
    d_key = halved(
        jnp.einsum("hqk,qhd->khd", d_scores, query_heads, preferred_element_type=jnp.float32)
    )
    d_value = halved(
        jnp.einsum(
            "hqk,qhd->khd", halved(probability), grad_heads, preferred_element_type=jnp.float32
        )
    )
    width_pair = 2 * HEAD_DIM
    return (
        d_query.reshape(row_count, width_pair),
        d_key.reshape(row_count, width_pair),
        d_value.reshape(row_count, width_pair),
    )


LINE, PLANE = 4, 8

def place():
    me = lax.axis_index("dev")
    core = me % 2
    x = (me // 2) % 2
    y = (me // 4) % 2
    z = me // PLANE
    a_bit = x * (1 - core) + y * core
    b_bit = y * (1 - core) + x * core
    a_step = (2 + 2 * core) * (1 - 2 * a_bit)
    b_step = (4 - 2 * core) * (1 - 2 * b_bit)
    return me, z, core, a_step, b_step, x, y


def remote(src, dst, send_sem, recv_sem, device):
    return pltpu.make_async_remote_copy(
        src_ref=src, dst_ref=dst, send_sem=send_sem, recv_sem=recv_sem, device_id=(device,), device_id_type=MESH
    )


def wait_for(ref, sem):
    pltpu.make_async_copy(ref, ref, sem).wait()


def entry_barrier(z, devices, up, down, far):
    bar = pltpu.get_barrier_semaphore()
    for dev in devices:
        pl.semaphore_signal(bar, inc=1, device_id=(dev,), device_id_type=MESH)

    @pl.when(z < LINE - 1)
    def _():
        pl.semaphore_signal(bar, inc=1, device_id=(up,), device_id_type=MESH)

    @pl.when(z > 0)
    def _():
        pl.semaphore_signal(bar, inc=1, device_id=(down,), device_id_type=MESH)

    pl.semaphore_signal(bar, inc=1, device_id=(far,), device_id_type=MESH)
    count = len(devices) + 1
    inner = (z > 0) & (z < LINE - 1)

    @pl.when(inner)
    def _():
        pl.semaphore_wait(bar, count + 2)

    @pl.when(jnp.logical_not(inner))
    def _():
        pl.semaphore_wait(bar, count + 1)


class Vec:
    def __init__(self, held, got, send, recv):
        me, z, core, _, _, x, y = place()
        self.to = [
            me + 1 - 2 * core,
            me + 2 - 4 * x,
            me + 4 - 8 * y,
            me + 8 - 16 * (z % 2),
            me + 16 - 32 * (z // 2),
        ]
        self.held, self.got, self.send, self.recv = held, got, send, recv

    def copy(self, i):
        return remote(self.held.at[i], self.got.at[i], self.send.at[i], self.recv.at[i], self.to[i])

    def start(self, i):
        self.copy(i).start()

    def step(self, i):
        self.copy(i).wait()
        self.held[i + 1] = self.held[i] + self.got[i]
        if i < 4:
            self.start(i + 1)


class Gather:
    def __init__(self, piece, shard, full, z_first, send, recv, core_recv, own):
        self.p, self.shard, self.full, self.z_first = piece, shard, full, z_first
        self.send, self.recv, self.core_recv, self.own_sem = send, recv, core_recv, own
        self.rows = shard.shape[0]
        self.me, self.z, self.core, self.a_step, self.b_step, _, _ = place()
        self.sib = self.me + 1 - 2 * self.core

    def block(self, dev):
        return self.full.at[pl.ds(pl.multiple_of(dev * self.rows, self.rows), self.rows)]

    def ici(self, src, dev, way, to):
        remote(src, self.block(dev), self.send.at[self.p, way], self.recv.at[self.p, dev // 2], to).start()

    def to_a(self, src, dev):
        self.ici(src, dev, 0, self.me + self.a_step)

    def to_b(self, src, dev):
        self.ici(src, dev, 1, self.me + self.b_step)

    def to_core(self, src, dev):
        remote(src, self.block(dev), self.send.at[self.p, 2], self.core_recv.at[self.p], self.sib).start()

    def up(self, src, dev):
        @pl.when(self.z < LINE - 1)
        def _():
            self.ici(src, dev, 3, self.me + PLANE)

    def down(self, src, dev):
        @pl.when(self.z > 0)
        def _():
            self.ici(src, dev, 3, self.me - PLANE)

    def arrive(self, dev):
        wait_for(self.block(dev), self.recv.at[self.p, dev // 2])

    def own(self):
        pltpu.make_async_copy(self.shard, self.block(self.me), self.own_sem.at[self.p]).start()
        src = self.shard
        if self.z_first:
            self.up(src, self.me)
            self.down(src, self.me)
            self.to_a(src, self.me)
        else:
            self.to_a(src, self.me)
            self.up(src, self.me)
            self.down(src, self.me)
        self.to_b(src, self.me)
        self.to_core(src, self.me)

    def from_a(self, k=None):
        if not self.z_first:
            dev = self.me + self.a_step
            self.arrive(dev)
            src = self.block(dev)
            self.up(src, dev)
            self.down(src, dev)
            self.to_b(src, dev)
            self.to_core(src, dev)
            return

        def one(dev):
            self.arrive(dev)
            src = self.block(dev)
            self.to_b(src, dev)
            self.to_core(src, dev)

        self.sides(k, lambda off: one(self.me + self.a_step + off))

    def sides(self, k, fn):
        if k == 0:
            fn(0)
            return

        @pl.when(self.z >= k)
        def _():
            fn(-PLANE * k)

        @pl.when(self.z + k <= LINE - 1)
        def _():
            fn(PLANE * k)

    def from_z(self, k):
        for base in [self.me] if self.z_first else [self.me, self.me + self.a_step]:

            @pl.when(self.z >= k)
            def _():
                dev = base - PLANE * k
                self.arrive(dev)
                src = self.block(dev)
                self.up(src, dev)
                if self.z_first:
                    self.to_a(src, dev)
                self.to_b(src, dev)
                self.to_core(src, dev)

            @pl.when(self.z + k <= LINE - 1)
            def _():
                dev = base + PLANE * k
                self.arrive(dev)
                src = self.block(dev)
                self.down(src, dev)
                if self.z_first:
                    self.to_a(src, dev)
                self.to_b(src, dev)
                self.to_core(src, dev)

    def from_b(self, k):
        for base in [self.me + self.b_step, self.me + self.b_step + self.a_step]:

            def one(off):
                dev = base + off
                self.arrive(dev)
                self.to_core(self.block(dev), dev)

            self.sides(k, one)

    def many(self, count):
        return self.full.at[pl.ds(0, count * self.rows)]

    def ready(self):
        wait_for(self.shard, self.own_sem.at[self.p])
        wait_for(self.many(16), self.core_recv.at[self.p])

    def drain(self):
        a_count = 4 if self.z_first else 1
        z_unit = 1 if self.z_first else 2
        wait_for(self.many(a_count), self.send.at[self.p, 0])
        wait_for(self.many(8), self.send.at[self.p, 1])
        wait_for(self.many(16), self.send.at[self.p, 2])
        inner = (self.z > 0) & (self.z < LINE - 1)

        @pl.when(inner)
        def _():
            wait_for(self.many(5 * z_unit), self.send.at[self.p, 3])

        @pl.when(jnp.logical_not(inner))
        def _():
            wait_for(self.many(z_unit), self.send.at[self.p, 3])


def add_blocks(dst, terms, rows):
    def body(i, carry):
        r = pl.multiple_of(i * 16, 16)
        total = terms[0][pl.ds(r, 16), :].astype(jnp.float32)
        for term in terms[1:]:
            total = total + term[pl.ds(r, 16), :].astype(jnp.float32)
        dst[pl.ds(r, 16), :] = total.astype(dst.dtype)
        return carry

    lax.fori_loop(0, rows // 16, body, 0)


class Scatter:
    def __init__(self, piece, grad, out, z_first, mine, sib_buf, b_buf, z_buf, a_buf, send, load, c_recv, b_recv, z_recv, a_recv):
        self.p, self.grad, self.out, self.z_first = piece, grad, out, z_first
        self.mine, self.sib_buf, self.b_buf, self.z_buf, self.a_buf = mine, sib_buf, b_buf, z_buf, a_buf
        self.send, self.load, self.c_recv, self.b_recv, self.z_recv, self.a_recv = send, load, c_recv, b_recv, z_recv, a_recv
        self.rows = out.shape[0]
        self.me, self.z, self.core, self.a_step, self.b_step, self.x, self.y = place()
        self.sib = self.me + 1 - 2 * self.core

    def block(self, dev):
        return self.grad.at[pl.ds(pl.multiple_of(dev * self.rows, self.rows), self.rows)]

    def sides(self, k, fn):
        if k == 0:
            fn(0)
            return

        @pl.when(self.z >= k)
        def _():
            fn(-k)

        @pl.when(self.z + k <= LINE - 1)
        def _():
            fn(k)

    def order(self):
        return [3, 2, 1, 0]

    def exchange(self):
        def one(dev):
            chip = dev // 2
            pltpu.make_async_copy(self.block(dev), self.mine.at[chip], self.load.at[self.p, chip]).start()
            sdev = dev + 1 - 2 * self.core
            remote(self.block(sdev), self.sib_buf.at[chip], self.send.at[self.p, 2], self.c_recv.at[self.p, chip], self.sib).start()

        for b in (self.b_step, 0):
            for k in self.order():
                for a in (self.a_step, 0):
                    self.sides(k, lambda s: one(self.me + b + a + PLANE * s))

    def local(self, dev):
        chip = dev // 2
        wait_for(self.mine.at[chip], self.load.at[self.p, chip])
        wait_for(self.sib_buf.at[chip], self.c_recv.at[self.p, chip])
        return [self.mine.at[chip], self.sib_buf.at[chip]]

    def send_b(self, k):
        for a in (self.a_step, 0):

            def one(s):
                dev = self.me + self.b_step + a + PLANE * s
                chip = dev // 2
                terms = self.local(dev)
                add_blocks(self.mine.at[chip], terms, self.rows)
                slot = self.b_slot(dev)
                remote(self.mine.at[chip], self.b_buf.at[slot], self.send.at[self.p, 1], self.b_recv.at[self.p, slot], self.me + self.b_step).start()

            self.sides(k, one)

    def b_slot(self, dev):
        x = (dev // 2) % 2
        y = (dev // 4) % 2
        a_bit = x * (1 - self.core) + y * self.core
        return (dev // PLANE) * 2 + a_bit

    def after_b(self, dev):
        slot = self.b_slot(dev)
        wait_for(self.b_buf.at[slot], self.b_recv.at[self.p, slot])
        return self.local(dev) + [self.b_buf.at[slot]]

    def a_slot(self, dev):
        return dev // PLANE if self.z_first else 0

    def send_a(self, dev, terms):
        chip = dev // 2
        add_blocks(self.mine.at[chip], terms, self.rows)
        slot = self.a_slot(dev)
        remote(self.mine.at[chip], self.a_buf.at[slot], self.send.at[self.p, 0], self.a_recv.at[self.p, slot], self.me + self.a_step).start()

    def send_a_early(self, k):
        def one(s):
            dev = self.me + self.a_step + PLANE * s
            self.send_a(dev, self.after_b(dev))

        self.sides(k, one)

    def after_a(self, dev):
        slot = self.a_slot(dev)
        wait_for(self.a_buf.at[slot], self.a_recv.at[self.p, slot])
        return [self.a_buf.at[slot]]

    def z_index(self, i, dest):
        return i * 5 + dest

    def along_z(self, k):
        for i, a in [(0, 0)] if self.z_first else [(1, self.a_step), (0, 0)]:
            for sign in (-1, 1):

                @pl.when((self.z >= k) if sign < 0 else (self.z + k <= LINE - 1))
                def _():
                    dev = self.me + a + sign * PLANE * k
                    chip = dev // 2
                    dest = self.z + sign * k
                    terms = self.after_b(dev)
                    if self.z_first:
                        terms = terms + self.after_a(dev)
                    slot = self.z_index(i, dest)
                    last = k == 1
                    there = self.z_index(i, LINE) if (last and sign > 0) else slot
                    more = (self.z < LINE - 1) if sign < 0 else (self.z > 0)

                    @pl.when(more)
                    def _():
                        wait_for(self.z_buf.at[slot], self.z_recv.at[self.p, slot])
                        add_blocks(self.mine.at[chip], terms + [self.z_buf.at[slot]], self.rows)

                    @pl.when(jnp.logical_not(more))
                    def _():
                        add_blocks(self.mine.at[chip], terms, self.rows)

                    remote(self.mine.at[chip], self.z_buf.at[there], self.send.at[self.p, 3], self.z_recv.at[self.p, there], self.me + sign * PLANE).start()

    def at_home(self, i, a):
        dev = self.me + a
        chip = dev // 2
        terms = self.after_b(dev)
        if self.z_first:
            terms = terms + self.after_a(dev)
        above = self.z_index(i, self.z)
        below = self.z_index(i, LINE)
        def finish(terms):
            if i == 1:
                add_blocks(self.mine.at[chip], terms, self.rows)
            else:
                if not self.z_first:
                    terms = terms + self.after_a(dev)
                add_blocks(self.out, terms, self.rows)

        for has_above, has_below, cond in (
            (True, False, self.z == 0),
            (True, True, (self.z > 0) & (self.z < LINE - 1)),
            (False, True, self.z == LINE - 1),
        ):

            @pl.when(cond)
            def _():
                more = list(terms)
                if has_above:
                    wait_for(self.z_buf.at[above], self.z_recv.at[self.p, above])
                    more.append(self.z_buf.at[above])
                if has_below:
                    wait_for(self.z_buf.at[below], self.z_recv.at[self.p, below])
                    more.append(self.z_buf.at[below])
                finish(more)

        if i == 1:
            remote(self.mine.at[chip], self.a_buf.at[0], self.send.at[self.p, 0], self.a_recv.at[self.p, 0], self.me + self.a_step).start()

    def stages(self):
        first = [functools.partial(self.send_b, k) for k in self.order()]
        second = []
        if self.z_first:
            second += [functools.partial(self.send_a_early, k) for k in self.order()]
            second += [functools.partial(self.along_z, k) for k in (3, 2, 1)]
            third = [functools.partial(self.at_home, 0, 0)]
        else:
            second += [functools.partial(self.along_z, k) for k in (3, 2, 1)]
            second += [functools.partial(self.at_home, 1, self.a_step)]
            third = [functools.partial(self.at_home, 0, 0)]
        return first, second, third

    def drain(self):
        wait_for(self.mine, self.send.at[self.p, 2])
        wait_for(self.mine.at[pl.ds(0, 8)], self.send.at[self.p, 1])
        wait_for(self.mine.at[pl.ds(0, 4 if self.z_first else 1)], self.send.at[self.p, 0])
        wait_for(self.mine.at[pl.ds(0, 3 if self.z_first else 6)], self.send.at[self.p, 3])


def peers():
    me, z, core, a_step, b_step, x, y = place()
    near = [me + 1 - 2 * core, me + a_step, me + b_step]
    return z, near, me + PLANE, me - PLANE, me + 16 - 32 * (z // 2)


Z_FIRST = (False, False, True, False)


def gather_kernel(shards, vec, fulls, vec_out, held, got, send, recv, core_recv, own, vsend, vrecv):
    z, near, up, down, far = peers()
    entry_barrier(z, near, up, down, far)
    held[0] = vec[...]
    v = Vec(held, got, vsend, vrecv)
    v.start(0)
    q, o, u, d = [Gather(p, shards[p], fulls[p], Z_FIRST[p], send, recv, core_recv, own) for p in range(4)]
    q.own(); o.own()
    v.step(0)
    q.from_a(); o.from_a()
    v.step(1)
    u.own()
    q.from_z(1); o.from_z(1)
    v.step(2)
    u.from_z(1)
    q.from_z(2); o.from_z(2)
    v.step(3)
    u.from_z(2)
    d.own()
    q.from_z(3); o.from_z(3)
    v.step(4)
    u.from_z(3)
    d.from_a()
    for k in range(4):
        q.from_b(k); o.from_b(k)
    u.from_a(0)
    d.from_z(1)
    u.from_a(1)
    d.from_z(2)
    u.from_a(2)
    d.from_z(3)
    u.from_a(3)
    for k in range(4):
        u.from_b(k); d.from_b(k)
    vec_out[...] = held[5]
    for g in (q, o, u, d):
        g.ready()
    for g in (q, o, u, d):
        g.drain()


def gather_all(shards, vec):
    count = len(shards)
    n = 32

    def kernel(*refs):
        sh, v = refs[:count], refs[count]
        fulls, vo = refs[count + 1 : 2 * count + 1], refs[2 * count + 1]
        gather_kernel(sh, v, fulls, vo, *refs[2 * count + 2 :])

    anyspec = pl.BlockSpec(memory_space=pl.ANY)
    vm = pl.BlockSpec(memory_space=pltpu.VMEM)
    dma = pltpu.SemaphoreType.DMA
    return pl.pallas_call(
        kernel,
        out_shape=[jax.ShapeDtypeStruct((n * s.shape[0], s.shape[1]), s.dtype) for s in shards] + [jax.ShapeDtypeStruct(vec.shape, vec.dtype)],
        in_specs=[anyspec] * count + [vm],
        out_specs=[anyspec] * count + [vm],
        scratch_shapes=[
            pltpu.VMEM((6,) + vec.shape, jnp.float32),
            pltpu.VMEM((5,) + vec.shape, jnp.float32),
            dma((count, 4)), dma((count, 16)), dma((count,)), dma((count,)), dma((5,)), dma((5,)),
        ],
        compiler_params=pltpu.CompilerParams(collective_id=0, has_side_effects=True),
    )(*shards, vec)


def scatter_kernel(grads, vec, outs, vec_out, bufs, held, got, send, load, c_recv, b_recv, z_recv, a_recv, vsend, vrecv, order):
    z, near, up, down, far = peers()
    entry_barrier(z, near, up, down, far)
    pieces = {}
    for p in order:
        pieces[p] = Scatter(p, grads[p], outs[p], Z_FIRST[p], *bufs[5 * p : 5 * p + 5], send, load, c_recv, b_recv, z_recv, a_recv)
        pieces[p].exchange()
    held[0] = vec[...]
    v = Vec(held, got, vsend, vrecv)
    v.start(0)
    st = [pieces[p].stages() for p in order]
    seq = []
    n = len(order)
    for i in range(n + 2):
        groups = []
        if i < n:
            groups.append(st[i][0])
        if 0 <= i - 1 < n:
            groups.append(st[i - 1][1])
        if 0 <= i - 2 < n:
            groups.append(st[i - 2][2])
        longest = max(len(g) for g in groups)
        for j in range(longest):
            for g in groups:
                if j < len(g):
                    seq.append(g[j])
    step = 0
    for i, fn in enumerate(seq):
        fn()
        if i % 4 == 3 and step < 5:
            v.step(step)
            step += 1
    vec_out[...] = held[5]
    for p in order:
        pieces[p].drain()


def scatter_all(grads, vec):
    count = len(grads)
    n = 32

    def kernel(*refs):
        gr, v = refs[:count], refs[count]
        outs, vo = refs[count + 1 : 2 * count + 1], refs[2 * count + 1]
        rest = refs[2 * count + 2 :]
        scatter_kernel(gr, v, outs, vo, rest[: 5 * count], *rest[5 * count :], order=(3, 2, 1, 0))

    anyspec = pl.BlockSpec(memory_space=pl.ANY)
    vm = pl.BlockSpec(memory_space=pltpu.VMEM)
    dma = pltpu.SemaphoreType.DMA
    bufs = []
    for p, g in enumerate(grads):
        blk = (g.shape[0] // n, g.shape[1])
        zf = Z_FIRST[p]
        bufs += [pltpu.VMEM((c,) + blk, jnp.bfloat16) for c in (16, 16, 8, 5 if zf else 10, 4 if zf else 1)]
    return pl.pallas_call(
        kernel,
        out_shape=[jax.ShapeDtypeStruct((g.shape[0] // n, g.shape[1]), jnp.float32) for g in grads] + [jax.ShapeDtypeStruct(vec.shape, vec.dtype)],
        in_specs=[anyspec] * count + [vm],
        out_specs=[vm] * (count + 1),
        scratch_shapes=bufs
        + [
            pltpu.VMEM((6,) + vec.shape, jnp.float32),
            pltpu.VMEM((5,) + vec.shape, jnp.float32),
            dma((count, 4)), dma((count, 16)), dma((count, 16)), dma((count, 8)), dma((count, 10)), dma((count, 4)), dma((5,)), dma((5,)),
        ],
        compiler_params=pltpu.CompilerParams(collective_id=1, has_side_effects=True, vmem_limit_bytes=56 << 20),
    )(*grads, vec)

VECTOR_ROWS = 16


def spread_vectors(parts, position, count):
    rows = []
    for part in parts:
        size = part.shape[0]
        whole = jnp.where(
            (jnp.arange(count) == position)[:, None], halved(part).astype(jnp.float32)[None], 0.0
        )
        rows.append(whole.reshape(size * count))
    return jnp.concatenate(rows)


def local_math(tokens, segments, cotangent, vectors, weights):
    gain_one, bias_one, mix_bias, proj_bias, gain_two, bias_two, up_bias, down_bias = vectors
    mix_weight, proj_weight, up_weight, down_weight = weights
    model_width = tokens.shape[1]
    valid_slot = segments < IMG_DEV
    allowed = (segments[:, None] == segments[None, :]) & valid_slot[None, :]
    gain_one_f = gain_one.astype(jnp.float32)
    bias_one_f = bias_one.astype(jnp.float32)
    first = halved(layer_norm(tokens, gain_one_f, bias_one_f))
    mix_bias_f = mix_bias.astype(jnp.float32)
    bias_row = jnp.concatenate(
        [mix_bias_f[:model_width], jnp.zeros((model_width,), jnp.float32), mix_bias_f[model_width:]]
    )
    projected = jnp.dot(first, mix_weight, preferred_element_type=jnp.float32) + bias_row
    queries = halved(projected[:, :model_width] * HEAD_DIM ** (-0.5))
    key_rows = halved(projected[:, model_width : 2 * model_width])
    values = halved(projected[:, 2 * model_width :])
    attended_stack, lse_stack = lax.map(
        lambda pieces: pair_forward(pieces, allowed),
        (head_pairs(queries), head_pairs(key_rows), head_pairs(values)),
    )
    attended = halved(join_pairs(attended_stack))
    residual = (
        tokens
        + jnp.dot(attended, proj_weight, preferred_element_type=jnp.float32)
        + proj_bias.astype(jnp.float32)
    )
    gain_two_f = gain_two.astype(jnp.float32)
    bias_two_f = bias_two.astype(jnp.float32)
    second = halved(layer_norm(residual, gain_two_f, bias_two_f))
    inner = jnp.dot(second, up_weight, preferred_element_type=jnp.float32) + up_bias.astype(
        jnp.float32
    )
    active = halved(jax.nn.gelu(inner, approximate=False))
    branch = jnp.dot(active, down_weight, preferred_element_type=jnp.float32) + down_bias.astype(
        jnp.float32
    )
    activations = jnp.where(valid_slot[:, None], residual + branch, 0.0)
    d_out = jnp.where(valid_slot[:, None], cotangent, 0.0)
    d_mlp = halved(d_out)
    grad_fc2_bias = jnp.sum(d_mlp, 0, dtype=jnp.float32)
    grad_fc2_weight = contract_rows(active, d_mlp)
    d_active = contract_cols(d_mlp, down_weight)
    gelu_back = jax.vjp(partial(jax.nn.gelu, approximate=False), inner)[1]
    d_inner = halved(gelu_back(d_active)[0])
    grad_fc1_bias = jnp.sum(d_inner, 0, dtype=jnp.float32)
    grad_fc1_weight = contract_rows(second, d_inner)
    d_second = contract_cols(d_inner, up_weight)
    norm_two_back = jax.vjp(layer_norm, residual, gain_two_f, bias_two_f)[1]
    d_norm2, grad_norm2_gain, grad_norm2_bias = norm_two_back(d_second)
    d_resid = d_out + d_norm2
    d_branch = halved(d_resid)
    grad_out_bias = jnp.sum(d_branch, 0, dtype=jnp.float32)
    grad_out_weight = contract_rows(attended, d_branch)
    d_attended = halved(contract_cols(d_branch, proj_weight))
    d_query_stack, d_key_stack, d_value_stack = lax.map(
        lambda pieces: pair_backward(pieces, allowed),
        (
            head_pairs(queries),
            head_pairs(key_rows),
            head_pairs(values),
            head_pairs(d_attended),
            lse_stack,
        ),
    )
    d_query = join_pairs(d_query_stack)
    d_value = join_pairs(d_value_stack)
    d_projected = jnp.concatenate([d_query, join_pairs(d_key_stack), d_value], 1)
    grad_qv_bias = jnp.concatenate(
        [jnp.sum(d_query, 0, dtype=jnp.float32), jnp.sum(d_value, 0, dtype=jnp.float32)]
    )
    grad_qkv_weight = contract_rows(first, d_projected)
    d_first = contract_cols(d_projected, mix_weight)
    norm_one_back = jax.vjp(layer_norm, tokens, gain_one_f, bias_one_f)[1]
    d_norm1, grad_norm1_gain, grad_norm1_bias = norm_one_back(d_first)
    input_grad = d_resid + d_norm1
    return (
        activations,
        input_grad,
        (grad_qkv_weight, grad_out_weight, grad_fc1_weight, grad_fc2_weight),
        (
            grad_norm1_gain,
            grad_norm1_bias,
            grad_qv_bias,
            grad_out_bias,
            grad_norm2_gain,
            grad_norm2_bias,
            grad_fc1_bias,
            grad_fc2_bias,
        ),
    )


def shards(count, tokens,
    segments,
    norm1_gain,
    norm1_bias,
    qkv_weight,
    qv_bias,
    out_weight,
    out_bias,
    norm2_gain,
    norm2_bias,
    fc1_weight,
    fc1_bias,
    fc2_weight,
    fc2_bias,
    cotangent,
):
    vector_shards = (norm1_gain, norm1_bias, qv_bias, out_bias, norm2_gain, norm2_bias, fc1_bias, fc2_bias)
    weight_shards = tuple(halved(w) for w in (qkv_weight, out_weight, fc1_weight, fc2_weight))
    sizes = [v.shape[0] * count for v in vector_shards]
    starts = [sum(sizes[:i]) for i in range(len(sizes) + 1)]
    width = tokens.shape[1]
    position = lax.axis_index("dev")
    kernels = count == 32

    def packed(flat):
        rows = flat.reshape(-1, width)
        return jnp.pad(rows, ((0, VECTOR_ROWS - rows.shape[0]), (0, 0)))

    if kernels:
        *weights, vector_rows = gather_all(
            weight_shards, packed(spread_vectors(vector_shards, position, count))
        )
        flat = vector_rows.reshape(-1)
        vectors = [flat[starts[i] : starts[i + 1]] for i in range(len(sizes))]
    else:
        weights = [lax.all_gather(w, "dev", axis=0, tiled=True) for w in weight_shards]
        vectors = [
            lax.all_gather(halved(v), "dev", axis=0, tiled=True).astype(jnp.float32)
            for v in vector_shards
        ]
    activations, input_grad, weight_grads, vector_grads = local_math(
        tokens, segments, cotangent, vectors, weights
    )
    if kernels:
        *weight_owned, vector_rows = scatter_all(
            [halved(g) for g in weight_grads], packed(jnp.concatenate(vector_grads))
        )
        flat = vector_rows.reshape(-1)
        vector_owned = [
            lax.dynamic_slice(flat, (starts[i] + position * (sizes[i] // count),), (sizes[i] // count,))
            for i in range(len(sizes))
        ]
    else:
        weight_owned = [
            lax.psum_scatter(g, "dev", scatter_dimension=0, tiled=True) for g in weight_grads
        ]
        vector_owned = [
            lax.psum_scatter(g, "dev", scatter_dimension=0, tiled=True) for g in vector_grads
        ]
    g1, b1, qvb, ob, g2, b2, f1b, f2b = vector_owned
    qkv_g, out_g, fc1_g, fc2_g = weight_owned
    return (activations, input_grad, g1, b1, qkv_g, qvb, out_g, ob, g2, b2, fc1_g, f1b, fc2_g, f2b)


def solution(mesh):
    in_specs = (
        P("dev", None),
        P("dev"),
        P("dev"),
        P("dev"),
        P("dev", None),
        P("dev"),
        P("dev", None),
        P("dev"),
        P("dev"),
        P("dev"),
        P("dev", None),
        P("dev"),
        P("dev", None),
        P("dev"),
        P("dev", None),
    )
    out_specs = (
        P("dev", None),
        P("dev", None),
        P("dev"),
        P("dev"),
        P("dev", None),
        P("dev"),
        P("dev", None),
        P("dev"),
        P("dev"),
        P("dev"),
        P("dev", None),
        P("dev"),
        P("dev", None),
        P("dev"),
    )
    return jax.shard_map(
        partial(shards, mesh.size), mesh=mesh, in_specs=in_specs, out_specs=out_specs, check_vma=False)
```

time: 1280 us -> 420 us (0.33)
  waiting for transfers between devices: 852 us -> 0 us
  Pallas kernels: 0 us -> 225 us
  blocking collectives: 203 us -> 0 us
  matrix products: 119 us -> 97.6 us
  between operations: 15.2 us -> 1.37 us
    reduce_scatter x4 -> x0, waiting for transfers between devices: 566 us -> none  [the longest x1 185 us: shards(): lax.psum_scatter(grad_fc1_weight, 'dev', scatter_dimension=0, tiled=True)]
    all_gather x8 -> x0, waiting for transfers between devices: 285 us -> none  [the longest x1 76.9 us: shards(): lax.all_gather(mlp_shards[2], 'dev', axis=0, tiled=True)]
    pallas_call x0 -> x2, Pallas kernels: none -> 225 us  [the longest x1 117 us: scatter_all(): pl.pallas_call(kernel, out_shape=[jax.ShapeDtypeStruct((g.shape[0] // n,...]
    unnamed x4 -> x0, blocking collectives: 163 us -> none
    all_gather x1 -> x0, blocking collectives: 40.6 us -> none  [shards(): lax.all_gather(mlp_shards[3], 'dev', axis=0, tiled=True)]
    dynamic_slice x48 -> x51, local copies, waits for them, and re-layouts: 37 us -> 31.6 us  [the longest x48 29.8 us: local_math(): lax.map(lambda pieces: pair_forward(pieces, allowed), (head_pairs(queries...]
  transfers between devices with their start and end apart: 12 -> 0, of which waited for: 10 -> 0; matrix products, arithmetic and copies ran while one was open for 15% -> 0% of each run, Pallas kernels for 0% -> 0%
where the time goes in v1:
time: 420 us; the launch traced here: 414 us
  Pallas kernels  225 us (54%)
  matrix products  97.6 us (23%)
  local copies, waits for them, and re-layouts  65.8 us (16%)
  other arithmetic  23.2 us (6%)
    pallas_call x1, Pallas kernels, scatter_all(): pl.pallas_call(kernel, out_shape=[jax.ShapeDtypeStruct((g.shape[0] // n,...  117 us
    pallas_call x1, Pallas kernels, gather_all(): pl.pallas_call(kernel, out_shape=[jax.ShapeDtypeStruct((n * s.shape[0], s...  107 us
    dot_general x4, matrix products, contract_cols(): lax.dot_general(left, right, (((1,), (1,)), ((), ())), preferred_element_...  30 us
    dynamic_slice x48, local copies, waits for them, and re-layouts, local_math(): lax.map(lambda pieces: pair_forward(pieces, allowed), (head_pairs(queries...  29.8 us
    dot_general x4, matrix products, contract_rows(): lax.dot_general(left, right, (((0,), (0,)), ((), ())), preferred_element_...  26.6 us
    dynamic_update_slice x16, local copies, waits for them, and re-layouts, local_math(): lax.map(lambda pieces: pair_backward(pieces, allowed), (head_pairs(querie...  10.9 us
    unnamed x91, local copies, waits for them, and re-layouts  9.28 us
    convert_element_type x14, other arithmetic, halved(): return array_in.astype(jnp.bfloat16)  9.25 us

profile of v1, /device:TPU:0, one launch (start us, length us, event | category | flops | bytes accessed | tf_op | source)
XLA Modules:
  0.0 413.9 jit_solution(3355913677870950636)
XLA Ops:
  5.6 1.8 convert_element_type.154.refs_2_
  7.3 1.8 convert_element_type.155.refs_3_
  9.1 1.7 convert_element_type.152.refs_0_
  11.5 107.3 %shard_map.254 = (bf16[1024,3072]{1,0:T(8,128)(2,1)}, bf16[1024,1024]{1,0:T(8,128)(2,1)}, bf16[1024,4096]{1,0:T(8,128)(2,1)}, bf16[4096,1024]{1,0:T(8,128)(2,1)}, f32[16,1024]{1,0:T(8,128)}) custom-call(bf16[32,3072]{1,0:T(8,128)(2,1)} %convert_element_type.152.refs_0_, bf16[32,1024]{1,0:T(8,128)(2,1)} %convert_element_type.153.refs_1_, ...), custom_call_target="tpu_custom_call" | custom-call | tf_op jit(solution)/shard_map/pallas_call | solution.py:568
  118.7 1.8 fusion.33
  121.0 7.0 %fusion.34 = (bf16[320,3072]{1,0:T(8,128)(2,1)S(1)}, f32[320,3072]{1,0:T(8,128)}) fusion(f32[3072]{0:T(1024)S(1)} %pad_maximum_fusion.3, bf16[1024,3072]{1,0:T(8,128)(2,1)} %get-tuple-element.117, f32[320,1024]{1,0:T(8,128)S(1)} %copy-done, f32[1024]{0:T(1024)S(1)} %bitcast.187, f32[1024]{0:T(1024)S(1)} %bitcast.175, f32[320]{0:T(512)S(1)} %fusion.21, ...), kind=kOutput, calls=%fused_computation.140 | convolution fusion | flops 2016870400 | bytes 13523456 | tf_op jit(solution)/shard_map/dot_general | solution.py:678
  128.1 1.2 copy.43
  129.6 1.4 fusion.19
  131.1 1.2 copy.42
  132.2 21.5 %while.28 = (s32[]{:T(128)}, bf16[8,320,128]{1,2,0:T(8,128)(2,1)}, f32[8,2,320,1]{2,1,3,0:T(2,128)S(1)}, bf16[8,320,128]{1,2,0:T(8,128)(2,1)S(1)}, bf16[8,320,12...) while((s32[]{:T(128)}, bf16[8,320,128]{1,2,0:T(8,128)(2,1)}, ...), condition=%wide.region_5.6_spmd.clone, body=%wide.region_2.5_spmd.clone.sunk | while | flops 54066560 | bytes 3686057 | solution.py:682
  132.4 1.0 constant_dynamic-slice_fusion.14
  135.1 1.0 constant_dynamic-slice_fusion.14
  137.8 1.0 constant_dynamic-slice_fusion.14
  140.4 1.0 constant_dynamic-slice_fusion.14
  143.1 1.0 constant_dynamic-slice_fusion.14
  145.8 1.0 constant_dynamic-slice_fusion.14
  148.5 1.0 constant_dynamic-slice_fusion.14
  151.1 1.0 constant_dynamic-slice_fusion.14
  153.8 2.8 fusion.35
  156.9 1.0 slice_bitcast_fusion
  158.0 5.6 %convolution_add_fusion = f32[320,4096]{1,0:T(8,128)S(1)} fusion(bf16[1024,4096]{1,0:T(8,128)(2,1)} %get-tuple-element.120, f32[4096]{0:T(1024)S(1)} %bitcast.183, f32[320,1024]{1,0:T(8,128)S(1)} %get-tuple-element.265, f32[1024]{0:T(1024)S(1)} %bitcast.189, f32[1024]{0:T(1024)S(1)} %bitcast.179, f32[320]{0:T(512)S(1)} %fusion.22, ...), kind=kOutput, calls=%fused_computation.36 | convolution fusion | flops 2687303680 | bytes 14969344 | tf_op jit(solution)/shard_map/dot_general | solution.py:695
  163.9 16.5 %convert_reduce_fusion = (f32[4096]{0:T(1024)S(1)}, bf16[320,4096]{1,0:T(8,128)(2,1)S(1)}, f32[320,4096]{1,0:T(8,128)}) fusion(f32[320,4096]{1,0:T(8,128)S(1)} %convolution_add_fusion, bf16[320,1024]{1,0:T(8,128)(2,1)S(1)} %get-tuple-element.222, bf16[4096,1024]{1,0:T(8,128)(2,1)S(1)} %bitcast.192), kind=kOutput, calls=%fused_computation.38 | convolution fusion | flops 2781343744 | bytes 22167552 | tf_op jit(solution)/shard_map/dot_general | solution.py:33
  180.4 3.7 multiply_reduce_fusion.1
  184.9 1.0 copy-done.1
  186.7 1.7 convolution_convert_fusion.7
  188.4 2.3 copy.44
  190.7 48.6 %while.29 = (s32[]{:T(128)}, bf16[8,320,128]{1,2,0:T(8,128)(2,1)}, bf16[8,320,128]{1,2,0:T(8,128)(2,1)}, bf16[8,320,128]{1,2,0:T(8,128)(2,1)}, bf16[8,320,128]{1...) while((s32[]{:T(128)}, bf16[8,320,128]{1,2,0:T(8,128)(2,1)}, ...), condition=%wide.region_12.13_spmd.clone, body=%wide.region_10.12_spmd.clone.sunk | while | flops 133078400 | bytes 8379593 | solution.py:720
  192.0 0.9 constant_dynamic-slice_fusion.15
  198.0 0.9 constant_dynamic-slice_fusion.15
  204.1 0.9 constant_dynamic-slice_fusion.15
  210.1 0.9 constant_dynamic-slice_fusion.15
  216.2 0.9 constant_dynamic-slice_fusion.15
  222.3 0.9 constant_dynamic-slice_fusion.15
  228.3 0.9 constant_dynamic-slice_fusion.15
  234.4 0.9 constant_dynamic-slice_fusion.15
  239.4 8.0 %multiply_reduce_fusion.2 = (f32[1024]{0:T(1024)S(1)}, f32[320]{0:T(512)}, f32[1024]{0:T(1024)S(1)}, f32[320,1024]{1,0:T(8,128)}) fusion(f32[320,1024]{1,0:T(8,128)S(1)} %copy-done, f32[320]{0:T(512)S(1)} %fusion.21, f32[320]{0:T(512)S(1)} %broadcast_multiply_fusion.1, f32[1024]{0:T(1024)S(1)} %bitcast.176, bf16[1024,3072]{1,0:T(8,128)(2,1)} %get-tuple-element.117, ...), kind=kOutput, calls=%fused_computation.72 | convolution fusion | flops 2021783296 | bytes 10895104 | tf_op jit(solution)/shard_map/dot_general | solution.py:33
  247.4 1.3 convert_reduce_fusion.2
  249.7 8.9 %convolution_convert_fusion.4.refs_2_ = bf16[1024,4096]{1,0:T(8,128)(2,1)} fusion(bf16[320,4096]{1,0:T(8,128)(2,1)} %copy-done.26, f32[320,1024]{1,0:T(8,128)S(1)} %get-tuple-element.265, f32[1024]{0:T(1024)} %bitcast.190, f32[1024]{0:T(1024)S(1)} %bitcast.182, f32[320]{0:T(512)S(1)} %fusion.22, f32[320]{0:T(512)S(1)} %broadcast_multiply_fusion), kind=kOutput, calls=%fused_computation.34 | convolution fusion | flops 2690187264 | bytes 12331520 | tf_op jit(solution)/shard_map/dot_general | solution.py:27
  258.6 3.9 convolution_convert_fusion.6.refs_1_
  262.5 7.1 %convolution_convert_fusion.5.refs_0_ = bf16[1024,3072]{1,0:T(8,128)(2,1)} fusion(bf16[320,1024]{0,1:T(8,128)(2,1)S(1)} %bitcast.169, bf16[320,1024]{0,1:T(8,128)(2,1)S(1)} %bitcast.196, bf16[320,1024]{0,1:T(8,128)(2,1)} %bitcast.23, f32[320,1024]{1,0:T(8,128)S(1)} %copy-done, f32[1024]{0:T(1024)S(1)} %bitcast.188, f32[1024]{0:T(1024)S(1)} %bitcast.177, ...), kind=kOutput, calls=%fused_computation.35 | convolution fusion | flops 2023948288 | bytes 9579008 | tf_op jit(solution)/shard_map/dot_general | solution.py:27
  269.7 1.1 multiply_convert_fusion.1
  270.8 1.5 copy-done.6
  272.3 6.8 %convolution_convert_fusion.3.refs_3_ = bf16[4096,1024]{1,0:T(8,128)(2,1)} fusion(bf16[320,4096]{1,0:T(8,128)(2,1)S(1)} %multiply_convert_fusion.1, bf16[320,1024]{1,0:T(8,128)(2,1)S(1)} %copy-done.12), kind=kOutput, calls=%fused_computation.33 | convolution fusion | flops 2688548864 | bytes 11665408 | tf_op jit(solution)/shard_map/dot_general | solution.py:27
  279.1 117.5 %shard_map.255 = (f32[32,3072]{1,0:T(8,128)}, f32[32,1024]{1,0:T(8,128)}, f32[32,4096]{1,0:T(8,128)}, f32[128,1024]{1,0:T(8,128)}, f32[16,1024]{1,0:T(8,128)}) custom-call(bf16[1024,3072]{1,0:T(8,128)(2,1)} %convolution_convert_fusion.5.refs_0_, bf16[1024,1024]{1,0:T(8,128)(2,1)} %convolution_convert_fusion.6.refs_1_, ...), custom_call_target="tpu_custom_call" | custom-call | tf_op jit(solution)/shard_map/pallas_call | solution.py:637
  399.2 1.8 fusion.28
  401.1 1.2 add_add_fusion.2
  402.3 0.9 copy-done.7
  403.3 7.4 %fusion.18 = f32[320,1024]{1,0:T(8,128)} fusion(f32[320,1024]{1,0:T(8,128)S(1)} %get-tuple-element.265, bf16[320,4096]{1,0:T(8,128)(2,1)S(1)} %copy-done.7, bf16[4096,1024]{1,0:T(8,128)(2,1)} %get-tuple-element.121, f32[1024]{0:T(1024)S(1)} %bitcast.186, pred[320]{0:T(512)(128)(4,1)S(1)} %get-tuple-element.500), kind=kOutput, calls=%fused_computation.65 | convolution fusion | flops 2685337600 | bytes 13635904 | tf_op jit(solution)/shard_map/dot_general | solution.py:699
  (302 shorter events, 69.1 us)
Async XLA Ops:
  0.6 10.2 %copy-start.16 = (f32[32,1024]{1,0:T(8,128)S(1)}, f32[32,1024]{1,0:T(8,128)}, u32[]{:S(2)}) copy-start(f32[32,1024]{1,0:T(8,128)} %param.25) | copy-start | bytes 393220
  0.7 119.9 %copy-start = (f32[320,1024]{1,0:T(8,128)S(1)}, f32[320,1024]{1,0:T(8,128)}, u32[]{:S(2)}) copy-start(f32[320,1024]{1,0:T(8,128)} %param.19) | copy-start | bytes 3932164
  120.5 7.5 %copy-start.19 = (f32[1,1024]{1,0:T(1,128)}, f32[1,1024]{1,0:T(1,128)S(1)}, u32[]{:S(2)}) copy-start(f32[1,1024]{1,0:T(1,128)S(1)} %get-tuple-element.254) | copy-start | bytes 12292
  120.5 37.4 %copy-start.21 = (f32[1,1024]{1,0:T(1,128)}, f32[1,1024]{1,0:T(1,128)S(1)}, u32[]{:S(2)}) copy-start(f32[1,1024]{1,0:T(1,128)S(1)} %get-tuple-element.249) | copy-start | bytes 12292
  129.3 2.9 copy-start.9
  156.6 7.2 %slice-start.4 = ((s8[8388608]{0:T(1024)(128)(4,1)}), s8[4194304]{0:T(1024)(128)(4,1)S(1)}, s32[]{:S(2)}) async-start(s8[8388608]{0:T(1024)(128)(4,1)} %bitcast.191), calls=%async_computation.4 | async-start | bytes 8388608
  157.9 5.7 %copy-start.5 = (f32[320,1024]{1,0:T(8,128)S(1)}, f32[320,1024]{1,0:T(8,128)}, u32[]{:S(2)}) copy-start(f32[320,1024]{1,0:T(8,128)} %param.33) | copy-start | bytes 3932164
  157.9 5.9 %slice-start.5 = ((s8[8388608]{0:T(1024)(128)(4,1)}), s8[4194304]{0:T(1024)(128)(4,1)S(1)}, s32[]{:S(2)}) async-start(s8[8388608]{0:T(1024)(128)(4,1)} %bitcast.191), calls=%async_computation.5 | async-start | bytes 8388608
  157.9 22.4 %slice-start.6 = ((s8[8388608]{0:T(1024)(128)(4,1)}), s8[4194304]{0:T(1024)(128)(4,1)S(1)}, s32[]{:S(2)}) async-start(s8[8388608]{0:T(1024)(128)(4,1)} %bitcast.193), calls=%async_computation.6 | async-start | bytes 8388608
  163.6 16.8 %copy-start.4 = (f32[320,4096]{1,0:T(8,128)}, f32[320,4096]{1,0:T(8,128)S(1)}, u32[]{:S(2)}) copy-start(f32[320,4096]{1,0:T(8,128)S(1)} %convolution_add_fusion) | copy-start | bytes 15728644
  163.8 16.6 %copy-start.11 = (bf16[320,1024]{1,0:T(8,128)(2,1)}, bf16[320,1024]{1,0:T(8,128)(2,1)S(1)}, u32[]{:S(2)}) copy-start(bf16[320,1024]{1,0:T(8,128)(2,1)S(1)} %get-tuple-element.222) | copy-start | bytes 1966084
  163.9 16.5 %slice-start.7 = ((s8[8388608]{0:T(1024)(128)(4,1)}), s8[4194304]{0:T(1024)(128)(4,1)S(1)}, s32[]{:S(2)}) async-start(s8[8388608]{0:T(1024)(128)(4,1)} %bitcast.193), calls=%async_computation.7 | async-start | bytes 8388608
  180.4 3.8 copy-start.26
  184.6 2.1 copy-start.8
  184.9 1.1 copy-start.1
  239.4 9.4 %copy-start.10 = (bf16[8,320,128]{1,2,0:T(8,128)(2,1)S(1)}, bf16[8,320,128]{1,2,0:T(8,128)(2,1)}, u32[]{:S(2)}) copy-start(bf16[8,320,128]{1,2,0:T(8,128)(2,1)} %get-tuple-element.125) | copy-start | bytes 1966084
  239.4 9.6 %copy-start.23 = (f32[1024]{0:T(1024)S(1)}, f32[1024]{0:T(1024)}, u32[]{:S(2)}) copy-start(f32[1024]{0:T(1024)} %get-tuple-element.177) | copy-start | bytes 12292
  239.4 9.7 %copy-start.22 = (f32[1024]{0:T(1024)S(1)}, f32[1024]{0:T(1024)}, u32[]{:S(2)}) copy-start(f32[1024]{0:T(1024)} %get-tuple-element.181) | copy-start | bytes 12292
  249.7 8.9 %copy-start.2 = (f32[320,1024]{1,0:T(8,128)S(1)}, f32[320,1024]{1,0:T(8,128)}, u32[]{:S(2)}) copy-start(f32[320,1024]{1,0:T(8,128)} %copy-done.1) | copy-start | bytes 3932164
  249.7 12.7 %copy-start.20 = (f32[1,1024]{1,0:T(1,128)S(1)}, f32[1,1024]{1,0:T(1,128)}, u32[]{:S(2)}) copy-start(f32[1,1024]{1,0:T(1,128)} %copy-done.19) | copy-start | bytes 12292
  249.7 12.7 %copy-start.25 = (bf16[8,320,128]{1,2,0:T(8,128)(2,1)S(1)}, bf16[8,320,128]{1,2,0:T(8,128)(2,1)}, u32[]{:S(2)}) copy-start(bf16[8,320,128]{1,2,0:T(8,128)(2,1)} %get-tuple-element.124) | copy-start | bytes 1966084
  258.6 11.0 %slice-start = ((s8[5242880]{0:T(1024)(128)(4,1)}), s8[1048576]{0:T(1024)(128)(4,1)S(1)}, s32[]{:S(2)}) async-start(s8[5242880]{0:T(1024)(128)(4,1)} %bitcast.160), calls=%async_computation | async-start | bytes 2097152
  258.6 11.0 %slice-start.2 = ((s8[5242880]{0:T(1024)(128)(4,1)}), s8[4194304]{0:T(1024)(128)(4,1)S(1)}, s32[]{:S(2)}) async-start(s8[5242880]{0:T(1024)(128)(4,1)} %bitcast.162), calls=%async_computation.2 | async-start | bytes 8388608
  262.5 7.2 %slice-start.1 = ((s8[5242880]{0:T(1024)(128)(4,1)}), s8[4194304]{0:T(1024)(128)(4,1)S(1)}, s32[]{:S(2)}) async-start(s8[5242880]{0:T(1024)(128)(4,1)} %bitcast.160), calls=%async_computation.1 | async-start | bytes 8388608
  262.5 7.2 %slice-start.3 = ((s8[5242880]{0:T(1024)(128)(4,1)}), s8[1048576]{0:T(1024)(128)(4,1)S(1)}, s32[]{:S(2)}) async-start(s8[5242880]{0:T(1024)(128)(4,1)} %bitcast.162), calls=%async_computation.3 | async-start | bytes 2097152
  269.7 2.6 copy-start.12
  270.8 1.5 copy-start.6
  279.1 120.1 %copy-start.24 = (f32[320]{0:T(512)S(1)}, f32[320]{0:T(512)}, u32[]{:S(2)}) copy-start(f32[320]{0:T(512)} %get-tuple-element.180) | copy-start | bytes 3844
  398.6 2.4 copy-start.3
  401.0 2.2 copy-start.7
  401.0 2.2 copy-start.18
  403.2 7.5 %copy-start.15 = (f32[32,3072]{1,0:T(8,128)S(1)}, f32[32,3072]{1,0:T(8,128)}, u32[]{:S(2)}) copy-start(f32[32,3072]{1,0:T(8,128)} %get-tuple-element.487) | copy-start | bytes 1179652
  403.2 8.2 %copy-start.17 = (f32[32,1024]{1,0:T(8,128)S(1)}, f32[32,1024]{1,0:T(8,128)}, u32[]{:S(2)}) copy-start(f32[32,1024]{1,0:T(8,128)} %get-tuple-element.489) | copy-start | bytes 393220
  403.2 8.9 %copy-start.14 = (f32[32,4096]{1,0:T(8,128)S(1)}, f32[32,4096]{1,0:T(8,128)}, u32[]{:S(2)}) copy-start(f32[32,4096]{1,0:T(8,128)} %get-tuple-element.493) | copy-start | bytes 1572868
  403.2 9.7 %copy-start.13 = (f32[128,1024]{1,0:T(8,128)S(1)}, f32[128,1024]{1,0:T(8,128)}, u32[]{:S(2)}) copy-start(f32[128,1024]{1,0:T(8,128)} %get-tuple-element.495) | copy-start | bytes 1572868

commit v2 on v1

--- a/solution.py
+++ b/solution.py
@@ -325,17 +325,410 @@
     lax.fori_loop(0, rows // 16, body, 0)
 
 
-class Scatter:
-    def __init__(self, piece, grad, out, z_first, mine, sib_buf, b_buf, z_buf, a_buf, send, load, c_recv, b_recv, z_recv, a_recv):
-        self.p, self.grad, self.out, self.z_first = piece, grad, out, z_first
-        self.mine, self.sib_buf, self.b_buf, self.z_buf, self.a_buf = mine, sib_buf, b_buf, z_buf, a_buf
-        self.send, self.load, self.c_recv, self.b_recv, self.z_recv, self.a_recv = send, load, c_recv, b_recv, z_recv, a_recv
-        self.rows = out.shape[0]
+def peers():
+    me, z, core, a_step, b_step, x, y = place()
+    near = [me + 1 - 2 * core, me + a_step, me + b_step]
+    return z, near, me + PLANE, me - PLANE, me + 16 - 32 * (z // 2)
+
+
+Z_FIRST = (False, False, True, False)
+
+
+EPS = 1e-06
+PAIR = 128
+TILE = 512
+ROWS = 32
+GAIN_ONE, BIAS_ONE, QUERY_BIAS, VALUE_BIAS, OUT_BIAS, GAIN_TWO, BIAS_TWO, UP_BIAS, DOWN_BIAS = 0, 1, 2, 3, 4, 5, 6, 7, 11
+
+
+def dot(left, right):
+    return jnp.dot(left, right, preferred_element_type=jnp.float32)
+
+
+def dot_nt(left, right):
+    return lax.dot_general(left, right, (((1,), (1,)), ((), ())), preferred_element_type=jnp.float32)
+
+
+def dot_tn(left, right):
+    return lax.dot_general(left, right, (((0,), (0,)), ((), ())), preferred_element_type=jnp.float32)
+
+
+def columns(start, size):
+    return pl.ds(pl.multiple_of(start, 128), size)
+
+
+def loop(count, body):
+    def step(i, carry):
+        body(i)
+        return carry
+
+    lax.fori_loop(0, count, step, 0)
+
+
+def centred(rows):
+    centre = rows - jnp.mean(rows, -1, keepdims=True)
+    spread = jnp.mean(centre * centre, -1, keepdims=True)
+    return centre, lax.rsqrt(spread + EPS)
+
+
+def norm_into(dst, src, vec, gain_row, bias_row):
+    gain = vec[gain_row : gain_row + 1, :]
+    bias = vec[bias_row : bias_row + 1, :]
+
+    def body(i):
+        r = pl.ds(pl.multiple_of(i * ROWS, ROWS), ROWS)
+        centre, scale = centred(src[r, :])
+        dst[r, :] = (centre * scale * gain + bias).astype(dst.dtype)
+
+    loop(src.shape[0] // ROWS, body)
+
+
+def norm_back(d_rows, src, vec, gain_row, sums, emit):
+    gain = vec[gain_row : gain_row + 1, :]
+    sums[...] = jnp.zeros_like(sums)
+
+    def body(i):
+        r = pl.ds(pl.multiple_of(i * ROWS, ROWS), ROWS)
+        centre, scale = centred(src[r, :])
+        n = centre * scale
+        d = d_rows[r, :]
+        e = d * gain
+        dn = d * n
+        for part in range(ROWS // 8):
+            sums[0:8, :] += dn[8 * part : 8 * part + 8, :]
+            sums[8:16, :] += d[8 * part : 8 * part + 8, :]
+        back = scale * (e - jnp.mean(e, -1, keepdims=True) - n * jnp.mean(e * n, -1, keepdims=True))
+        emit(r, back)
+
+    loop(src.shape[0] // ROWS, body)
+
+
+def mask_bias(out, seg_col, seg_row):
+    row = seg_row[...]
+    allowed = (seg_col[...] == row) & (row < IMG_DEV)
+    out[...] = jnp.where(allowed, 0.0, -1e30)
+
+
+def own_half(rows, head):
+    lane = lax.broadcasted_iota(jnp.int32, rows.shape, 1)
+    inside = (lane < HEAD_DIM) if head == 0 else (lane >= HEAD_DIM)
+    return jnp.where(inside, rows, jnp.zeros_like(rows))
+
+
+def halves(first, second):
+    lane = lax.broadcasted_iota(jnp.int32, first.shape, 1)
+    return jnp.where(lane < HEAD_DIM, first, second)
+
+
+def probabilities(query, key, bias):
+    scores = dot_nt(query, key) + bias
+    powered = jnp.exp(scores - jnp.max(scores, -1, keepdims=True))
+    return powered * (1.0 / jnp.sum(powered, -1, keepdims=True))
+
+
+def attend_pair(i, width, qkv, bias, attended):
+    q = qkv[:, columns(i * PAIR, PAIR)]
+    k = qkv[:, columns(width + i * PAIR, PAIR)]
+    v = qkv[:, columns(2 * width + i * PAIR, PAIR)]
+    parts = []
+    for head in (0, 1):
+        p = probabilities(own_half(q, head), k, bias[...]).astype(jnp.bfloat16)
+        parts.append(dot(p, v))
+    attended[:, columns(i * PAIR, PAIR)] = halves(*parts).astype(jnp.bfloat16)
+
+
+class Forward:
+    def __init__(self, width, hidden, tokens, seg_col, seg_row, cotangent, vec, weights, s):
+        self.width, self.hidden = width, hidden
+        self.tokens, self.seg_col, self.seg_row, self.cotangent, self.vec = tokens, seg_col, seg_row, cotangent, vec
+        self.wq, self.wo, self.wu, self.wd = weights
+        self.__dict__.update(s)
+
+    def start(self):
+        mask_bias(self.bias, self.seg_col, self.seg_row)
+        valid = self.seg_col[...] < IMG_DEV
+        self.d_mlp[...] = jnp.where(valid, self.cotangent[...], 0.0).astype(jnp.bfloat16)
+
+    def first_norm(self):
+        norm_into(self.first, self.tokens, self.vec, GAIN_ONE, BIAS_ONE)
+
+    def project(self, part):
+        w = self.width
+
+        def body(j):
+            c = columns(part * w + j * TILE, TILE)
+            out = dot(self.first[...], self.wq[:, c])
+            if part == 0:
+                out = (out + self.vec[QUERY_BIAS : QUERY_BIAS + 1, columns(j * TILE, TILE)]) * HEAD_DIM ** (-0.5)
+            elif part == 2:
+                out = out + self.vec[VALUE_BIAS : VALUE_BIAS + 1, columns(j * TILE, TILE)]
+            self.qkv[:, c] = out.astype(jnp.bfloat16)
+
+        loop(w // TILE, body)
+
+    def attend(self, begin, count):
+        loop(count, lambda i: attend_pair(begin + i, self.width, self.qkv, self.bias, self.attended))
+
+    def project_out(self):
+        def body(j):
+            c = columns(j * TILE, TILE)
+            self.residual[:, c] = (
+                self.tokens[:, c] + dot(self.attended[...], self.wo[:, c]) + self.vec[OUT_BIAS : OUT_BIAS + 1, c]
+            )
+
+        loop(self.width // TILE, body)
+
+    def second_norm(self):
+        norm_into(self.second, self.residual, self.vec, GAIN_TWO, BIAS_TWO)
+
+    def up(self, begin, count):
+        per = self.width // TILE
+
+        def body(n):
+            j = begin + n
+            c = columns(j * TILE, TILE)
+            t = dot(self.second[...], self.wu[:, c])
+            t = t + self.vec[pl.ds(UP_BIAS + j // per, 1), columns((j % per) * TILE, TILE)]
+            cdf = 0.5 + 0.5 * lax.erf(t * (0.5**0.5))
+            act = (t * cdf).astype(jnp.bfloat16)
+            self.active[:, c] = act
+            for part in range(TILE // 128):
+                own = self.split.at[part % 2]
+                own[:, columns((2 * j + part // 2) * 128, 128)] = act[:, 128 * part : 128 * part + 128]
+            self.slope[:, c] = cdf + t * (0.3989422804014327 * jnp.exp(-0.5 * t * t))
+
+        loop(count, body)
+
+    def d_inner_tiles(self, begin, count):
+        per = self.width // TILE
+
+        def body(n):
+            j = begin + n
+            rows = pl.ds(pl.multiple_of(j * TILE, TILE), TILE)
+            c = columns(j * TILE, TILE)
+            d = (dot_nt(self.d_mlp[...], self.wd[rows, :]) * self.slope[:, c]).astype(jnp.bfloat16)
+            self.d_inner[:, c] = d
+            self.gvec[pl.ds(UP_BIAS + j // per, 1), columns((j % per) * TILE, TILE)] = jnp.sum(
+                d.astype(jnp.float32), 0, keepdims=True
+            )
+
+        loop(count, body)
+
+    def down(self):
+        valid = self.seg_col[...] < IMG_DEV
+
+        def body(j):
+            c = columns(j * TILE, TILE)
+            branch = dot(self.active[...], self.wd[:, c]) + self.vec[DOWN_BIAS : DOWN_BIAS + 1, c]
+            self.activations[:, c] = jnp.where(valid, self.residual[:, c] + branch, 0.0)
+            self.gvec[DOWN_BIAS : DOWN_BIAS + 1, c] = jnp.sum(self.d_mlp[:, c].astype(jnp.float32), 0, keepdims=True)
+
+        loop(self.width // TILE, body)
+
+    def d_second_rows(self):
+        size = TILE // 2
+
+        def body(j):
+            rows = pl.ds(pl.multiple_of(j * size, size), size)
+            self.d_norm[:, columns(j * size, size)] = dot_nt(self.d_inner[...], self.wu[rows, :])
+
+        loop(self.width // size, body)
+
+    def second_norm_back(self):
+        def emit(r, back):
+            valid = self.seg_col[r, :] < IMG_DEV
+            d_resid = jnp.where(valid, self.cotangent[r, :], 0.0) + back
+            self.d_resid[r, :] = d_resid
+            self.d_branch[r, :] = d_resid.astype(jnp.bfloat16)
+
+        norm_back(self.d_norm, self.residual, self.vec, GAIN_TWO, self.sums, emit)
+        self.gvec[GAIN_TWO : GAIN_TWO + 1, :] = jnp.sum(self.sums[0:8, :], 0, keepdims=True)
+        self.gvec[BIAS_TWO : BIAS_TWO + 1, :] = jnp.sum(self.sums[8:16, :], 0, keepdims=True)
+
+
+FORWARD_OUT = ("activations", "d_resid", "first", "qkv", "attended", "second", "split", "d_inner", "d_mlp", "d_branch")
+
+
+def forward_all(count, tokens, segments, cotangent, shards, vec, comm=True):
+    rows, width = tokens.shape
+    hidden = shards[2].shape[1]
+    f32, b16 = jnp.float32, jnp.bfloat16
+    kinds = {
+        "activations": ((rows, width), f32),
+        "d_resid": ((rows, width), f32),
+        "first": ((rows, width), b16),
+        "qkv": ((rows, 3 * width), b16),
+        "attended": ((rows, width), b16),
+        "second": ((rows, width), b16),
+        "active": ((rows, hidden), b16),
+        "split": ((2, rows, hidden // 2), b16),
+        "d_branch": ((rows, width), b16),
+        "d_inner": ((rows, hidden), b16),
+        "d_mlp": ((rows, width), b16),
+        "residual": ((rows, width), f32),
+        "slope": ((rows, hidden), f32),
+        "d_norm": ((rows, width), f32),
+        "bias": ((rows, rows), f32),
+        "sums": ((16, width), f32),
+    }
+    names = list(kinds)
+    fulls = [((count * s.shape[0], s.shape[1]), b16) for s in shards]
+
+    def kernel(tok, sc, sr, cot, q_sh, o_sh, u_sh, d_sh, v_in, *refs):
+        outs = dict(zip(FORWARD_OUT, refs[: len(FORWARD_OUT)]))
+        refs = refs[len(FORWARD_OUT) :]
+        wq_out, wo_out, vec_out, gvec = refs[:4]
+        refs = refs[4:]
+        s = dict(zip(names, refs[: len(names)]))
+        refs = refs[len(names) :]
+        weights = refs[:4]
+        held, got, send, recv, core_recv, own, vsend, vrecv, out_sem = refs[4:]
+        s["gvec"] = gvec
+        started = []
+
+        def put(src, dst):
+            copy = pltpu.make_async_copy(src, dst, out_sem.at[len(started)])
+            copy.start()
+            started.append(copy)
+
+        def leave(*which):
+            for name in which:
+                put(s[name], outs[name])
+
+        f = Forward(width, hidden, tok, sc, sr, cot, vec_out, weights, s)
+        z, near, up, down, far = peers()
+        entry_barrier(z, near, up, down, far)
+        held[0] = v_in[...]
+        v = Vec(held, got, vsend, vrecv)
+        v.start(0)
+        q, o, u, d = [
+            Gather(p, sh, weights[p], Z_FIRST[p], send, recv, core_recv, own)
+            for p, sh in enumerate((q_sh, o_sh, u_sh, d_sh))
+        ]
+        gvec[...] = jnp.zeros_like(gvec)
+        q.own()
+        o.own()
+        v.step(0)
+        q.from_a()
+        o.from_a()
+        v.step(1)
+        u.own()
+        q.from_z(1)
+        o.from_z(1)
+        v.step(2)
+        u.from_z(1)
+        q.from_z(2)
+        o.from_z(2)
+        v.step(3)
+        u.from_z(2)
+        d.own()
+        q.from_z(3)
+        o.from_z(3)
+        v.step(4)
+        vec_out[...] = held[5]
+        u.from_z(3)
+        d.from_a()
+        f.start()
+        q.from_b(0)
+        o.from_b(0)
+        q.from_b(1)
+        o.from_b(1)
+        f.first_norm()
+        leave("d_mlp", "first")
+        u.from_a(0)
+        d.from_z(1)
+        q.from_b(2)
+        o.from_b(2)
+        q.from_b(3)
+        o.from_b(3)
+        u.from_a(1)
+        d.from_z(2)
+        q.ready()
+        put(weights[0], wq_out)
+        f.project(0)
+        u.from_a(2)
+        d.from_z(3)
+        f.project(1)
+        u.from_a(3)
+        u.from_b(0)
+        d.from_b(0)
+        f.project(2)
+        leave("qkv")
+        u.from_b(1)
+        d.from_b(1)
+        f.attend(0, 2)
+        u.from_b(2)
+        f.attend(2, 2)
+        u.from_b(3)
+        f.attend(4, 2)
+        d.from_b(2)
+        f.attend(6, 2)
+        leave("attended")
+        o.ready()
+        put(weights[1], wo_out)
+        f.project_out()
+        d.from_b(3)
+        f.second_norm()
+        leave("second")
+        u.ready()
+        f.up(0, hidden // TILE)
+        leave("split")
+        d.ready()
+        f.d_inner_tiles(0, hidden // TILE)
+        leave("d_inner")
+        f.d_second_rows()
+        f.down()
+        leave("activations")
+        f.second_norm_back()
+        leave("d_resid", "d_branch")
+        for g in (q, o, u, d):
+            g.drain()
+        for copy in started:
+            copy.wait()
+
+    anyspec = pl.BlockSpec(memory_space=pl.ANY)
+    vm = pl.BlockSpec(memory_space=pltpu.VMEM)
+    dma = pltpu.SemaphoreType.DMA
+    n = len(shards)
+    shape = jax.ShapeDtypeStruct
+    results = pl.pallas_call(
+        kernel,
+        out_shape=[shape(*kinds[k]) for k in FORWARD_OUT]
+        + [shape(*fulls[0]), shape(*fulls[1]), shape(vec.shape, f32), shape(vec.shape, f32)],
+        in_specs=[vm] * 4 + [anyspec] * n + [vm],
+        out_specs=[anyspec] * (len(FORWARD_OUT) + 2) + [vm] * 2,
+        scratch_shapes=[pltpu.VMEM(*kinds[k]) for k in names]
+        + [pltpu.VMEM(*f) for f in fulls]
+        + [
+            pltpu.VMEM((6,) + vec.shape, f32),
+            pltpu.VMEM((5,) + vec.shape, f32),
+            dma((n, 4)),
+            dma((n, 16)),
+            dma((n,)),
+            dma((n,)),
+            dma((5,)),
+            dma((5,)),
+            dma((len(FORWARD_OUT) + 2,)),
+        ],
+        compiler_params=pltpu.CompilerParams(collective_id=0, has_side_effects=True, vmem_limit_bytes=60 << 20),
+    )(tokens, segments.reshape(rows, 1), segments.reshape(1, rows), cotangent, *shards, vec)
+    saved = dict(zip(FORWARD_OUT, results))
+    saved["wq"], saved["wo"], saved["vec"], saved["gvec"] = results[len(FORWARD_OUT) :]
+    return saved
+
+
+UNITS = 4
+UNIT = 32
+CHIPS = 16
+
+
+class Reduce:
+    def __init__(self, piece, z_first, mine, b_buf, z_buf, a_buf, send, b_recv, z_recv, a_recv, emit):
+        self.p, self.z_first, self.emit = piece, z_first, emit
+        self.mine, self.b_buf, self.z_buf, self.a_buf = mine, b_buf, z_buf, a_buf
+        self.send, self.b_recv, self.z_recv, self.a_recv = send, b_recv, z_recv, a_recv
+        self.rows = mine.shape[1]
         self.me, self.z, self.core, self.a_step, self.b_step, self.x, self.y = place()
-        self.sib = self.me + 1 - 2 * self.core
-
-    def block(self, dev):
-        return self.grad.at[pl.ds(pl.multiple_of(dev * self.rows, self.rows), self.rows)]
 
     def sides(self, k, fn):
         if k == 0:
@@ -349,40 +742,6 @@
         @pl.when(self.z + k <= LINE - 1)
         def _():
             fn(k)
-
-    def order(self):
-        return [3, 2, 1, 0]
-
-    def exchange(self):
-        def one(dev):
-            chip = dev // 2
-            pltpu.make_async_copy(self.block(dev), self.mine.at[chip], self.load.at[self.p, chip]).start()
-            sdev = dev + 1 - 2 * self.core
-            remote(self.block(sdev), self.sib_buf.at[chip], self.send.at[self.p, 2], self.c_recv.at[self.p, chip], self.sib).start()
-
-        for b in (self.b_step, 0):
-            for k in self.order():
-                for a in (self.a_step, 0):
-                    self.sides(k, lambda s: one(self.me + b + a + PLANE * s))
-
-    def local(self, dev):
-        chip = dev // 2
-        wait_for(self.mine.at[chip], self.load.at[self.p, chip])
-        wait_for(self.sib_buf.at[chip], self.c_recv.at[self.p, chip])
-        return [self.mine.at[chip], self.sib_buf.at[chip]]
-
-    def send_b(self, k):
-        for a in (self.a_step, 0):
-
-            def one(s):
-                dev = self.me + self.b_step + a + PLANE * s
-                chip = dev // 2
-                terms = self.local(dev)
-                add_blocks(self.mine.at[chip], terms, self.rows)
-                slot = self.b_slot(dev)
-                remote(self.mine.at[chip], self.b_buf.at[slot], self.send.at[self.p, 1], self.b_recv.at[self.p, slot], self.me + self.b_step).start()
-
-            self.sides(k, one)
 
     def b_slot(self, dev):
         x = (dev // 2) % 2
@@ -390,24 +749,45 @@
         a_bit = x * (1 - self.core) + y * self.core
         return (dev // PLANE) * 2 + a_bit
 
+    def send_b(self, k):
+        for a in (self.a_step, 0):
+
+            def one(s):
+                dev = self.me + self.b_step + a + PLANE * s
+                slot = self.b_slot(dev)
+                remote(
+                    self.mine.at[dev // 2],
+                    self.b_buf.at[slot],
+                    self.send.at[self.p, 1],
+                    self.b_recv.at[self.p, slot],
+                    self.me + self.b_step,
+                ).start()
+
+            self.sides(k, one)
+
     def after_b(self, dev):
         slot = self.b_slot(dev)
         wait_for(self.b_buf.at[slot], self.b_recv.at[self.p, slot])
-        return self.local(dev) + [self.b_buf.at[slot]]
+        return [self.mine.at[dev // 2], self.b_buf.at[slot]]
 
     def a_slot(self, dev):
         return dev // PLANE if self.z_first else 0
 
-    def send_a(self, dev, terms):
-        chip = dev // 2
-        add_blocks(self.mine.at[chip], terms, self.rows)
+    def to_a(self, dev):
         slot = self.a_slot(dev)
-        remote(self.mine.at[chip], self.a_buf.at[slot], self.send.at[self.p, 0], self.a_recv.at[self.p, slot], self.me + self.a_step).start()
-
-    def send_a_early(self, k):
+        remote(
+            self.mine.at[dev // 2],
+            self.a_buf.at[slot],
+            self.send.at[self.p, 0],
+            self.a_recv.at[self.p, slot],
+            self.me + self.a_step,
+        ).start()
+
+    def send_a(self, k):
         def one(s):
             dev = self.me + self.a_step + PLANE * s
-            self.send_a(dev, self.after_b(dev))
+            add_blocks(self.mine.at[dev // 2], self.after_b(dev), self.rows)
+            self.to_a(dev)
 
         self.sides(k, one)
 
@@ -416,8 +796,8 @@
         wait_for(self.a_buf.at[slot], self.a_recv.at[self.p, slot])
         return [self.a_buf.at[slot]]
 
-    def z_index(self, i, dest):
-        return i * 5 + dest
+    def z_slot(self, i, dest):
+        return i * (LINE + 1) + dest
 
     def along_z(self, k):
         for i, a in [(0, 0)] if self.z_first else [(1, self.a_step), (0, 0)]:
@@ -427,13 +807,11 @@
                 def _():
                     dev = self.me + a + sign * PLANE * k
                     chip = dev // 2
-                    dest = self.z + sign * k
                     terms = self.after_b(dev)
                     if self.z_first:
                         terms = terms + self.after_a(dev)
-                    slot = self.z_index(i, dest)
-                    last = k == 1
-                    there = self.z_index(i, LINE) if (last and sign > 0) else slot
+                    slot = self.z_slot(i, self.z + sign * k)
+                    there = self.z_slot(i, LINE) if (k == 1 and sign > 0) else slot
                     more = (self.z < LINE - 1) if sign < 0 else (self.z > 0)
 
                     @pl.when(more)
@@ -445,24 +823,20 @@
                     def _():
                         add_blocks(self.mine.at[chip], terms, self.rows)
 
-                    remote(self.mine.at[chip], self.z_buf.at[there], self.send.at[self.p, 3], self.z_recv.at[self.p, there], self.me + sign * PLANE).start()
-
-    def at_home(self, i, a):
-        dev = self.me + a
-        chip = dev // 2
+                    remote(
+                        self.mine.at[chip],
+                        self.z_buf.at[there],
+                        self.send.at[self.p, 3],
+                        self.z_recv.at[self.p, there],
+                        self.me + sign * PLANE,
+                    ).start()
+
+    def home_terms(self, i, dev, fn):
         terms = self.after_b(dev)
         if self.z_first:
             terms = terms + self.after_a(dev)
-        above = self.z_index(i, self.z)
-        below = self.z_index(i, LINE)
-        def finish(terms):
-            if i == 1:
-                add_blocks(self.mine.at[chip], terms, self.rows)
-            else:
-                if not self.z_first:
-                    terms = terms + self.after_a(dev)
-                add_blocks(self.out, terms, self.rows)
-
+        above = self.z_slot(i, self.z)
+        below = self.z_slot(i, LINE)
         for has_above, has_below, cond in (
             (True, False, self.z == 0),
             (True, True, (self.z > 0) & (self.z < LINE - 1)),
@@ -472,181 +846,343 @@
             @pl.when(cond)
             def _():
                 more = list(terms)
-                if has_above:
-                    wait_for(self.z_buf.at[above], self.z_recv.at[self.p, above])
-                    more.append(self.z_buf.at[above])
-                if has_below:
-                    wait_for(self.z_buf.at[below], self.z_recv.at[self.p, below])
-                    more.append(self.z_buf.at[below])
-                finish(more)
-
-        if i == 1:
-            remote(self.mine.at[chip], self.a_buf.at[0], self.send.at[self.p, 0], self.a_recv.at[self.p, 0], self.me + self.a_step).start()
+                for slot, has in ((above, has_above), (below, has_below)):
+                    if has:
+                        wait_for(self.z_buf.at[slot], self.z_recv.at[self.p, slot])
+                        more.append(self.z_buf.at[slot])
+                fn(more)
+
+    def home_a(self):
+        dev = self.me + self.a_step
+        self.home_terms(1, dev, lambda terms: add_blocks(self.mine.at[dev // 2], terms, self.rows))
+        self.to_a(dev)
+
+    def home(self):
+        def finish(terms):
+            if not self.z_first:
+                terms = terms + self.after_a(self.me)
+            for chunk in range(self.rows // 16):
+                r = slice(16 * chunk, 16 * chunk + 16)
+                total = terms[0][r, :].astype(jnp.float32)
+                for term in terms[1:]:
+                    total = total + term[r, :].astype(jnp.float32)
+                self.emit(chunk, total)
+
+        self.home_terms(0, self.me, finish)
 
     def stages(self):
-        first = [functools.partial(self.send_b, k) for k in self.order()]
-        second = []
         if self.z_first:
-            second += [functools.partial(self.send_a_early, k) for k in self.order()]
-            second += [functools.partial(self.along_z, k) for k in (3, 2, 1)]
-            third = [functools.partial(self.at_home, 0, 0)]
-        else:
-            second += [functools.partial(self.along_z, k) for k in (3, 2, 1)]
-            second += [functools.partial(self.at_home, 1, self.a_step)]
-            third = [functools.partial(self.at_home, 0, 0)]
-        return first, second, third
+            later = [functools.partial(self.send_a, k) for k in (3, 2, 1, 0)]
+            later += [functools.partial(self.along_z, k) for k in (3, 2, 1)]
+            return later + [self.home]
+        return [functools.partial(self.along_z, k) for k in (3, 2, 1)] + [self.home_a, self.home]
+
+    def send_all_b(self):
+        for k in (3, 2, 1, 0):
+            self.send_b(k)
 
     def drain(self):
-        wait_for(self.mine, self.send.at[self.p, 2])
         wait_for(self.mine.at[pl.ds(0, 8)], self.send.at[self.p, 1])
         wait_for(self.mine.at[pl.ds(0, 4 if self.z_first else 1)], self.send.at[self.p, 0])
         wait_for(self.mine.at[pl.ds(0, 3 if self.z_first else 6)], self.send.at[self.p, 3])
 
 
-def peers():
-    me, z, core, a_step, b_step, x, y = place()
-    near = [me + 1 - 2 * core, me + a_step, me + b_step]
-    return z, near, me + PLANE, me - PLANE, me + 16 - 32 * (z // 2)
-
-
-Z_FIRST = (False, False, True, False)
-
-
-def gather_kernel(shards, vec, fulls, vec_out, held, got, send, recv, core_recv, own, vsend, vrecv):
-    z, near, up, down, far = peers()
-    entry_barrier(z, near, up, down, far)
-    held[0] = vec[...]
-    v = Vec(held, got, vsend, vrecv)
-    v.start(0)
-    q, o, u, d = [Gather(p, shards[p], fulls[p], Z_FIRST[p], send, recv, core_recv, own) for p in range(4)]
-    q.own(); o.own()
-    v.step(0)
-    q.from_a(); o.from_a()
-    v.step(1)
-    u.own()
-    q.from_z(1); o.from_z(1)
-    v.step(2)
-    u.from_z(1)
-    q.from_z(2); o.from_z(2)
-    v.step(3)
-    u.from_z(2)
-    d.own()
-    q.from_z(3); o.from_z(3)
-    v.step(4)
-    u.from_z(3)
-    d.from_a()
-    for k in range(4):
-        q.from_b(k); o.from_b(k)
-    u.from_a(0)
-    d.from_z(1)
-    u.from_a(1)
-    d.from_z(2)
-    u.from_a(2)
-    d.from_z(3)
-    u.from_a(3)
-    for k in range(4):
-        u.from_b(k); d.from_b(k)
-    vec_out[...] = held[5]
-    for g in (q, o, u, d):
-        g.ready()
-    for g in (q, o, u, d):
-        g.drain()
-
-
-def gather_all(shards, vec):
-    count = len(shards)
-    n = 32
-
-    def kernel(*refs):
-        sh, v = refs[:count], refs[count]
-        fulls, vo = refs[count + 1 : 2 * count + 1], refs[2 * count + 1]
-        gather_kernel(sh, v, fulls, vo, *refs[2 * count + 2 :])
+def attend_back_pair(i, width, qkv, d_attended, bias, d_proj, gvec):
+    rows = d_attended.shape[0]
+    q = qkv[:, columns(i * PAIR, PAIR)]
+    k = qkv[:, columns(width + i * PAIR, PAIR)]
+    v = qkv[:, columns(2 * width + i * PAIR, PAIR)]
+    g = d_attended[:, columns(i * PAIR, PAIR)]
+    d_query, d_key, d_value = [], 0.0, 0.0
+    for head in (0, 1):
+        qh, gh = own_half(q, head), own_half(g, head)
+        p = probabilities(qh, k, bias[...])
+        d_p = dot_nt(gh, v)
+        inner = jnp.sum(p * d_p, -1, keepdims=True)
+        d_s = (p * (d_p - inner)).astype(jnp.bfloat16)
+        d_query.append(dot(d_s, k))
+        d_key = d_key + dot_tn(d_s, qh)
+        d_value = d_value + dot_tn(p.astype(jnp.bfloat16), gh)
+    d_q = halves(*d_query).astype(jnp.bfloat16).astype(jnp.float32) * HEAD_DIM ** (-0.5)
+    d_v = d_value.astype(jnp.bfloat16)
+    top = pl.ds(0, rows)
+    d_proj[top, columns(i * PAIR, PAIR)] = d_q.astype(jnp.bfloat16)
+    d_proj[top, columns(width + i * PAIR, PAIR)] = d_key.astype(jnp.bfloat16)
+    d_proj[top, columns(2 * width + i * PAIR, PAIR)] = d_v
+    gvec[QUERY_BIAS : QUERY_BIAS + 1, columns(i * PAIR, PAIR)] = jnp.sum(d_q, 0, keepdims=True)
+    gvec[VALUE_BIAS : VALUE_BIAS + 1, columns(i * PAIR, PAIR)] = jnp.sum(
+        d_v.astype(jnp.float32), 0, keepdims=True
+    )
+
+
+def transpose_blocks(stack, turned):
+    def body(i):
+        part = stack[:, columns(i * 128, 128)].astype(jnp.float32).T.astype(jnp.bfloat16)
+        turned[pl.ds(2 * i, 2)] = part.reshape(2, 2, UNIT, stack.shape[0])
+
+    loop(stack.shape[1] // 128, body)
+
+
+def turned_product(turned, core, right, mine, unit, right_column):
+    width = mine.shape[2]
+    tokens = turned.shape[3]
+
+    def body(j):
+        left = turned[:, pl.ds(core, 1)].reshape(CHIPS * UNIT, tokens)
+        out = dot(left, right[:, columns(right_column + j * TILE, TILE)]).astype(jnp.bfloat16)
+        mine[:, UNIT * unit : UNIT * unit + UNIT, columns(j * TILE, TILE)] = out.reshape(CHIPS, UNIT, TILE)
+
+    loop(width // TILE, body)
+
+
+SAVED_IN = ("d_resid", "first", "qkv", "attended", "second", "active", "d_inner", "d_mlp", "d_branch", "wq", "wo")
+
+
+def backward_all(count, tokens, segments, saved):
+    rows, width = tokens.shape
+    hidden = saved["d_inner"].shape[1]
+    f32, b16 = jnp.float32, jnp.bfloat16
+    both = 2 * rows
+    half = hidden // 2
+    block = (hidden // count, width)
+    z_first = (False, True, False)
+    kinds = {
+        "x_active": ((both, half), b16),
+        "y_mlp": ((both, width), b16),
+        "y_inner": ((both, hidden), b16),
+        "x_second": ((both, width), b16),
+        "x_attended": ((both, width), b16),
+        "y_branch": ((both, width), b16),
+        "x_first": ((both, width), b16),
+        "y_proj": ((both, 3 * width), b16),
+        "turned": ((CHIPS, 2, UNIT, both), b16),
+        "qkv": ((rows, 3 * width), b16),
+        "wo": (saved["wo"].shape, b16),
+        "wq": ((2, TILE // 2, 3 * width), b16),
+        "d_attended": ((rows, width), b16),
+        "d_norm": ((rows, width), f32),
+        "d_resid": ((rows, width), f32),
+        "bias": ((rows, rows), f32),
+        "sums": ((16, width), f32),
+        "gvec": (saved["gvec"].shape, f32),
+    }
+    names = list(kinds)
+    sent = ("active", "d_mlp", "second", "d_inner", "attended", "d_branch", "first")
+    stacks = ("x_active", "y_mlp", "x_second", "y_inner", "x_attended", "y_branch", "x_first")
+
+    def kernel(tok, sc, sr, vec, gvec_in, *refs):
+        src = dict(zip(SAVED_IN, refs[: len(SAVED_IN)]))
+        refs = refs[len(SAVED_IN) :]
+        grad_out, q_out, o_out, u_out, d_out, gvec_out = refs[:6]
+        refs = refs[6:]
+        s = dict(zip(names, refs[: len(names)]))
+        refs = refs[len(names) :]
+        bufs, refs = refs[:12], refs[12:]
+        held, got, send, b_recv, z_recv, a_recv, vsend, vrecv, x_send, x_recv, load, misc = refs
+        me, z, core, _, _, _, _ = place()
+        sib = me + 1 - 2 * core
+        _, near, up, down, far = peers()
+        entry_barrier(z, near, up, down, far)
+
+        def source(name, which):
+            return src[name].at[which] if name == "active" else src[name]
+
+        top, low = pl.ds(0, rows), pl.ds(rows, rows)
+
+        def load_copy(i):
+            return pltpu.make_async_copy(source(sent[i], core), s[stacks[i]].at[top], load.at[i])
+
+        def cross_copy(i):
+            return remote(source(sent[i], 1 - core), s[stacks[i]].at[low], x_send.at[i], x_recv.at[i], sib)
+
+        for i in range(len(sent)):
+            load_copy(i).start()
+            cross_copy(i).start()
+        early = [pltpu.make_async_copy(src[n], s[n], misc.at[i]) for i, n in enumerate(("qkv", "wo", "d_resid"))]
+        for copy in early:
+            copy.start()
+
+        def ready(*which):
+            for i in which:
+                load_copy(i).wait()
+                cross_copy(i).wait()
+
+        def emit_down(chunk, total):
+            d_out[16 * chunk : 16 * chunk + 16, :] = total
+
+        def emit_up(chunk, total):
+            unit, r = chunk // 2, 16 * (chunk % 2)
+            u_out[r : r + 16, width * unit : width * unit + width] = total
+
+        def emit_attn(chunk, total):
+            unit, r = chunk // 2, 16 * (chunk % 2)
+            if unit == 3:
+                o_out[r : r + 16, :] = total
+            else:
+                q_out[r : r + 16, width * unit : width * unit + width] = total
+
+        down_r, up_r, attn_r = [
+            Reduce(p, z_first[p], *bufs[4 * p : 4 * p + 4], send, b_recv, z_recv, a_recv, emit)
+            for p, emit in enumerate((emit_down, emit_up, emit_attn))
+        ]
+        gvec = s["gvec"]
+        gvec[...] = gvec_in[...]
+        mask_bias(s["bias"], sc, sr)
+        ready(0, 1)
+
+        def down_grad(i):
+            left = s["x_active"][:, columns(i * TILE, TILE)]
+            out = dot_tn(left, s["y_mlp"][...]).astype(b16)
+            down_r.mine[pl.ds(4 * i, 4)] = out.reshape(4, block[0], width)
+
+        loop(half // TILE, down_grad)
+        down_r.send_all_b()
+        ready(2, 3)
+        transpose_blocks(s["x_second"], s["turned"])
+        for unit in range(UNITS):
+            turned_product(s["turned"], core, s["y_inner"], up_r.mine, unit, unit * width)
+        up_r.send_all_b()
+        for copy in early:
+            copy.wait()
+        ready(4, 5, 6)
+
+        def d_attended_tile(j):
+            size = TILE // 2
+            wrows = pl.ds(pl.multiple_of(j * size, size), size)
+            c = columns(j * size, size)
+            s["d_attended"][:, c] = dot_nt(s["y_branch"][top, :], s["wo"][wrows, :]).astype(b16)
+            gvec[OUT_BIAS : OUT_BIAS + 1, c] = jnp.sum(s["y_branch"][top, c].astype(f32), 0, keepdims=True)
+
+        loop(width // (TILE // 2), d_attended_tile)
+
+        def attend_back(begin, n):
+            loop(
+                n,
+                lambda i: attend_back_pair(
+                    begin + i, width, s["qkv"], s["d_attended"], s["bias"], s["y_proj"], gvec
+                ),
+            )
+
+        dn, upn, att = down_r.stages(), up_r.stages(), attn_r.stages()
+        attend_back(0, 2)
+        dn[0]()
+        attend_back(2, 2)
+        dn[1]()
+        upn[0]()
+        attend_back(4, 2)
+        dn[2]()
+        upn[1]()
+        attend_back(6, 2)
+        proj_cross = remote(s["y_proj"].at[top], s["y_proj"].at[low], misc.at[3], misc.at[4], sib)
+        proj_cross.start()
+        upn[2]()
+        upn[3]()
+        transpose_blocks(s["x_attended"], s["turned"])
+        turned_product(s["turned"], core, s["y_branch"], attn_r.mine, 3, 0)
+        transpose_blocks(s["x_first"], s["turned"])
+        proj_cross.wait()
+        for unit in range(3):
+            turned_product(s["turned"], core, s["y_proj"], attn_r.mine, unit, unit * width)
+        attn_r.send_all_b()
+        dn[3]()
+        upn[4]()
+        size = TILE // 2
+        tiles = width // size
+
+        def wq_copy(j):
+            wrows = pl.ds(pl.multiple_of(j * size, size), size)
+            return pltpu.make_async_copy(src["wq"].at[wrows], s["wq"].at[j % 2], load.at[len(sent) + j % 2])
+
+        wq_copy(0).start()
+
+        def d_first_tile(j):
+            @pl.when(j + 1 < tiles)
+            def _():
+                wq_copy(j + 1).start()
+
+            wq_copy(j).wait()
+            s["d_norm"][:, columns(j * size, size)] = dot_nt(s["y_proj"][top, :], s["wq"][j % 2])
+
+        for j in range(tiles):
+            d_first_tile(j)
+        upn[5]()
+
+        def emit(r, back):
+            s["d_resid"][r, :] += back
+
+        norm_back(s["d_norm"], tok, vec, GAIN_ONE, s["sums"], emit)
+        gvec[GAIN_ONE : GAIN_ONE + 1, :] = jnp.sum(s["sums"][0:8, :], 0, keepdims=True)
+        gvec[BIAS_ONE : BIAS_ONE + 1, :] = jnp.sum(s["sums"][8:16, :], 0, keepdims=True)
+        leave = pltpu.make_async_copy(s["d_resid"], grad_out, misc.at[5])
+        leave.start()
+        held[0] = gvec[...]
+        v = Vec(held, got, vsend, vrecv)
+        v.start(0)
+        upn[6]()
+        v.step(0)
+        att[0]()
+        dn[4]()
+        v.step(1)
+        att[1]()
+        v.step(2)
+        upn[7]()
+        att[2]()
+        v.step(3)
+        att[3]()
+        v.step(4)
+        gvec_out[...] = held[5]
+        att[4]()
+        for r in (down_r, up_r, attn_r):
+            r.drain()
+        leave.wait()
 
     anyspec = pl.BlockSpec(memory_space=pl.ANY)
     vm = pl.BlockSpec(memory_space=pltpu.VMEM)
     dma = pltpu.SemaphoreType.DMA
+    shape = jax.ShapeDtypeStruct
+    vec_shape = saved["vec"].shape
+    bufs = []
+    for zf in z_first:
+        bufs += [pltpu.VMEM((n,) + block, b16) for n in (CHIPS, 8, 5 if zf else 10, 4 if zf else 1)]
+    outs = [
+        ((rows, width), f32),
+        ((width // count, 3 * width), f32),
+        ((width // count, width), f32),
+        ((width // count, hidden), f32),
+        (block, f32),
+        (vec_shape, f32),
+    ]
     return pl.pallas_call(
         kernel,
-        out_shape=[jax.ShapeDtypeStruct((n * s.shape[0], s.shape[1]), s.dtype) for s in shards] + [jax.ShapeDtypeStruct(vec.shape, vec.dtype)],
-        in_specs=[anyspec] * count + [vm],
-        out_specs=[anyspec] * count + [vm],
-        scratch_shapes=[
-            pltpu.VMEM((6,) + vec.shape, jnp.float32),
-            pltpu.VMEM((5,) + vec.shape, jnp.float32),
-            dma((count, 4)), dma((count, 16)), dma((count,)), dma((count,)), dma((5,)), dma((5,)),
+        out_shape=[shape(*o) for o in outs],
+        in_specs=[vm] * 5 + [anyspec] * len(SAVED_IN),
+        out_specs=[anyspec] + [vm] * 5,
+        scratch_shapes=[pltpu.VMEM(*kinds[k]) for k in names]
+        + bufs
+        + [
+            pltpu.VMEM((6,) + vec_shape, f32),
+            pltpu.VMEM((5,) + vec_shape, f32),
+            dma((3, 4)),
+            dma((3, 8)),
+            dma((3, 10)),
+            dma((3, 4)),
+            dma((5,)),
+            dma((5,)),
+            dma((len(sent),)),
+            dma((len(sent),)),
+            dma((len(sent) + 2,)),
+            dma((6,)),
         ],
-        compiler_params=pltpu.CompilerParams(collective_id=0, has_side_effects=True),
-    )(*shards, vec)
-
-
-def scatter_kernel(grads, vec, outs, vec_out, bufs, held, got, send, load, c_recv, b_recv, z_recv, a_recv, vsend, vrecv, order):
-    z, near, up, down, far = peers()
-    entry_barrier(z, near, up, down, far)
-    pieces = {}
-    for p in order:
-        pieces[p] = Scatter(p, grads[p], outs[p], Z_FIRST[p], *bufs[5 * p : 5 * p + 5], send, load, c_recv, b_recv, z_recv, a_recv)
-        pieces[p].exchange()
-    held[0] = vec[...]
-    v = Vec(held, got, vsend, vrecv)
-    v.start(0)
-    st = [pieces[p].stages() for p in order]
-    seq = []
-    n = len(order)
-    for i in range(n + 2):
-        groups = []
-        if i < n:
-            groups.append(st[i][0])
-        if 0 <= i - 1 < n:
-            groups.append(st[i - 1][1])
-        if 0 <= i - 2 < n:
-            groups.append(st[i - 2][2])
-        longest = max(len(g) for g in groups)
-        for j in range(longest):
-            for g in groups:
-                if j < len(g):
-                    seq.append(g[j])
-    step = 0
-    for i, fn in enumerate(seq):
-        fn()
-        if i % 4 == 3 and step < 5:
-            v.step(step)
-            step += 1
-    vec_out[...] = held[5]
-    for p in order:
-        pieces[p].drain()
-
-
-def scatter_all(grads, vec):
-    count = len(grads)
-    n = 32
-
-    def kernel(*refs):
-        gr, v = refs[:count], refs[count]
-        outs, vo = refs[count + 1 : 2 * count + 1], refs[2 * count + 1]
-        rest = refs[2 * count + 2 :]
-        scatter_kernel(gr, v, outs, vo, rest[: 5 * count], *rest[5 * count :], order=(3, 2, 1, 0))
-
-    anyspec = pl.BlockSpec(memory_space=pl.ANY)
-    vm = pl.BlockSpec(memory_space=pltpu.VMEM)
-    dma = pltpu.SemaphoreType.DMA
-    bufs = []
-    for p, g in enumerate(grads):
-        blk = (g.shape[0] // n, g.shape[1])
-        zf = Z_FIRST[p]
-        bufs += [pltpu.VMEM((c,) + blk, jnp.bfloat16) for c in (16, 16, 8, 5 if zf else 10, 4 if zf else 1)]
-    return pl.pallas_call(
-        kernel,
-        out_shape=[jax.ShapeDtypeStruct((g.shape[0] // n, g.shape[1]), jnp.float32) for g in grads] + [jax.ShapeDtypeStruct(vec.shape, vec.dtype)],
-        in_specs=[anyspec] * count + [vm],
-        out_specs=[vm] * (count + 1),
-        scratch_shapes=bufs
-        + [
-            pltpu.VMEM((6,) + vec.shape, jnp.float32),
-            pltpu.VMEM((5,) + vec.shape, jnp.float32),
-            dma((count, 4)), dma((count, 16)), dma((count, 16)), dma((count, 8)), dma((count, 10)), dma((count, 4)), dma((5,)), dma((5,)),
-        ],
-        compiler_params=pltpu.CompilerParams(collective_id=1, has_side_effects=True, vmem_limit_bytes=56 << 20),
-    )(*grads, vec)
+        compiler_params=pltpu.CompilerParams(collective_id=1, has_side_effects=True, vmem_limit_bytes=63 << 20),
+    )(
+        tokens,
+        segments.reshape(rows, 1),
+        segments.reshape(1, rows),
+        saved["vec"],
+        saved["gvec"],
+        *[saved[k] for k in SAVED_IN],
+    )
+
 
 VECTOR_ROWS = 16
 
@@ -656,7 +1192,7 @@
     for part in parts:
         size = part.shape[0]
         whole = jnp.where(
-            (jnp.arange(count) == position)[:, None], halved(part).astype(jnp.float32)[None], 0.0
+            (jnp.arange(count) == position)[:, None], lax.reduce_precision(part, 8, 7)[None], 0.0
         )
         rows.append(whole.reshape(size * count))
     return jnp.concatenate(rows)
@@ -784,24 +1320,27 @@
         return jnp.pad(rows, ((0, VECTOR_ROWS - rows.shape[0]), (0, 0)))
 
     if kernels:
-        *weights, vector_rows = gather_all(
-            weight_shards, packed(spread_vectors(vector_shards, position, count))
+        saved = forward_all(
+            count,
+            tokens,
+            segments,
+            cotangent,
+            weight_shards,
+            packed(spread_vectors(vector_shards, position, count)),
         )
-        flat = vector_rows.reshape(-1)
-        vectors = [flat[starts[i] : starts[i + 1]] for i in range(len(sizes))]
+        activations = saved["activations"]
+        saved["active"] = saved["split"]
+        input_grad, *weight_owned, vector_rows = backward_all(count, tokens, segments, saved)
     else:
         weights = [lax.all_gather(w, "dev", axis=0, tiled=True) for w in weight_shards]
         vectors = [
             lax.all_gather(halved(v), "dev", axis=0, tiled=True).astype(jnp.float32)
             for v in vector_shards
         ]
-    activations, input_grad, weight_grads, vector_grads = local_math(
-        tokens, segments, cotangent, vectors, weights
-    )
+        activations, input_grad, weight_grads, vector_grads = local_math(
+            tokens, segments, cotangent, vectors, weights
+        )
     if kernels:
-        *weight_owned, vector_rows = scatter_all(
-            [halved(g) for g in weight_grads], packed(jnp.concatenate(vector_grads))
-        )
         flat = vector_rows.reshape(-1)
         vector_owned = [
             lax.dynamic_slice(flat, (starts[i] + position * (sizes[i] // count),), (sizes[i] // count,))

time: 420 us -> 281 us (0.67); the launches traced: 414 us -> 280 us
  matrix products: 97.6 us -> 0 us
  local copies, waits for them, and re-layouts: 65.8 us -> 13.5 us
  Pallas kernels: 225 us -> 261 us
  other arithmetic: 23.2 us -> 4.97 us
    dot_general x68 -> x0, matrix products: 97.6 us -> none  [the longest x4 30 us: contract_cols(): lax.dot_general(left, right, (((1,), (1,)), ((), ())), preferred_element_...]
    pallas_call x2, Pallas kernels: 225 us -> 261 us  [the longest x1 134 us: forward_all(): pl.pallas_call(kernel, out_shape=[shape(*kinds[k]) for k in FORWARD_OUT]...]
    dynamic_slice x48 -> x0, local copies, waits for them, and re-layouts: 29.8 us -> none  [local_math(): lax.map(lambda pieces: pair_forward(pieces, allowed), (head_pairs(queries...]
    dynamic_update_slice x24 -> x0, local copies, waits for them, and re-layouts: 16.2 us -> none  [the longest x16 10.9 us: local_math(): lax.map(lambda pieces: pair_backward(pieces, allowed), (head_pairs(querie...]
    reduce_sum x17 -> x0, other arithmetic: 6.3 us -> none  [the longest x3 2.44 us: layer_norm(): centre = rows_in - jnp.mean(rows_in, -1, keepdims=True)]
    convert_element_type x14 -> x4, other arithmetic: 9.25 us -> 4.71 us  [halved(): return array_in.astype(jnp.bfloat16)]
    unnamed x91 -> x43, local copies, waits for them, and re-layouts: 9.28 us -> 7.76 us
where the time goes in v2:
time: 281 us; the launch traced here: 280 us
  Pallas kernels  261 us (93%)
  local copies, waits for them, and re-layouts  13.5 us (5%)
  other arithmetic  4.97 us (2%)
    pallas_call x1, Pallas kernels, forward_all(): pl.pallas_call(kernel, out_shape=[shape(*kinds[k]) for k in FORWARD_OUT]...  134 us
    pallas_call x1, Pallas kernels, backward_all(): pl.pallas_call(kernel, out_shape=[shape(*o) for o in outs], in_specs=[vm]...  127 us
    unnamed x43, local copies, waits for them, and re-layouts  7.76 us

profile of v2, /device:TPU:0, one launch (start us, length us, event | category | flops | bytes accessed | tf_op | source)
XLA Modules:
  0.0 280.4 jit_solution(6732616514647774507)
XLA Ops:
  0.6 0.0 copy-start.1
  0.7 0.0 copy-start.2
  0.7 0.0 copy-start.7
  0.7 0.0 copy-start.8
  0.7 0.0 copy-start.9
  0.7 0.0 copy-start.10
  0.7 0.0 copy-start.11
  0.7 0.0 copy-start.12
  0.7 1.5 reshape.98.sc
  2.3 1.2 reshape.95.sr
  3.5 1.7 convert_element_type.14.q_sh
  5.2 1.5 convert_element_type.15.o_sh
  6.8 0.0 copy-done.1
  6.8 0.7 convert_element_type.16.u_sh
  7.5 0.0 copy-done.2
  7.5 0.7 convert_element_type.17.d_sh
  8.2 0.0 copy-done.7
  8.2 0.0 copy-done.8
  8.3 0.0 copy-done.9
  8.3 0.0 copy-done.10
  8.3 0.0 copy-done.11
  8.3 0.0 copy-done.12
  8.3 0.1 broadcast_select_fusion
  8.4 0.1 select_n.84
  8.5 0.1 select_n.86
  8.6 0.0 copy-done.13
  8.6 0.1 broadcast_select_fusion.4
  8.7 0.1 select_n.88
  8.7 0.1 select_n.90
  8.8 0.1 select_n.92
  8.9 0.1 select_n.94
  9.0 0.0 copy-done.14
  9.0 0.1 bitcast_dynamic-update-slice_fusion
  9.1 0.1 select_n.98
  9.2 0.6 pad.4.v_in
  9.8 134.4 %shard_map.254 = (f32[320,1024]{1,0:T(8,128)}, f32[320,1024]{1,0:T(8,128)}, bf16[320,1024]{1,0:T(8,128)(2,1)}, bf16[320,3072]{1,0:T(8,128)(2,1)}, bf16[320,1024]...) custom-call(f32[320,1024]{1,0:T(8,128)} %tok.3, ...), custom_call_target="tpu_custom_call" | custom-call | tf_op jit(solution)/shard_map/pallas_call | solution.py:694
  144.2 126.7 %shard_map.255 = (f32[320,1024]{1,0:T(8,128)}, f32[32,3072]{1,0:T(8,128)}, f32[32,1024]{1,0:T(8,128)}, f32[32,4096]{1,0:T(8,128)}, f32[128,1024]{1,0:T(8,128)}, /*index=5*/f32[16,1024]{1,0:T(8,128)}) custom-call(f32[320,1024]{1,0:T(8,128)} %tok.3, s32[320,1]{1,0:T(8,128)} %reshape.98.sc, s32[1,320]{1,0:T(1,128)} %reshape.95.sr, ...), custom_call_target="tpu_custom_call" | custom-call | tf_op jit(solution)/shard_map/pallas_call | solution.py:1155
  270.9 0.9 copy.31
  271.8 0.6 fusion
  272.4 0.6 dynamic_slice.26
  273.0 0.6 dynamic_slice.30
  273.6 2.6 copy.45
  276.2 1.1 copy.46
  277.3 0.1 copy-done.5
  277.4 0.7 copy.47
  278.2 0.7 copy.48
  278.8 0.8 copy.49
  279.6 0.8 copy.50
  (28 shorter events, 0.1 us)
Async XLA Ops:
  0.6 6.1 %copy-start.1 = (f32[32,4096]{1,0:T(8,128)S(1)}, f32[32,4096]{1,0:T(8,128)}, u32[]{:S(2)}) copy-start(f32[32,4096]{1,0:T(8,128)} %param.25) | copy-start | bytes 1572868
  0.7 6.8 %copy-start.2 = (f32[128,1024]{1,0:T(8,128)S(1)}, f32[128,1024]{1,0:T(8,128)}, u32[]{:S(2)}) copy-start(f32[128,1024]{1,0:T(8,128)} %param.27) | copy-start | bytes 1572868
  0.7 7.6 %copy-start.7 = (f32[32]{0:T(128)S(1)}, f32[32]{0:T(128)}, u32[]{:S(2)}) copy-start(f32[32]{0:T(128)} %param.28) | copy-start | bytes 388
  0.7 7.6 %copy-start.8 = (f32[32]{0:T(128)S(1)}, f32[32]{0:T(128)}, u32[]{:S(2)}) copy-start(f32[32]{0:T(128)} %param.18) | copy-start | bytes 388
  0.7 7.6 %copy-start.9 = (f32[32]{0:T(128)S(1)}, f32[32]{0:T(128)}, u32[]{:S(2)}) copy-start(f32[32]{0:T(128)} %param.22) | copy-start | bytes 388
  0.7 7.6 %copy-start.10 = (f32[32]{0:T(128)S(1)}, f32[32]{0:T(128)}, u32[]{:S(2)}) copy-start(f32[32]{0:T(128)} %param.23) | copy-start | bytes 388
  0.7 7.6 %copy-start.11 = (f32[32]{0:T(128)S(1)}, f32[32]{0:T(128)}, u32[]{:S(2)}) copy-start(f32[32]{0:T(128)} %param.24) | copy-start | bytes 388
  0.7 7.6 %copy-start.12 = (f32[32]{0:T(128)S(1)}, f32[32]{0:T(128)}, u32[]{:S(2)}) copy-start(f32[32]{0:T(128)} %param.17) | copy-start | bytes 388
  2.3 6.3 %copy-start.13 = (f32[64]{0:T(128)S(1)}, f32[64]{0:T(128)}, u32[]{:S(2)}) copy-start(f32[64]{0:T(128)} %param.20) | copy-start | bytes 772
  3.5 5.5 %copy-start.14 = (f32[128]{0:T(128)S(1)}, f32[128]{0:T(128)}, u32[]{:S(2)}) copy-start(f32[128]{0:T(128)} %param.26) | copy-start | bytes 1540
  273.6 2.6 copy-start
  276.2 1.2 copy-start.5
  276.2 2.0 copy-start.6
  276.2 2.6 copy-start.4
  277.4 2.2 copy-start.3

commit v3 on v1

v3 whole, which is shorter than its diff:
```python
import functools
from functools import partial

import jax
import jax.numpy as jnp
from jax import lax
from jax.experimental import pallas as pl
from jax.experimental.pallas import tpu as pltpu
from jax.sharding import PartitionSpec as P

HEAD_DIM = 64
IMG_DEV = 1
AXIS = "dev"
MESH = pl.DeviceIdType.MESH


def layer_norm(rows_in, gain, bias):
    centre = rows_in - jnp.mean(rows_in, -1, keepdims=True)
    spread = jnp.mean(centre * centre, -1, keepdims=True)
    return centre * lax.rsqrt(spread + 1e-06) * gain + bias


def halved(array_in):
    return array_in.astype(jnp.bfloat16)


def contract_rows(left, right):
    return lax.dot_general(
        left, right, (((0,), (0,)), ((), ())), preferred_element_type=jnp.float32
    )


def contract_cols(left, right):
    return lax.dot_general(
        left, right, (((1,), (1,)), ((), ())), preferred_element_type=jnp.float32
    )


def head_pairs(block):
    return block.reshape(block.shape[0], -1, 2 * HEAD_DIM).transpose(1, 0, 2)


def join_pairs(stack):
    return stack.transpose(1, 0, 2).reshape(stack.shape[1], stack.shape[0] * stack.shape[2])


def masked_scores(query_heads, key_heads, allowed):
    scores = jnp.einsum("qhd,khd->hqk", query_heads, key_heads, preferred_element_type=jnp.float32)
    return jnp.where(allowed[None], scores, -1e30)


def pair_forward(pieces, allowed):
    q_pair, k_pair, v_pair = pieces
    row_count = q_pair.shape[0]
    query_heads = q_pair.reshape(row_count, 2, HEAD_DIM)
    key_heads = k_pair.reshape(row_count, 2, HEAD_DIM)
    value_heads = v_pair.reshape(row_count, 2, HEAD_DIM)
    scores = masked_scores(query_heads, key_heads, allowed)
    row_top = jnp.max(scores, -1, keepdims=True)
    powered = jnp.exp(scores - row_top)
    totals = jnp.sum(powered, -1, keepdims=True)
    probability = halved(powered / totals)
    attended = jnp.einsum(
        "hqk,khd->qhd", probability, value_heads, preferred_element_type=jnp.float32
    )
    return (attended.reshape(row_count, 2 * HEAD_DIM), row_top + jnp.log(totals))


def pair_backward(pieces, allowed):
    q_pair, k_pair, v_pair, g_pair, lse_pair = pieces
    row_count = q_pair.shape[0]
    query_heads = q_pair.reshape(row_count, 2, HEAD_DIM)
    key_heads = k_pair.reshape(row_count, 2, HEAD_DIM)
    value_heads = v_pair.reshape(row_count, 2, HEAD_DIM)
    grad_heads = g_pair.reshape(row_count, 2, HEAD_DIM)
    probability = jnp.exp(masked_scores(query_heads, key_heads, allowed) - lse_pair)
    d_prob = jnp.einsum("qhd,khd->hqk", grad_heads, value_heads, preferred_element_type=jnp.float32)
    row_inner = jnp.sum(probability * d_prob, -1, keepdims=True)
    d_scores = halved(probability * (d_prob - row_inner))
    d_query = halved(
        jnp.einsum("hqk,khd->qhd", d_scores, key_heads, preferred_element_type=jnp.float32)
    )
    d_query = d_query * jnp.bfloat16(HEAD_DIM ** (-0.5))
    d_key = halved(
        jnp.einsum("hqk,qhd->khd", d_scores, query_heads, preferred_element_type=jnp.float32)
    )
    d_value = halved(
        jnp.einsum(
            "hqk,qhd->khd", halved(probability), grad_heads, preferred_element_type=jnp.float32
        )
    )
    width_pair = 2 * HEAD_DIM
    return (
        d_query.reshape(row_count, width_pair),
        d_key.reshape(row_count, width_pair),
        d_value.reshape(row_count, width_pair),
    )


LINE, PLANE = 4, 8

def place():
    me = lax.axis_index(AXIS)
    core = me % 2
    x = (me // 2) % 2
    y = (me // 4) % 2
    z = me // PLANE
    a_bit = x * (1 - core) + y * core
    b_bit = y * (1 - core) + x * core
    a_step = (2 + 2 * core) * (1 - 2 * a_bit)
    b_step = (4 - 2 * core) * (1 - 2 * b_bit)
    return me, z, core, a_step, b_step, x, y


def remote(src, dst, send_sem, recv_sem, device):
    return pltpu.make_async_remote_copy(
        src_ref=src, dst_ref=dst, send_sem=send_sem, recv_sem=recv_sem, device_id=(device,), device_id_type=MESH
    )


def wait_for(ref, sem):
    pltpu.make_async_copy(ref, ref, sem).wait()


def entry_barrier(z, devices, up, down, far):
    bar = pltpu.get_barrier_semaphore()
    for dev in devices:
        pl.semaphore_signal(bar, inc=1, device_id=(dev,), device_id_type=MESH)

    @pl.when(z < LINE - 1)
    def _():
        pl.semaphore_signal(bar, inc=1, device_id=(up,), device_id_type=MESH)

    @pl.when(z > 0)
    def _():
        pl.semaphore_signal(bar, inc=1, device_id=(down,), device_id_type=MESH)

    pl.semaphore_signal(bar, inc=1, device_id=(far,), device_id_type=MESH)
    count = len(devices) + 1
    inner = (z > 0) & (z < LINE - 1)

    @pl.when(inner)
    def _():
        pl.semaphore_wait(bar, count + 2)

    @pl.when(jnp.logical_not(inner))
    def _():
        pl.semaphore_wait(bar, count + 1)


class Vec:
    def __init__(self, held, got, send, recv):
        me, z, core, _, _, x, y = place()
        self.to = [
            me + 1 - 2 * core,
            me + 2 - 4 * x,
            me + 4 - 8 * y,
            me + 8 - 16 * (z % 2),
            me + 16 - 32 * (z // 2),
        ]
        self.held, self.got, self.send, self.recv = held, got, send, recv

    def copy(self, i):
        return remote(self.held, self.got.at[i], self.send.at[i], self.recv.at[i], self.to[i])

    def start(self, i):
        self.copy(i).start()

    def step(self, i):
        self.copy(i).wait()
        self.held[...] += self.got[i]
        if i < 4:
            self.start(i + 1)


class Gather:
    def __init__(self, part, shard, full, z_first, start, size, send, recv, core_recv, own):
        self.p, self.z_first = part, z_first
        cols = pl.ds(start, size)
        self.shard, self.full, self.cols = shard.at[:, cols], full, cols
        self.send, self.recv, self.core_recv, self.own_sem = send, recv, core_recv, own
        self.rows = shard.shape[0]
        self.me, self.z, self.core, self.a_step, self.b_step, _, _ = place()
        self.sib = self.me + 1 - 2 * self.core

    def block(self, dev):
        return self.full.at[pl.ds(pl.multiple_of(dev * self.rows, self.rows), self.rows), self.cols]

    def ici(self, src, dev, way, to):
        remote(src, self.block(dev), self.send.at[self.p, way], self.recv.at[self.p, dev // 2], to).start()

    def to_a(self, src, dev):
        self.ici(src, dev, 0, self.me + self.a_step)

    def to_b(self, src, dev):
        self.ici(src, dev, 1, self.me + self.b_step)

    def to_core(self, src, dev):
        remote(src, self.block(dev), self.send.at[self.p, 2], self.core_recv.at[self.p], self.sib).start()

    def up(self, src, dev):
        @pl.when(self.z < LINE - 1)
        def _():
            self.ici(src, dev, 3, self.me + PLANE)

    def down(self, src, dev):
        @pl.when(self.z > 0)
        def _():
            self.ici(src, dev, 3, self.me - PLANE)

    def arrive(self, dev):
        wait_for(self.block(dev), self.recv.at[self.p, dev // 2])

    def own(self):
        pltpu.make_async_copy(self.shard, self.block(self.me), self.own_sem.at[self.p]).start()
        src = self.shard
        if self.z_first:
            self.up(src, self.me)
            self.down(src, self.me)
            self.to_a(src, self.me)
        else:
            self.to_a(src, self.me)
            self.up(src, self.me)
            self.down(src, self.me)
        self.to_b(src, self.me)
        self.to_core(src, self.me)

    def from_a(self, k=None):
        if not self.z_first:
            dev = self.me + self.a_step
            self.arrive(dev)
            src = self.block(dev)
            self.up(src, dev)
            self.down(src, dev)
            self.to_b(src, dev)
            self.to_core(src, dev)
            return

        def one(dev):
            self.arrive(dev)
            src = self.block(dev)
            self.to_b(src, dev)
            self.to_core(src, dev)

        self.sides(k, lambda off: one(self.me + self.a_step + off))

    def sides(self, k, fn):
        if k == 0:
            fn(0)
            return

        @pl.when(self.z >= k)
        def _():
            fn(-PLANE * k)

        @pl.when(self.z + k <= LINE - 1)
        def _():
            fn(PLANE * k)

    def from_z(self, k):
        for base in [self.me] if self.z_first else [self.me, self.me + self.a_step]:

            @pl.when(self.z >= k)
            def _():
                dev = base - PLANE * k
                self.arrive(dev)
                src = self.block(dev)
                self.up(src, dev)
                if self.z_first:
                    self.to_a(src, dev)
                self.to_b(src, dev)
                self.to_core(src, dev)

            @pl.when(self.z + k <= LINE - 1)
            def _():
                dev = base + PLANE * k
                self.arrive(dev)
                src = self.block(dev)
                self.down(src, dev)
                if self.z_first:
                    self.to_a(src, dev)
                self.to_b(src, dev)
                self.to_core(src, dev)

    def from_b(self, k):
        for base in [self.me + self.b_step, self.me + self.b_step + self.a_step]:

            def one(off):
                dev = base + off
                self.arrive(dev)
                self.to_core(self.block(dev), dev)

            self.sides(k, one)

    def many(self, count):
        return self.full.at[pl.ds(0, count * self.rows), self.cols]

    def steps(self):
        step = functools.partial
        z_steps = [step(self.from_z, k) for k in (1, 2, 3)]
        a_steps = [step(self.from_a, k) for k in range(LINE)] if self.z_first else [self.from_a]
        b_steps = [step(self.from_b, k) for k in range(LINE)]
        middle = z_steps + a_steps if self.z_first else a_steps + z_steps
        return [self.own] + middle + b_steps

    def ready(self):
        wait_for(self.shard, self.own_sem.at[self.p])
        wait_for(self.many(16), self.core_recv.at[self.p])

    def drain(self):
        a_count = 4 if self.z_first else 1
        z_unit = 1 if self.z_first else 2
        wait_for(self.many(a_count), self.send.at[self.p, 0])
        wait_for(self.many(8), self.send.at[self.p, 1])
        wait_for(self.many(16), self.send.at[self.p, 2])
        inner = (self.z > 0) & (self.z < LINE - 1)

        @pl.when(inner)
        def _():
            wait_for(self.many(5 * z_unit), self.send.at[self.p, 3])

        @pl.when(jnp.logical_not(inner))
        def _():
            wait_for(self.many(z_unit), self.send.at[self.p, 3])


def add_blocks(dst, terms, rows):
    def body(i, carry):
        r = pl.multiple_of(i * 16, 16)
        total = terms[0][pl.ds(r, 16), :].astype(jnp.float32)
        for term in terms[1:]:
            total = total + term[pl.ds(r, 16), :].astype(jnp.float32)
        dst[pl.ds(r, 16), :] = total.astype(dst.dtype)
        return carry

    lax.fori_loop(0, rows // 16, body, 0)


def peers():
    me, z, core, a_step, b_step, x, y = place()
    near = [me + 1 - 2 * core, me + a_step, me + b_step]
    return z, near, me + PLANE, me - PLANE, me + 16 - 32 * (z // 2)


GATHER_PARTS = (
    (0, 0, 0.5, True),
    (0, 0.5, 0.5, False),
    (1, 0, 1, False),
    (2, 0, 0.375, True),
    (2, 0.375, 0.625, False),
    (3, 0, 0.375, True),
    (3, 0.375, 0.625, False),
)
GROUPS = ((0, 1, 2), (3, 4), (5, 6))
LAG = 6
SPLIT_ROWS = 48


EPS = 1e-06
PAIR = 128
TILE = 512
ROWS = 32
GAIN_ONE, BIAS_ONE, QUERY_BIAS, VALUE_BIAS, OUT_BIAS, GAIN_TWO, BIAS_TWO, UP_BIAS, DOWN_BIAS = 0, 1, 2, 3, 4, 5, 6, 7, 11


def dot(left, right):
    return jnp.dot(left, right, preferred_element_type=jnp.float32)


def dot_nt(left, right):
    return lax.dot_general(left, right, (((1,), (1,)), ((), ())), preferred_element_type=jnp.float32)


def dot_tn(left, right):
    return lax.dot_general(left, right, (((0,), (0,)), ((), ())), preferred_element_type=jnp.float32)


def column_sums(block):
    return dot(jnp.ones((16, block.shape[0]), block.dtype), block)[0:1, :]


def columns(start, size):
    return pl.ds(pl.multiple_of(start, 128), size)


def loop(count, body):
    def step(i, carry):
        body(i)
        return carry

    lax.fori_loop(0, count, step, 0)


def centred(rows):
    centre = rows - jnp.mean(rows, -1, keepdims=True)
    spread = jnp.mean(centre * centre, -1, keepdims=True)
    return centre, lax.rsqrt(spread + EPS)


def norm_into(dst, src, vec, gain_row, bias_row):
    gain = vec[gain_row : gain_row + 1, :]
    bias = vec[bias_row : bias_row + 1, :]

    def body(i):
        r = pl.ds(pl.multiple_of(i * ROWS, ROWS), ROWS)
        centre, scale = centred(src[r, :])
        dst[r, :] = (centre * scale * gain + bias).astype(dst.dtype)

    loop(src.shape[0] // ROWS, body)


def norm_back(d_rows, src, vec, gain_row, sums, emit):
    gain = vec[gain_row : gain_row + 1, :]
    sums[...] = jnp.zeros_like(sums)

    def body(i):
        r = pl.ds(pl.multiple_of(i * ROWS, ROWS), ROWS)
        centre, scale = centred(src[r, :])
        n = centre * scale
        d = d_rows[r, :]
        e = d * gain
        dn = d * n
        for part in range(ROWS // 8):
            sums[0:8, :] += dn[8 * part : 8 * part + 8, :]
            sums[8:16, :] += d[8 * part : 8 * part + 8, :]
        back = scale * (e - jnp.mean(e, -1, keepdims=True) - n * jnp.mean(e * n, -1, keepdims=True))
        emit(r, back)

    loop(src.shape[0] // ROWS, body)


def own_half(rows, head):
    lane = lax.broadcasted_iota(jnp.int32, rows.shape, 1)
    inside = (lane < HEAD_DIM) if head == 0 else (lane >= HEAD_DIM)
    return jnp.where(inside, rows, jnp.zeros_like(rows))


def halves(first, second):
    lane = lax.broadcasted_iota(jnp.int32, first.shape, 1)
    return jnp.where(lane < HEAD_DIM, first, second)


def probabilities(query, key, bias):
    scores = dot_nt(query, key) + bias
    powered = jnp.exp(scores - jnp.max(scores, -1, keepdims=True))
    return powered * (1.0 / jnp.sum(powered, -1, keepdims=True))


def attend_pair(i, width, qkv, bias, attended):
    q = qkv[:, columns(i * PAIR, PAIR)]
    k = qkv[:, columns(width + i * PAIR, PAIR)]
    v = qkv[:, columns(2 * width + i * PAIR, PAIR)]
    parts = []
    for head in (0, 1):
        p = probabilities(own_half(q, head), k, bias[...]).astype(jnp.bfloat16)
        parts.append(dot(p, v))
    attended[:, columns(i * PAIR, PAIR)] = halves(*parts).astype(jnp.bfloat16)


UNITS = 4
VECTOR_ROWS = 16
UNIT = 32
CHIPS = 16


class Reduce:
    def __init__(self, part, z_first, first_row, mine, b_buf, z_buf, a_buf, send, b_recv, z_recv, a_recv, emit):
        self.p, self.z_first, self.first_row, self.emit = part, z_first, first_row, emit
        self.whole, self.b_buf, self.z_buf, self.a_buf = mine, b_buf, z_buf, a_buf
        self.send, self.b_recv, self.z_recv, self.a_recv = send, b_recv, z_recv, a_recv
        self.rows = b_buf.shape[1]
        self.me, self.z, self.core, self.a_step, self.b_step, self.x, self.y = place()

    def mine(self, chip):
        return self.whole.at[chip, pl.ds(self.first_row, self.rows)]

    def many(self, count):
        return self.whole.at[pl.ds(0, count), pl.ds(0, self.rows)]

    def sides(self, k, fn):
        if k == 0:
            fn(0)
            return

        @pl.when(self.z >= k)
        def _():
            fn(-k)

        @pl.when(self.z + k <= LINE - 1)
        def _():
            fn(k)

    def b_slot(self, dev):
        x = (dev // 2) % 2
        y = (dev // 4) % 2
        a_bit = x * (1 - self.core) + y * self.core
        return (dev // PLANE) * 2 + a_bit

    def send_plane(self, plane):
        for a in (self.a_step, 0):
            dev = self.me + self.b_step + a + PLANE * (plane - self.z)
            slot = self.b_slot(dev)
            remote(
                self.mine(dev // 2),
                self.b_buf.at[slot],
                self.send.at[self.p, 1],
                self.b_recv.at[self.p, slot],
                self.me + self.b_step,
            ).start()

    def send_b(self, k):
        self.sides(k, lambda sign: self.send_plane(self.z + sign))

    def after_b(self, dev):
        slot = self.b_slot(dev)
        wait_for(self.b_buf.at[slot], self.b_recv.at[self.p, slot])
        return [self.mine(dev // 2), self.b_buf.at[slot]]

    def a_slot(self, dev):
        return dev // PLANE if self.z_first else 0

    def to_a(self, dev):
        slot = self.a_slot(dev)
        remote(
            self.mine(dev // 2),
            self.a_buf.at[slot],
            self.send.at[self.p, 0],
            self.a_recv.at[self.p, slot],
            self.me + self.a_step,
        ).start()

    def send_a(self, k):
        def one(s):
            dev = self.me + self.a_step + PLANE * s
            add_blocks(self.mine(dev // 2), self.after_b(dev), self.rows)
            self.to_a(dev)

        self.sides(k, one)

    def after_a(self, dev):
        slot = self.a_slot(dev)
        wait_for(self.a_buf.at[slot], self.a_recv.at[self.p, slot])
        return [self.a_buf.at[slot]]

    def z_slot(self, i, dest):
        return i * (LINE + 1) + dest

    def along_z(self, k):
        for i, a in [(0, 0)] if self.z_first else [(1, self.a_step), (0, 0)]:
            for sign in (-1, 1):

                @pl.when((self.z >= k) if sign < 0 else (self.z + k <= LINE - 1))
                def _():
                    dev = self.me + a + sign * PLANE * k
                    chip = dev // 2
                    terms = self.after_b(dev)
                    if self.z_first:
                        terms = terms + self.after_a(dev)
                    slot = self.z_slot(i, self.z + sign * k)
                    there = self.z_slot(i, LINE) if (k == 1 and sign > 0) else slot
                    more = (self.z < LINE - 1) if sign < 0 else (self.z > 0)

                    @pl.when(more)
                    def _():
                        wait_for(self.z_buf.at[slot], self.z_recv.at[self.p, slot])
                        add_blocks(self.mine(chip), terms + [self.z_buf.at[slot]], self.rows)

                    @pl.when(jnp.logical_not(more))
                    def _():
                        add_blocks(self.mine(chip), terms, self.rows)

                    remote(
                        self.mine(chip),
                        self.z_buf.at[there],
                        self.send.at[self.p, 3],
                        self.z_recv.at[self.p, there],
                        self.me + sign * PLANE,
                    ).start()

    def home_terms(self, i, dev, fn):
        terms = self.after_b(dev)
        if self.z_first:
            terms = terms + self.after_a(dev)
        above = self.z_slot(i, self.z)
        below = self.z_slot(i, LINE)
        for has_above, has_below, cond in (
            (True, False, self.z == 0),
            (True, True, (self.z > 0) & (self.z < LINE - 1)),
            (False, True, self.z == LINE - 1),
        ):

            @pl.when(cond)
            def _():
                more = list(terms)
                for slot, has in ((above, has_above), (below, has_below)):
                    if has:
                        wait_for(self.z_buf.at[slot], self.z_recv.at[self.p, slot])
                        more.append(self.z_buf.at[slot])
                fn(more)

    def home_a(self):
        dev = self.me + self.a_step
        self.home_terms(1, dev, lambda terms: add_blocks(self.mine(dev // 2), terms, self.rows))
        self.to_a(dev)

    def home(self):
        def finish(terms):
            if not self.z_first:
                terms = terms + self.after_a(self.me)
            for chunk in range(self.rows // 16):
                r = slice(16 * chunk, 16 * chunk + 16)
                total = terms[0][r, :].astype(jnp.float32)
                for term in terms[1:]:
                    total = total + term[r, :].astype(jnp.float32)
                self.emit(self.first_row // 16 + chunk, total)

        self.home_terms(0, self.me, finish)

    def stages(self):
        step = functools.partial
        z_steps = [step(self.along_z, k) for k in (3, 2, 1)]
        if self.z_first:
            return [step(self.send_a, k) for k in (3, 2, 1, 0)] + z_steps + [self.home]
        return z_steps + [None, None, None, self.home_a, self.home]

    def drain(self):
        wait_for(self.many(8), self.send.at[self.p, 1])
        wait_for(self.many(4 if self.z_first else 1), self.send.at[self.p, 0])
        wait_for(self.many(3 if self.z_first else 6), self.send.at[self.p, 3])


def attend_back_pair(i, width, qkv, d_attended, bias, d_proj, gvec):
    rows = d_attended.shape[0]
    q = qkv[:, columns(i * PAIR, PAIR)]
    k = qkv[:, columns(width + i * PAIR, PAIR)]
    v = qkv[:, columns(2 * width + i * PAIR, PAIR)]
    g = d_attended[:, columns(i * PAIR, PAIR)]
    d_query, d_key, d_value = [], 0.0, 0.0
    for head in (0, 1):
        qh, gh = own_half(q, head), own_half(g, head)
        p = probabilities(qh, k, bias[...])
        d_p = dot_nt(gh, v)
        inner = jnp.sum(p * d_p, -1, keepdims=True)
        d_s = (p * (d_p - inner)).astype(jnp.bfloat16)
        d_query.append(dot(d_s, k))
        d_key = d_key + dot_tn(d_s, qh)
        d_value = d_value + dot_tn(p.astype(jnp.bfloat16), gh)
    d_q = (halves(*d_query).astype(jnp.bfloat16).astype(jnp.float32) * HEAD_DIM ** (-0.5)).astype(jnp.bfloat16)
    d_v = d_value.astype(jnp.bfloat16)
    top = pl.ds(0, rows)
    d_proj[top, columns(i * PAIR, PAIR)] = d_q
    d_proj[top, columns(width + i * PAIR, PAIR)] = d_key.astype(jnp.bfloat16)
    d_proj[top, columns(2 * width + i * PAIR, PAIR)] = d_v
    gvec[QUERY_BIAS : QUERY_BIAS + 1, columns(i * PAIR, PAIR)] = column_sums(d_q)
    gvec[VALUE_BIAS : VALUE_BIAS + 1, columns(i * PAIR, PAIR)] = column_sums(d_v)


def transpose_blocks(stack, turned):
    def body(i):
        part = stack[:, columns(i * 128, 128)].astype(jnp.float32).T.astype(jnp.bfloat16)
        turned[pl.ds(2 * i, 2)] = part.reshape(2, 2, UNIT, stack.shape[0])

    loop(stack.shape[1] // 128, body)


def turned_product(turned, core, right, mine, unit, right_column):
    width = mine.shape[2]
    tokens = turned.shape[3]

    def body(j):
        left = turned[:, pl.ds(core, 1)].reshape(CHIPS * UNIT, tokens)
        out = dot(left, right[:, columns(right_column + j * TILE, TILE)]).astype(jnp.bfloat16)
        mine[:, UNIT * unit : UNIT * unit + UNIT, columns(j * TILE, TILE)] = out.reshape(CHIPS, UNIT, TILE)

    loop(width // TILE, body)


class Both:
    def __init__(self, copies):
        self.copies = copies

    def start(self):
        for copy in self.copies:
            copy.start()

    def wait(self):
        for copy in self.copies:
            copy.wait()


def stream(total, begin, count, copy_of, body):
    if begin == 0:
        copy_of(0, 0).start()

    def step(n):
        j = begin + n

        @pl.when(j + 1 < total)
        def _():
            copy_of(j + 1, (j + 1) % 2).start()

        copy_of(j, j % 2).wait()
        body(j, j % 2)

    loop(count, step)


OPERANDS = ("tokens", "cotangent", "qkv", "out", "fc1", "fc2")


def small_rows(segments, parts):
    slots = jnp.pad(segments.astype(jnp.float32), (0, -segments.shape[0] % 128), constant_values=IMG_DEV)
    flat = jnp.concatenate([p for part in parts for p in [part] * (128 // part.shape[0])] + [slots])
    return jnp.pad(flat, (0, 2048 - flat.shape[0])).reshape(16, 128)


def spread(dst, small, sizes, count, width):
    me = lax.axis_index(AXIS)
    dst[...] = jnp.zeros_like(dst)
    at = 0
    for i, size in enumerate(sizes):
        row = small[i : i + 1, :].astype(jnp.bfloat16).astype(jnp.float32)
        lane = lax.broadcasted_iota(jnp.int32, (1, width), 1)
        for r in range(size * count // width):
            wide = jnp.concatenate([row] * (width // 128), 1)
            inside = (lane + r * width) // size == me
            dst[at : at + 1, :] = jnp.where(inside, wide, 0.0)
            at += 1


def settle(arrays):
    n = len(arrays)

    def kernel(*refs):
        sems = refs[3 * n]
        loads = [pltpu.make_async_copy(refs[i], refs[2 * n + i], sems.at[i]) for i in range(n)]
        stores = [pltpu.make_async_copy(refs[2 * n + i], refs[n + i], sems.at[n + i]) for i in range(n)]
        for copy in loads:
            copy.start()
        for load, store in zip(loads, stores):
            load.wait()
            store.start()
        for copy in stores:
            copy.wait()

    anyspec = pl.BlockSpec(memory_space=pl.ANY)
    return pl.pallas_call(
        kernel,
        out_shape=[jax.ShapeDtypeStruct(a.shape, a.dtype) for a in arrays],
        in_specs=[pl.BlockSpec(memory_space=pltpu.HBM)] * n,
        out_specs=[anyspec] * n,
        scratch_shapes=[pltpu.VMEM(a.shape, a.dtype) for a in arrays] + [pltpu.SemaphoreType.DMA((2 * n,))],
        compiler_params=pltpu.CompilerParams(vmem_limit_bytes=63 << 20),
    )(*arrays)


def block_all(count, tokens, segments, cotangent, shards, vectors):
    rows, width = tokens.shape
    hidden = shards[2].shape[1]
    f32, b16 = jnp.float32, jnp.bfloat16
    vec = jax.ShapeDtypeStruct((VECTOR_ROWS, width), f32)
    sizes = [v.shape[0] for v in vectors]
    both, half = 2 * rows, hidden // 2
    block = (hidden // count, width)
    tiles, tiles_in, per = hidden // TILE, width // TILE, width // TILE
    kinds = {
        "slope": ((rows, hidden), f32),
        "sh_q": (shards[0].shape, b16),
        "sh_o": (shards[1].shape, b16),
        "sh_u": (shards[2].shape, b16),
        "sh_d": (shards[3].shape, b16),
        "resid": ((rows, width), f32),
        "d_resid": ((rows, width), f32),
        "acc": ((rows, width), f32),
        "x_active": ((both, half), b16),
        "other": ((rows, half), b16),
        "y_mlp": ((both, width), b16),
        "y_inner": ((both, hidden), b16),
        "x_second": ((both, width), b16),
        "x_attended": ((both, width), b16),
        "y_branch": ((both, width), b16),
        "x_first": ((both, width), b16),
        "turned": ((CHIPS, 2, UNIT, both), b16),
        "qkv": ((rows, 3 * width), b16),
        "wo": ((width, width), b16),
        "cols": ((2, width, TILE), b16),
        "bias": ((rows, rows), f32),
        "gvec": (vec.shape, f32),
        "vecs": (vec.shape, f32),
    }
    names = list(kinds)
    crossing = ("y_mlp", "x_first", "x_second", "x_attended", "y_branch", "y_proj", "a0", "a1", "i0", "i1")

    def kernel(small, *refs):
        src = dict(zip(OPERANDS, refs[:6]))
        act_out, grad_out, wq_h, wu_h, wd_h, q_out, o_out, u_out, d_out, gvec_out = refs[6:16]
        refs = refs[16:]
        s = dict(zip(names, refs[: len(names)]))
        refs = refs[len(names) :]
        bufs, refs = refs[:21], refs[21:]
        (held, got, g_send, g_recv, g_core, g_own, vsend, vrecv) = refs[:8]
        (send, b_recv, z_recv, a_recv, x_send, x_recv, load, tile_sem, leave_sem, free) = refs[8:]
        me, z, core, _, _, _, _ = place()
        sib = me + 1 - 2 * core
        _, near, up, down, far = peers()
        top, low = pl.ds(0, rows), pl.ds(rows, rows)
        resid, d_resid, acc, vecs, gvec = (s[k] for k in ("resid", "d_resid", "acc", "vecs", "gvec"))
        tok = s["slope"].at[:, pl.ds(hidden - width, width)]

        homes = [tok, d_resid]
        at = 0
        for sh in shards:
            homes.append(s["slope"].at[pl.ds(at, sh.shape[0]), pl.ds(0, sh.shape[1])])
            at += sh.shape[0]
        loads = [pltpu.make_async_copy(src[n], h, load.at[i]) for i, (n, h) in enumerate(zip(OPERANDS, homes))]
        for i in (2, 3, 4, 5, 1):
            loads[i].start()
        entry_barrier(z, near, up, down, far)
        spread(held, small, sizes, count, width)
        v = Vec(held, got, vsend, vrecv)
        v.start(0)

        def cast_shard(i):
            loads[2 + i].wait()
            s[("sh_q", "sh_o", "sh_u", "sh_d")[i]][...] = homes[2 + i][...].astype(b16)

        homes_w = (wq_h, s["wo"], wu_h, wd_h)
        parts = []
        for p, (w, begin_at, share, zf) in enumerate(GATHER_PARTS):
            sh = s[("sh_q", "sh_o", "sh_u", "sh_d")[w]]
            wide = sh.shape[1]
            parts.append(
                Gather(p, sh, homes_w[w], zf, int(begin_at * wide), int(share * wide), g_send, g_recv, g_core, g_own)
            )
        timed = []
        for gi, group in enumerate(GROUPS):
            for p in group:
                timed += [(LAG * gi + j, gi, step) for j, step in enumerate(parts[p].steps())]

        def gather_at(t):
            for gi in range(len(GROUPS)):
                for tt, g, step in timed:
                    if (tt, g) == (t, gi):
                        step()

        def gathered(*which):
            for p in which:
                parts[p].ready()

        def cross_copy(name):
            i = crossing.index(name)
            if name == "y_proj":
                c = pl.ds(0, 3 * width)
                own, to = s["y_inner"].at[top, c], s["y_inner"].at[low, c]
            elif name in ("a0", "a1"):
                c = pl.ds(int(name[1]) * (half // 2), half // 2)
                own, to = s["other"].at[:, c], s["x_active"].at[low, c]
            elif name in ("i0", "i1"):
                c = pl.ds(int(name[1]) * half, half)
                own, to = s["y_inner"].at[top, c], s["y_inner"].at[low, c]
            else:
                own, to = s[name].at[top], s[name].at[low]
            return remote(own, to, x_send.at[i], x_recv.at[i], sib)

        def cross(name):
            cross_copy(name).start()

        def crossed(*which):
            for name in which:
                cross_copy(name).wait()

        def col_copy(full):
            return lambda j, slot: pltpu.make_async_copy(
                full.at[:, columns(j * TILE, TILE)], s["cols"].at[slot], tile_sem.at[slot]
            )

        def row_copy(full):
            def copy_of(j, slot):
                r = pl.ds(pl.multiple_of(j * TILE, TILE), TILE)
                return Both(
                    [
                        pltpu.make_async_copy(
                            full.at[r, pl.ds(i * TILE, TILE)],
                            s["cols"].at[slot, pl.ds(i * TILE, TILE)],
                            tile_sem.at[2 * (i + 1) + slot],
                        )
                        for i in range(width // TILE)
                    ]
                )

            return copy_of

        def leave(i, source, dst):
            return pltpu.make_async_copy(source, dst, leave_sem.at[i])

        first = len(sizes)
        seg_row = jnp.concatenate([small[first + i : first + i + 1, :] for i in range(-(-rows // 128))], 1)
        seg_col = jnp.broadcast_to(seg_row, (128, seg_row.shape[1])).T[:rows, 0:1]
        seg_row = seg_row[:, :rows]
        valid_col = seg_col < IMG_DEV

        def begin():
            allowed = (seg_col == seg_row) & (seg_row < IMG_DEV)
            s["bias"][...] = jnp.where(allowed, 0.0, -1e30)
            loads[1].wait()
            d_resid[...] = jnp.where(valid_col, d_resid[...], 0.0)
            s["y_mlp"][top, :] = d_resid[...].astype(b16)
            gvec[DOWN_BIAS : DOWN_BIAS + 1, :] = column_sums(s["y_mlp"][top, :])

        def project(part):
            def body(t, slot):
                j = t - tiles_in * part
                out = dot(s["x_first"][top, :], s["cols"][slot])
                if part == 0:
                    out = (out + vecs[QUERY_BIAS : QUERY_BIAS + 1, columns(j * TILE, TILE)]) * HEAD_DIM ** (-0.5)
                elif part == 2:
                    out = out + vecs[VALUE_BIAS : VALUE_BIAS + 1, columns(j * TILE, TILE)]
                s["qkv"][:, columns(t * TILE, TILE)] = out.astype(b16)

            stream(3 * tiles_in, tiles_in * part, tiles_in, col_copy(wq_h), body)

        def attend(first, n):
            loop(n, lambda i: attend_pair(first + i, width, s["qkv"], s["bias"], s["x_attended"].at[top]))

        def project_out():
            def body(j):
                c = columns(j * TILE, TILE)
                resid[:, c] = tok[:, c] + dot(s["x_attended"][top, :], s["wo"][:, c]) + vecs[OUT_BIAS : OUT_BIAS + 1, c]

            loop(tiles_in, body)

        def up_tiles(first, n):
            def body(j, slot):
                t = dot(s["x_second"][top, :], s["cols"][slot])
                t = t + vecs[pl.ds(UP_BIAS + j // per, 1), columns((j % per) * TILE, TILE)]
                cdf = 0.5 + 0.5 * lax.erf(t * (0.5**0.5))
                s["slope"][:, columns(j * TILE, TILE)] = cdf + t * (0.3989422804014327 * jnp.exp(-0.5 * t * t))
                act = (t * cdf).astype(b16)
                for i in range(TILE // 256):
                    even, odd = act[:, 256 * i : 256 * i + 128], act[:, 256 * i + 128 : 256 * i + 256]
                    c = columns((2 * j + i) * 128, 128)
                    s["x_active"][top, c] = jnp.where(core == 0, even, odd)
                    s["other"][:, c] = jnp.where(core == 0, odd, even)

            stream(tiles, first, n, col_copy(wu_h), body)

        def d_inner_tiles(first, n):
            def body(j, slot):
                size = TILE // 2
                for i in (0, 1):
                    c = columns(j * TILE + i * size, size)
                    d_act = 0.0
                    for part in range(width // TILE):
                        wrows = slice(part * TILE + i * size, part * TILE + i * size + size)
                        d_act = d_act + dot_nt(s["y_mlp"][top, part * TILE : part * TILE + TILE], s["cols"][slot, wrows, :])
                    dd = (d_act * s["slope"][:, c]).astype(b16)
                    s["y_inner"][top, c] = dd
                    gvec[pl.ds(UP_BIAS + j // per, 1), columns((j % per) * TILE + i * size, size)] = column_sums(dd)

            stream(tiles, first, n, row_copy(wd_h), body)

        def d_second_tiles(first, n):
            def body(j, slot):
                acc[...] += dot_nt(s["y_inner"][top, columns(j * TILE, TILE)], s["cols"][slot])

            stream(tiles, first, n, col_copy(wu_h), body)

        def d_first_tiles(first, n):
            def body(j, slot):
                acc[...] += dot_nt(s["y_inner"][top, columns(j * TILE, TILE)], s["cols"][slot])

            stream(3 * tiles_in, first, n, col_copy(wq_h), body)

        def down_tiles(first, n):
            def body(j, slot):
                c = columns(2 * j * 128, 256)
                for which, left in ((core, s["x_active"][top, c]), (1 - core, s["other"][:, c])):
                    for part in range(width // TILE):
                        right = [
                            s["cols"][slot, pl.ds(pl.multiple_of(part * TILE + (2 * i + which) * 128, 128), 128), :]
                            for i in (0, 1)
                        ]
                        acc[:, part * TILE : part * TILE + TILE] += dot(left, jnp.concatenate(right, 0))

            stream(tiles, first, n, row_copy(wd_h), body)

        def second_norm_back():
            def emit(r, back):
                total = d_resid[r, :] + back
                d_resid[r, :] = total
                s["y_branch"][r, :] = total.astype(b16)

            norm_back(acc, resid, vecs, GAIN_TWO, held, emit)
            gvec[GAIN_TWO : GAIN_TWO + 1, :] = jnp.sum(held[0:8, :], 0, keepdims=True)
            gvec[BIAS_TWO : BIAS_TWO + 1, :] = jnp.sum(held[8:16, :], 0, keepdims=True)

        def first_norm_back():
            def emit(r, back):
                d_resid[r, :] += back

            loads[0].wait()
            norm_back(acc, tok, vecs, GAIN_ONE, held, emit)
            gvec[GAIN_ONE : GAIN_ONE + 1, :] = jnp.sum(held[0:8, :], 0, keepdims=True)
            gvec[BIAS_ONE : BIAS_ONE + 1, :] = jnp.sum(held[8:16, :], 0, keepdims=True)

        stacked = pl.ds(96, block[0])
        results = [homes[2], homes[3]] + [s["slope"].at[stacked, pl.ds(i * width, width)] for i in (1, 0)]

        def leave_result(i):
            if i != 2:
                return leave(2 + i, results[i], (q_out, o_out, u_out, d_out)[i])
            return Both(
                [
                    leave(6 + unit, results[2].at[pl.ds(unit * UNIT, UNIT)], u_out.at[:, pl.ds(unit * width, width)])
                    for unit in range(UNITS)
                ]
            )

        def emit_down(chunk, total):
            results[3][pl.ds(16 * chunk, 16), :] = total

        def emit_up(chunk, total):
            results[2][pl.ds(16 * chunk, 16), :] = total

        def emit_attn(chunk, total):
            unit, r = chunk // 2, 16 * (chunk % 2)
            if unit == 3:
                results[1][pl.ds(r, 16), :] = total
            else:
                results[0][pl.ds(r, 16), width * unit : width * unit + width] = total

        mines = bufs[:3]
        reduces = []
        for piece, emit in enumerate((emit_down, emit_up, emit_attn)):
            pair = []
            for zf in (True, False):
                p = 2 * piece + (0 if zf else 1)
                mid = bufs[3 + 3 * p : 6 + 3 * p]
                row = 0 if zf else SPLIT_ROWS
                pair.append(Reduce(p, zf, row, mines[piece], *mid, send, b_recv, z_recv, a_recv, emit))
            reduces.append(pair)

        def stage(piece, j):
            for r in reduces[piece]:
                step = r.stages()[j]
                if step is not None:
                    step()

        def send_blocks(piece):
            for k in (3, 2, 1, 0):
                for r in reduces[piece]:
                    r.send_b(k)

        def drain(piece):
            for r in reduces[piece]:
                r.drain()

        def down_grad(n):
            i = n + (1 - z // 2) * (LINE - 1 - 2 * n)
            out = dot_tn(s["x_active"][:, columns(i * TILE, TILE)], s["y_mlp"][...]).astype(b16)
            mines[0][pl.ds(4 * i, 4)] = out.reshape(4, block[0], width)
            for r in reduces[0]:
                r.send_plane(i)

        def up_grad(first):
            for unit in (first, first + 1):
                turned_product(s["turned"], core, s["y_inner"], mines[1], unit, unit * width)

        def out_grad():
            transpose_blocks(s["x_attended"], s["turned"])
            turned_product(s["turned"], core, s["y_branch"], mines[2], 3, 0)
            transpose_blocks(s["x_first"], s["turned"])

        def qkv_grad():
            for unit in range(3):
                turned_product(s["turned"], core, s["y_inner"], mines[2], unit, unit * width)

        def finish_activations():
            resid[...] = jnp.where(valid_col, resid[...] + acc[...] + vecs[DOWN_BIAS : DOWN_BIAS + 1, :], 0.0)
            leave(0, resid, act_out).start()

        def clear():
            acc[...] = jnp.zeros_like(acc)

        def share_vectors():
            leave(1, d_resid, grad_out).start()
            held[...] = gvec[...]
            v.start(0)

        def d_attended_tile(j):
            size = TILE // 2
            wrows = pl.ds(pl.multiple_of(j * size, size), size)
            c = columns(j * size, size)
            s["y_mlp"][top, c] = dot_nt(s["y_branch"][top, :], s["wo"][wrows, :]).astype(b16)
            gvec[OUT_BIAS : OUT_BIAS + 1, c] = column_sums(s["y_branch"][top, c])

        def attend_back(first, n):
            loop(
                n,
                lambda i: attend_back_pair(
                    first + i, width, s["qkv"], s["y_mlp"].at[top], s["bias"], s["y_inner"], gvec
                ),
            )

        def known():
            vecs[...] = held[...]

        def norm_one():
            loads[0].wait()
            norm_into(s["x_first"].at[top], tok, vecs, GAIN_ONE, BIAS_ONE)

        def norm_two():
            norm_into(s["x_second"].at[top], resid, vecs, GAIN_TWO, BIAS_TWO)

        gvec[...] = jnp.zeros_like(gvec)
        for i in range(4):
            cast_shard(i)
        loads[0].start()
        gather_at(0)
        v.step(0)
        gather_at(1)
        v.step(1)
        gather_at(2)
        v.step(2)
        gather_at(3)
        v.step(3)
        gather_at(4)
        v.step(4)
        known()
        begin()
        cross("y_mlp")
        gather_at(5)
        gather_at(6)
        norm_one()
        cross("x_first")
        gather_at(7)
        gather_at(8)
        gather_at(9)
        gather_at(10)
        gather_at(11)
        gathered(0, 1)
        project(0)
        gather_at(12)
        project(1)
        project(2)
        gather_at(13)
        attend(0, 2)
        gather_at(14)
        attend(2, 2)
        attend(4, 2)
        gather_at(15)
        attend(6, 2)
        cross("x_attended")
        gathered(2)
        project_out()
        norm_two()
        cross("x_second")
        gather_at(16)
        gather_at(17)
        gathered(3, 4)
        up_tiles(0, 2)
        up_tiles(2, 2)
        cross("a0")
        gather_at(18)
        up_tiles(4, 2)
        gather_at(19)
        up_tiles(6, 2)
        cross("a1")
        gather_at(20)
        crossed("y_mlp", "a0", "a1")
        down_grad(0)
        down_grad(1)
        down_grad(2)
        down_grad(3)
        gather_at(21)
        gather_at(22)
        gather_at(23)
        crossed("x_second")
        transpose_blocks(s["x_second"], s["turned"])
        gathered(5, 6)
        d_inner_tiles(0, 2)
        d_inner_tiles(2, 2)
        cross("i0")
        stage(0, 0)
        d_inner_tiles(4, 2)
        d_inner_tiles(6, 2)
        cross("i1")
        loads[0].start()
        stage(0, 1)
        crossed("i0")
        up_grad(0)
        crossed("i1")
        up_grad(2)
        send_blocks(1)
        pl.semaphore_signal(free, inc=1, device_id=(sib,), device_id_type=MESH)
        stage(0, 2)
        clear()
        d_second_tiles(0, 4)
        d_second_tiles(4, 4)
        stage(0, 3)
        second_norm_back()
        cross("y_branch")
        loop(width // (TILE // 2), d_attended_tile)
        stage(0, 4)
        attend_back(0, 2)
        stage(0, 5)
        stage(1, 0)
        attend_back(2, 2)
        stage(1, 1)
        attend_back(4, 2)
        stage(0, 6)
        stage(1, 2)
        attend_back(6, 2)
        pl.semaphore_wait(free, 1)
        cross("y_proj")
        crossed("x_attended", "x_first", "y_branch")
        out_grad()
        stage(1, 3)
        crossed("y_proj")
        qkv_grad()
        send_blocks(2)
        stage(0, 7)
        leave_result(3).start()
        stage(1, 4)
        stage(1, 5)
        clear()
        d_first_tiles(0, 3)
        d_first_tiles(3, 3)
        stage(2, 0)
        first_norm_back()
        share_vectors()
        stage(1, 6)
        stage(2, 1)
        v.step(0)
        stage(2, 2)
        clear()
        down_tiles(0, 4)
        down_tiles(4, 4)
        finish_activations()
        stage(1, 7)
        leave_result(2).start()
        stage(2, 3)
        v.step(1)
        stage(2, 4)
        v.step(2)
        stage(2, 5)
        v.step(3)
        stage(2, 6)
        v.step(4)
        stage(2, 7)
        leave_result(0).start()
        leave_result(1).start()
        gvec_out[...] = held[...]
        for g in parts:
            g.drain()
        for piece in range(3):
            drain(piece)
        leave(0, resid, act_out).wait()
        leave(1, d_resid, grad_out).wait()
        for i in range(4):
            leave_result(i).wait()

    anyspec = pl.BlockSpec(memory_space=pl.ANY)
    vm = pl.BlockSpec(memory_space=pltpu.VMEM)
    dma = pltpu.SemaphoreType.DMA
    shape = jax.ShapeDtypeStruct
    n = len(GATHER_PARTS)
    bufs = [pltpu.VMEM((CHIPS,) + block, b16)] * 3
    for _ in range(3):
        for zf, height in ((True, SPLIT_ROWS), (False, block[0] - SPLIT_ROWS)):
            bufs += [pltpu.VMEM((m, height, width), b16) for m in (8, 5 if zf else 10, 4 if zf else 1)]
    outs = [
        ((rows, width), f32),
        ((rows, width), f32),
        ((width, 3 * width), b16),
        ((width, hidden), b16),
        ((hidden, width), b16),
        (shards[0].shape, f32),
        (shards[1].shape, f32),
        (shards[2].shape, f32),
        (shards[3].shape, f32),
        (vec.shape, f32),
    ]
    results = pl.pallas_call(
        kernel,
        out_shape=[shape(*o) for o in outs],
        in_specs=[vm] + [anyspec] * len(OPERANDS),
        out_specs=[anyspec] * 9 + [vm],
        scratch_shapes=[pltpu.VMEM(*kinds[k]) for k in names]
        + bufs
        + [
            pltpu.VMEM(vec.shape, f32),
            pltpu.VMEM((5,) + vec.shape, f32),
            dma((n, 4)),
            dma((n, 16)),
            dma((n,)),
            dma((n,)),
            dma((5,)),
            dma((5,)),
            dma((6, 4)),
            dma((6, 8)),
            dma((6, 10)),
            dma((6, 4)),
            dma((len(crossing),)),
            dma((len(crossing),)),
            dma((len(OPERANDS),)),
            dma((2 * (1 + width // TILE),)),
            dma((6 + UNITS,)),
            pltpu.SemaphoreType.REGULAR,
        ],
        compiler_params=pltpu.CompilerParams(collective_id=0, has_side_effects=True, vmem_limit_bytes=63 << 20),
    )(small_rows(segments, vectors), tokens, cotangent, *shards)
    settled = settle([results[0], results[1], *results[5:9]])
    return settled[0], settled[1], settled[2:], results[9]


def local_math(tokens, segments, cotangent, vectors, weights):
    gain_one, bias_one, mix_bias, proj_bias, gain_two, bias_two, up_bias, down_bias = vectors
    mix_weight, proj_weight, up_weight, down_weight = weights
    model_width = tokens.shape[1]
    valid_slot = segments < IMG_DEV
    allowed = (segments[:, None] == segments[None, :]) & valid_slot[None, :]
    gain_one_f = gain_one.astype(jnp.float32)
    bias_one_f = bias_one.astype(jnp.float32)
    first = halved(layer_norm(tokens, gain_one_f, bias_one_f))
    mix_bias_f = mix_bias.astype(jnp.float32)
    bias_row = jnp.concatenate(
        [mix_bias_f[:model_width], jnp.zeros((model_width,), jnp.float32), mix_bias_f[model_width:]]
    )
    projected = jnp.dot(first, mix_weight, preferred_element_type=jnp.float32) + bias_row
    queries = halved(projected[:, :model_width] * HEAD_DIM ** (-0.5))
    key_rows = halved(projected[:, model_width : 2 * model_width])
    values = halved(projected[:, 2 * model_width :])
    attended_stack, lse_stack = lax.map(
        lambda pieces: pair_forward(pieces, allowed),
        (head_pairs(queries), head_pairs(key_rows), head_pairs(values)),
    )
    attended = halved(join_pairs(attended_stack))
    residual = (
        tokens
        + jnp.dot(attended, proj_weight, preferred_element_type=jnp.float32)
        + proj_bias.astype(jnp.float32)
    )
    gain_two_f = gain_two.astype(jnp.float32)
    bias_two_f = bias_two.astype(jnp.float32)
    second = halved(layer_norm(residual, gain_two_f, bias_two_f))
    inner = jnp.dot(second, up_weight, preferred_element_type=jnp.float32) + up_bias.astype(
        jnp.float32
    )
    active = halved(jax.nn.gelu(inner, approximate=False))
    branch = jnp.dot(active, down_weight, preferred_element_type=jnp.float32) + down_bias.astype(
        jnp.float32
    )
    activations = jnp.where(valid_slot[:, None], residual + branch, 0.0)
    d_out = jnp.where(valid_slot[:, None], cotangent, 0.0)
    d_mlp = halved(d_out)
    grad_fc2_bias = jnp.sum(d_mlp, 0, dtype=jnp.float32)
    grad_fc2_weight = contract_rows(active, d_mlp)
    d_active = contract_cols(d_mlp, down_weight)
    gelu_back = jax.vjp(partial(jax.nn.gelu, approximate=False), inner)[1]
    d_inner = halved(gelu_back(d_active)[0])
    grad_fc1_bias = jnp.sum(d_inner, 0, dtype=jnp.float32)
    grad_fc1_weight = contract_rows(second, d_inner)
    d_second = contract_cols(d_inner, up_weight)
    norm_two_back = jax.vjp(layer_norm, residual, gain_two_f, bias_two_f)[1]
    d_norm2, grad_norm2_gain, grad_norm2_bias = norm_two_back(d_second)
    d_resid = d_out + d_norm2
    d_branch = halved(d_resid)
    grad_out_bias = jnp.sum(d_branch, 0, dtype=jnp.float32)
    grad_out_weight = contract_rows(attended, d_branch)
    d_attended = halved(contract_cols(d_branch, proj_weight))
    d_query_stack, d_key_stack, d_value_stack = lax.map(
        lambda pieces: pair_backward(pieces, allowed),
        (
            head_pairs(queries),
            head_pairs(key_rows),
            head_pairs(values),
            head_pairs(d_attended),
            lse_stack,
        ),
    )
    d_query = join_pairs(d_query_stack)
    d_value = join_pairs(d_value_stack)
    d_projected = jnp.concatenate([d_query, join_pairs(d_key_stack), d_value], 1)
    grad_qv_bias = jnp.concatenate(
        [jnp.sum(d_query, 0, dtype=jnp.float32), jnp.sum(d_value, 0, dtype=jnp.float32)]
    )
    grad_qkv_weight = contract_rows(first, d_projected)
    d_first = contract_cols(d_projected, mix_weight)
    norm_one_back = jax.vjp(layer_norm, tokens, gain_one_f, bias_one_f)[1]
    d_norm1, grad_norm1_gain, grad_norm1_bias = norm_one_back(d_first)
    input_grad = d_resid + d_norm1
    return (
        activations,
        input_grad,
        (grad_qkv_weight, grad_out_weight, grad_fc1_weight, grad_fc2_weight),
        (
            grad_norm1_gain,
            grad_norm1_bias,
            grad_qv_bias,
            grad_out_bias,
            grad_norm2_gain,
            grad_norm2_bias,
            grad_fc1_bias,
            grad_fc2_bias,
        ),
    )


def shards(count, tokens,
    segments,
    norm1_gain,
    norm1_bias,
    qkv_weight,
    qv_bias,
    out_weight,
    out_bias,
    norm2_gain,
    norm2_bias,
    fc1_weight,
    fc1_bias,
    fc2_weight,
    fc2_bias,
    cotangent,
):
    vector_shards = (norm1_gain, norm1_bias, qv_bias, out_bias, norm2_gain, norm2_bias, fc1_bias, fc2_bias)
    sizes = [v.shape[0] * count for v in vector_shards]
    starts = [sum(sizes[:i]) for i in range(len(sizes) + 1)]
    width = tokens.shape[1]
    position = lax.axis_index(AXIS)
    kernels = count == 32

    if kernels:
        activations, input_grad, weight_owned, vector_rows = block_all(
            count,
            tokens,
            segments,
            cotangent,
            (qkv_weight, out_weight, fc1_weight, fc2_weight),
            vector_shards,
        )
    else:
        weight_shards = [halved(w) for w in (qkv_weight, out_weight, fc1_weight, fc2_weight)]
        weights = [lax.all_gather(w, AXIS, axis=0, tiled=True) for w in weight_shards]
        vectors = [
            lax.all_gather(halved(v), AXIS, axis=0, tiled=True).astype(jnp.float32)
            for v in vector_shards
        ]
        activations, input_grad, weight_grads, vector_grads = local_math(
            tokens, segments, cotangent, vectors, weights
        )
    if kernels:
        flat = vector_rows.reshape(-1)
        vector_owned = [
            lax.dynamic_slice(flat, (starts[i] + position * (sizes[i] // count),), (sizes[i] // count,))
            for i in range(len(sizes))
        ]
    else:
        weight_owned = [
            lax.psum_scatter(g, AXIS, scatter_dimension=0, tiled=True) for g in weight_grads
        ]
        vector_owned = [
            lax.psum_scatter(g, AXIS, scatter_dimension=0, tiled=True) for g in vector_grads
        ]
    g1, b1, qvb, ob, g2, b2, f1b, f2b = vector_owned
    qkv_g, out_g, fc1_g, fc2_g = weight_owned
    return (activations, input_grad, g1, b1, qkv_g, qvb, out_g, ob, g2, b2, fc1_g, f1b, fc2_g, f2b)


def solution(mesh):
    in_specs = (
        P(AXIS, None),
        P(AXIS),
        P(AXIS),
        P(AXIS),
        P(AXIS, None),
        P(AXIS),
        P(AXIS, None),
        P(AXIS),
        P(AXIS),
        P(AXIS),
        P(AXIS, None),
        P(AXIS),
        P(AXIS, None),
        P(AXIS),
        P(AXIS, None),
    )
    out_specs = (
        P(AXIS, None),
        P(AXIS, None),
        P(AXIS),
        P(AXIS),
        P(AXIS, None),
        P(AXIS),
        P(AXIS, None),
        P(AXIS),
        P(AXIS),
        P(AXIS),
        P(AXIS, None),
        P(AXIS),
        P(AXIS, None),
        P(AXIS),
    )
    return jax.shard_map(
        partial(shards, mesh.size), mesh=mesh, in_specs=in_specs, out_specs=out_specs, check_vma=False)
```

time: 420 us -> 240 us (0.57); the launches traced: 414 us -> 239 us
  matrix products: 97.6 us -> 0 us
  local copies, waits for them, and re-layouts: 65.8 us -> 3.36 us
  other arithmetic: 23.2 us -> 0.68 us
  Pallas kernels: 225 us -> 234 us
    dot_general x68 -> x0, matrix products: 97.6 us -> none  [the longest x4 30 us: contract_cols(): lax.dot_general(left, right, (((1,), (1,)), ((), ())), preferred_element_...]
    dynamic_slice x48 -> x0, local copies, waits for them, and re-layouts: 29.8 us -> none  [local_math(): lax.map(lambda pieces: pair_forward(pieces, allowed), (head_pairs(queries...]
    dynamic_update_slice x24 -> x0, local copies, waits for them, and re-layouts: 16.2 us -> none  [the longest x16 10.9 us: local_math(): lax.map(lambda pieces: pair_backward(pieces, allowed), (head_pairs(querie...]
    convert_element_type x19 -> x1, other arithmetic: 12.7 us -> 0.68 us  [small_rows(): segments.astype(jnp.float32)]
    pallas_call x2, Pallas kernels: 225 us -> 234 us  [the longest x1 231 us: block_all(): pl.pallas_call(kernel, out_shape=[shape(*o) for o in outs], in_specs=[vm]...]
    unnamed x91 -> x3, local copies, waits for them, and re-layouts: 9.28 us -> 0.02 us
    reduce_sum x17 -> x0, other arithmetic: 6.3 us -> none  [the longest x3 2.44 us: layer_norm(): centre = rows_in - jnp.mean(rows_in, -1, keepdims=True)]
    reshape x6 -> x1, local copies, waits for them, and re-layouts: 4.98 us -> 0.61 us  [small_rows(): return jnp.pad(flat, (0, 2048 - flat.shape[0])).reshape(16, 128)]
where the time goes in v3:
time: 240 us; the launch traced here: 239 us
  Pallas kernels  234 us (98%)
  local copies, waits for them, and re-layouts  3.36 us (1%)
    pallas_call x1, Pallas kernels, block_all(): pl.pallas_call(kernel, out_shape=[shape(*o) for o in outs], in_specs=[vm]...  231 us

profile of v3, /device:TPU:0, one launch (start us, length us, event | category | flops | bytes accessed | tf_op | source)
XLA Modules:
  0.0 239.1 jit_solution(1882486854850895572)
XLA Ops:
  0.6 0.7 convert_element_type.7
  1.3 0.9 concatenate.3
  2.3 0.6 pad_bitcast_fusion.small
  2.9 230.9 %shard_map.254 = (f32[320,1024]{1,0:T(8,128)}, f32[320,1024]{1,0:T(8,128)}, bf16[1024,3072]{1,0:T(8,128)(2,1)}, bf16[1024,4096]{1,0:T(8,128)(2,1)}, bf16[4096,10...) custom-call(f32[16,128]{1,0:T(8,128)} %pad_bitcast_fusion.small, ...), custom_call_target="tpu_custom_call" | custom-call | tf_op jit(solution)/shard_map/pallas_call | solution.py:1284
  233.8 0.0 copy-start
  233.8 3.5 %shard_map.255 = (f32[320,1024]{1,0:T(8,128)}, f32[320,1024]{1,0:T(8,128)}, f32[32,3072]{1,0:T(8,128)}, f32[32,1024]{1,0:T(8,128)}, f32[32,4096]{1,0:T(8,128)}, /*index=5*/f32[128,1024]{1,0:T(8,128)}) custom-call(f32[320,1024]{1,0:T(8,128)} %get-tuple-element.27.refs_0_, f32[320,1024]{1,0:T(8,128)} %get-tuple-element.28.refs_1_, ...), custom_call_target="tpu_custom_call" | custom-call | tf_op jit(solution)/shard_map/pallas_call | solution.py:747
  237.3 0.0 copy-done
  237.3 0.6 fusion
  237.9 0.6 dynamic_slice.26
  238.5 0.6 dynamic_slice.30
  (2 shorter events, 0.0 us)
Async XLA Ops:
  233.8 3.5 %copy-start = (f32[16,1024]{1,0:T(8,128)S(1)}, f32[16,1024]{1,0:T(8,128)}, u32[]{:S(2)}) copy-start(f32[16,1024]{1,0:T(8,128)} %get-tuple-element.35) | copy-start | bytes 196612

commit v4 on v3

--- a/solution.py
+++ b/solution.py
@@ -352,7 +352,7 @@
     (3, 0.375, 0.625, False),
 )
 GROUPS = ((0, 1, 2), (3, 4), (5, 6))
-LAG = 6
+LAG = 5
 SPLIT_ROWS = 48
 
 
@@ -1119,22 +1119,22 @@
         gather_at(0)
         v.step(0)
         gather_at(1)
+        gather_at(2)
         v.step(1)
-        gather_at(2)
+        gather_at(3)
         v.step(2)
-        gather_at(3)
+        gather_at(4)
+        gather_at(5)
         v.step(3)
-        gather_at(4)
+        begin()
+        cross("y_mlp")
+        gather_at(6)
+        gather_at(7)
         v.step(4)
         known()
-        begin()
-        cross("y_mlp")
-        gather_at(5)
-        gather_at(6)
+        gather_at(8)
         norm_one()
         cross("x_first")
-        gather_at(7)
-        gather_at(8)
         gather_at(9)
         gather_at(10)
         gather_at(11)
@@ -1143,38 +1143,36 @@
         gather_at(12)
         project(1)
         project(2)
+        attend(0, 2)
         gather_at(13)
-        attend(0, 2)
-        gather_at(14)
         attend(2, 2)
         attend(4, 2)
-        gather_at(15)
+        gather_at(14)
         attend(6, 2)
         cross("x_attended")
         gathered(2)
         project_out()
         norm_two()
         cross("x_second")
+        gather_at(15)
         gather_at(16)
-        gather_at(17)
         gathered(3, 4)
         up_tiles(0, 2)
         up_tiles(2, 2)
         cross("a0")
+        gather_at(17)
+        up_tiles(4, 2)
         gather_at(18)
-        up_tiles(4, 2)
-        gather_at(19)
         up_tiles(6, 2)
         cross("a1")
-        gather_at(20)
+        gather_at(19)
         crossed("y_mlp", "a0", "a1")
         down_grad(0)
         down_grad(1)
         down_grad(2)
         down_grad(3)
+        gather_at(20)
         gather_at(21)
-        gather_at(22)
-        gather_at(23)
         crossed("x_second")
         transpose_blocks(s["x_second"], s["turned"])
         gathered(5, 6)
@@ -1232,21 +1230,21 @@
         stage(1, 6)
         stage(2, 1)
         v.step(0)
-        stage(2, 2)
         clear()
         down_tiles(0, 4)
         down_tiles(4, 4)
         finish_activations()
+        stage(2, 2)
         stage(1, 7)
         leave_result(2).start()
+        v.step(1)
         stage(2, 3)
-        v.step(1)
+        v.step(2)
         stage(2, 4)
-        v.step(2)
+        v.step(3)
         stage(2, 5)
-        v.step(3)
+        v.step(4)
         stage(2, 6)
-        v.step(4)
         stage(2, 7)
         leave_result(0).start()
         leave_result(1).start()

time: 240 us -> 237 us (0.988)
  Pallas kernels: 234 us -> 230 us
    pallas_call x1, Pallas kernels: 231 us -> 226 us  [block_all(): pl.pallas_call(kernel, out_shape=[shape(*o) for o in outs], in_specs=[vm]...]
where the time goes in v4:
time: 237 us; the launch traced here: 235 us
  Pallas kernels  230 us (97%)
  local copies, waits for them, and re-layouts  3.36 us (1%)
    pallas_call x1, Pallas kernels, block_all(): pl.pallas_call(kernel, out_shape=[shape(*o) for o in outs], in_specs=[vm]...  226 us

profile of v4, /device:TPU:0, one launch (start us, length us, event | category | flops | bytes accessed | tf_op | source)
XLA Modules:
  0.0 234.5 jit_solution(17361693962027609534)
XLA Ops:
  0.6 0.7 convert_element_type.7
  1.3 0.9 concatenate.3
  2.3 0.6 pad_bitcast_fusion.small
  2.9 226.3 %shard_map.254 = (f32[320,1024]{1,0:T(8,128)}, f32[320,1024]{1,0:T(8,128)}, bf16[1024,3072]{1,0:T(8,128)(2,1)}, bf16[1024,4096]{1,0:T(8,128)(2,1)}, bf16[4096,10...) custom-call(f32[16,128]{1,0:T(8,128)} %pad_bitcast_fusion.small, ...), custom_call_target="tpu_custom_call" | custom-call | tf_op jit(solution)/shard_map/pallas_call | solution.py:1282
  229.2 0.0 copy-start
  229.2 3.5 %shard_map.255 = (f32[320,1024]{1,0:T(8,128)}, f32[320,1024]{1,0:T(8,128)}, f32[32,3072]{1,0:T(8,128)}, f32[32,1024]{1,0:T(8,128)}, f32[32,4096]{1,0:T(8,128)}, /*index=5*/f32[128,1024]{1,0:T(8,128)}) custom-call(f32[320,1024]{1,0:T(8,128)} %get-tuple-element.27.refs_0_, f32[320,1024]{1,0:T(8,128)} %get-tuple-element.28.refs_1_, ...), custom_call_target="tpu_custom_call" | custom-call | tf_op jit(solution)/shard_map/pallas_call | solution.py:747
  232.7 0.0 copy-done
  232.7 0.6 fusion
  233.3 0.6 dynamic_slice.26
  233.9 0.6 dynamic_slice.30
  (2 shorter events, 0.0 us)
Async XLA Ops:
  229.2 3.5 %copy-start = (f32[16,1024]{1,0:T(8,128)S(1)}, f32[16,1024]{1,0:T(8,128)}, u32[]{:S(2)}) copy-start(f32[16,1024]{1,0:T(8,128)} %get-tuple-element.35) | copy-start | bytes 196612

commit v5 on v4

--- a/solution.py
+++ b/solution.py
@@ -1113,10 +1113,12 @@
             norm_into(s["x_second"].at[top], resid, vecs, GAIN_TWO, BIAS_TWO)
 
         gvec[...] = jnp.zeros_like(gvec)
-        for i in range(4):
-            cast_shard(i)
+        cast_shard(0)
+        cast_shard(1)
+        gather_at(0)
+        cast_shard(2)
+        cast_shard(3)
         loads[0].start()
-        gather_at(0)
         v.step(0)
         gather_at(1)
         gather_at(2)

time: 237 us -> 237 us (level)
  no operation moved by 1% of the time
where the time goes in v5:
time: 237 us; the launch traced here: 234 us
  Pallas kernels  230 us (97%)
  local copies, waits for them, and re-layouts  3.36 us (1%)
    pallas_call x1, Pallas kernels, block_all(): pl.pallas_call(kernel, out_shape=[shape(*o) for o in outs], in_specs=[vm]...  226 us

profile of v5, /device:TPU:0, one launch (start us, length us, event | category | flops | bytes accessed | tf_op | source)
XLA Modules:
  0.0 234.5 jit_solution(16927033397690800064)
XLA Ops:
  0.6 0.7 convert_element_type.7
  1.3 0.9 concatenate.3
  2.3 0.6 pad_bitcast_fusion.small
  2.9 226.3 %shard_map.254 = (f32[320,1024]{1,0:T(8,128)}, f32[320,1024]{1,0:T(8,128)}, bf16[1024,3072]{1,0:T(8,128)(2,1)}, bf16[1024,4096]{1,0:T(8,128)(2,1)}, bf16[4096,10...) custom-call(f32[16,128]{1,0:T(8,128)} %pad_bitcast_fusion.small, ...), custom_call_target="tpu_custom_call" | custom-call | tf_op jit(solution)/shard_map/pallas_call | solution.py:1284
  229.2 0.0 copy-start
  229.2 3.5 %shard_map.255 = (f32[320,1024]{1,0:T(8,128)}, f32[320,1024]{1,0:T(8,128)}, f32[32,3072]{1,0:T(8,128)}, f32[32,1024]{1,0:T(8,128)}, f32[32,4096]{1,0:T(8,128)}, /*index=5*/f32[128,1024]{1,0:T(8,128)}) custom-call(f32[320,1024]{1,0:T(8,128)} %get-tuple-element.27.refs_0_, f32[320,1024]{1,0:T(8,128)} %get-tuple-element.28.refs_1_, ...), custom_call_target="tpu_custom_call" | custom-call | tf_op jit(solution)/shard_map/pallas_call | solution.py:747
  232.7 0.0 copy-done
  232.7 0.6 fusion
  233.3 0.6 dynamic_slice.26
  233.9 0.6 dynamic_slice.30
  (2 shorter events, 0.0 us)
Async XLA Ops:
  229.2 3.5 %copy-start = (f32[16,1024]{1,0:T(8,128)S(1)}, f32[16,1024]{1,0:T(8,128)}, u32[]{:S(2)}) copy-start(f32[16,1024]{1,0:T(8,128)} %get-tuple-element.35) | copy-start | bytes 196612
